TPU v7x, 32 devices: a whole 2x2x4 slice. The times are simulated.
32 devices in a mesh: section: 4 (over x, core), tile: 8 (over z, y).
Axes of the slice: x: 2, y: 2, z: 4, core: 2. Of those that a mesh axis runs over, the one named last changes fastest.
Arguments:
- saved: float32 [4, 5, 8, 64, 128], P('section', None, None, 'tile'), may hold values from -2.5 to 2.5
- sched: int32 [4], replicated, may hold values from 0 to 3, each once
Outputs:
- gradient: float32 [5, 8, 64, 128], P(None, None, 'tile')
Inputs may be any that keep to these rules, and one draw needn't show every extreme that they name: sched is a permutation of 0 .. 3.
All inputs are finite; a program needn't handle non-finite values.
Results may differ from a plain program's by a relative error of at most 0.0001.
Values sent between devices are 32-bit elements; how exact they have to be, the bound alone decides.
No kernel may reach another device: no remote copies, remote signals or barrier semaphores. Data moves between devices by JAX's collectives and lax.ppermute only.
A program may use at most 64 MiB of HBM per device.

v0:
```python
import functools

import jax
import jax.numpy as jnp
from jax import lax
from jax.experimental import pallas as pl
from jax.experimental.pallas import tpu as pltpu
from jax.sharding import PartitionSpec as P

time_step = 0.1
hyper_coeff = 0.1
slope_unit = time_step / 12.0
hyper_unit = time_step * hyper_coeff
BLOCK = 4
FIELDS, NZ, NY = 5, 8, 128


def roll_y(plane, ahead):
    return pltpu.roll(plane, (-ahead) % NY, 1)


def roll_z(plane, ahead):
    return pltpu.roll(plane, (-ahead) % NZ, 0)


def sum_of(terms):
    return (terms[0] + terms[1]) + terms[2]


def blocks(low, high, visit):
    @pl.loop(0, (high - low) // BLOCK)
    def _(step):
        visit(low + step * BLOCK)


def forward_rows(state, margin, reach, slopes, finish):
    def visit(first):
        seen = {}

        def at(row, field):
            if (row, field) not in seen:
                seen[row, field] = state[first + (margin + row), field]
            return seen[row, field]

        for row in range(BLOCK):
            slope, near, far = {}, {}, {}
            for field in range(FIELDS if finish else 4):
                here = at(row, field)
                around = (
                    (at(row + 1, field), at(row - 1, field), at(row + 2, field), at(row - 2, field)),
                    tuple(roll_y(here, k) for k in (1, -1, 2, -2)),
                    tuple(roll_z(here, k) for k in (1, -1, 2, -2)),
                )
                for dim, (up, down, up2, down2) in enumerate(around):
                    slope[field, dim] = 8.0 * (up - down) - (up2 - down2)
                if finish:
                    near[field] = sum_of([a[0] + a[1] for a in around])
                    far[field] = sum_of([a[2] + a[3] for a in around])
            for field in range(4):
                for dim in range(3):
                    slopes[first + (reach + row), field * 3 + dim] = slope[field, dim]
            if not finish:
                continue
            vel = [at(row, dim) * slope_unit for dim in range(3)]
            moved = []
            for field in range(FIELDS):
                value = (1.0 - 18.0 * hyper_unit) * at(row, field)
                value = value + (4.0 * hyper_unit) * near[field] - hyper_unit * far[field]
                if field < 4:
                    value = value - sum_of([vel[dim] * slope[field, dim] for dim in range(3)])
                if field < 3:
                    value = value - slope_unit * slope[4, field]
                if field == 2:
                    value = value + time_step * at(row, 3)
                if field == 3:
                    value = value - time_step * at(row, 2)
                if field == 4:
                    value = value - slope_unit * sum_of([slope[dim, dim] for dim in range(3)])
                moved.append(value)
            finish(first, row, moved)

    blocks(-reach, 8 + reach, visit)


def back_rows(adjoint, state, margin, slopes, slope_margin, reach, finish):
    def visit(first):
        seen_adjoint, seen_vel, seen_prod, seen_hyper = {}, {}, {}, {}

        def adj(row, field):
            if (row, field) not in seen_adjoint:
                seen_adjoint[row, field] = adjoint[first + (reach + 2 + row), field]
            return seen_adjoint[row, field]

        def vel(row, dim):
            if (row, dim) not in seen_vel:
                seen_vel[row, dim] = state[first + (margin + row), dim] * slope_unit
            return seen_vel[row, dim]

        def prod(row, field, dim):
            key = (row, field, dim)
            if key not in seen_prod:
                if field < 4:
                    value = vel(row, dim) * adj(row, field)
                    if field == dim:
                        value = value + slope_unit * adj(row, 4)
                else:
                    value = slope_unit * adj(row, dim)
                seen_prod[key] = value
            return seen_prod[key]

        def hyper(row, field):
            if (row, field) not in seen_hyper:
                seen_hyper[row, field] = hyper_unit * adj(row, field)
            return seen_hyper[row, field]

        for row in range(BLOCK):
            pulled = []
            for field in range(FIELDS):

                def up(r, dim):
                    return 4.0 * hyper(r, field) + 8.0 * prod(r, field, dim)

                def down(r, dim):
                    return 4.0 * hyper(r, field) - 8.0 * prod(r, field, dim)

                def up2(r, dim):
                    return prod(r, field, dim) + hyper(r, field)

                def down2(r, dim):
                    return prod(r, field, dim) - hyper(r, field)

                along_x = (up(row + 1, 0) + down(row - 1, 0)) + (down2(row - 2, 0) - up2(row + 2, 0))
                along_y = (roll_y(up(row, 1), 1) + roll_y(down(row, 1), -1)) + (
                    roll_y(down2(row, 1), -2) - roll_y(up2(row, 1), 2)
                )
                along_z = (roll_z(up(row, 2), 1) + roll_z(down(row, 2), -1)) + (
                    roll_z(down2(row, 2), -2) - roll_z(up2(row, 2), 2)
                )
                value = (1.0 - 18.0 * hyper_unit) * adj(row, field) + sum_of([along_x, along_y, along_z])
                if field < 3:
                    s = [adj(row, k) * slopes[first + (slope_margin + row), k * 3 + field] for k in range(4)]
                    value = value - slope_unit * ((s[0] + s[1]) + (s[2] + s[3]))
                if field == 2:
                    value = value - time_step * adj(row, 3)
                if field == 3:
                    value = value + time_step * adj(row, 2)
                pulled.append(value)
            finish(first, row, pulled)

    blocks(-reach, 8 + reach, visit)


def store(ref, margin, scale=None):
    def finish(first, row, values):
        for field in range(FIELDS):
            ref[first + (margin + row), field] = values[field] if scale is None else scale * values[field]

    return finish


def stages(m, q0, q1, q2, slopes):
    def second(first, row, values):
        for field in range(FIELDS):
            kept = q0[first + (q0.shape[0] // 2 - 4 + row), field]
            q2[first + (q2.shape[0] // 2 - 4 + row), field] = 0.75 * kept + 0.25 * values[field]

    reach1, reach2 = q1.shape[0] // 2 - 4, q2.shape[0] // 2 - 4
    forward_rows(q0, q0.shape[0] // 2 - 4, reach1, slopes[0], store(q1, reach1))
    forward_rows(q1, reach1, reach2, slopes[1], second)


def step_back(m, adjoint, q0, q1, q2, slopes, back2, back1, finish):
    def margin(ref):
        return ref.shape[0] // 2 - 4

    back_rows(adjoint, q2, margin(q2), slopes[2], margin(slopes[2]), m + 4, store(back2, m + 4, 2.0 / 3.0))
    back_rows(back2, q1, margin(q1), slopes[1], margin(slopes[1]), m + 2, store(back1, m + 2, 0.25))

    def last(first, row, values):
        total = []
        for field in range(FIELDS):
            held = adjoint[first + (m + 6 + row), field] * (1.0 / 3.0)
            total.append((held + 0.75 * back2[first + (m + 4 + row), field]) + values[field])
        finish(first, row, total)

    back_rows(back1, q0, margin(q0), slopes[0], margin(slopes[0]), m, last)


def slot_of(sched, group, count):
    slot = jnp.int32(0)
    for k in range(count):
        slot = jnp.where(sched[k] == group, jnp.int32(k), slot)
    return slot


def take_row(states, slot, field, row):
    return states[slot, field, pl.ds(row, NZ, stride=8), :]


def pack_body(groups, sched, core, states, near, next_near, late_near, late_next):
    q0, q1, q2, target = (slot_of(sched, g, groups) for g in (0, 1, groups - 2, groups - 1))

    def fill(ref, at, slot, rows):
        for k, row in enumerate(rows):
            for field in range(FIELDS):
                ref[at + k, field] = take_row(states, slot, field, row)

    for c in (0, 1):

        @pl.when(core[0] == c)
        def _():
            def edge(count):
                return range(count) if c == 0 else range(8 - count, 8)

            fill(near, 0, q2, range(8))
            fill(near, 8, target, edge(6))
            fill(next_near, 0, q2, edge(4))
            fill(late_near, 0, q1, range(8))
            fill(late_near, 8, q0, range(8))
            fill(late_next, 0, q1, range(8))
            fill(late_next, 8, q0, edge(2))


def put_rows(dst, at, src, begin, count):
    for k in range(count):
        for field in range(FIELDS):
            dst[at + k, field] = src[begin + k, field]


def with_sides(core, own, other, place):
    @pl.when(core[0] == 0)
    def _():
        place(other, own)

    @pl.when(core[0] != 0)
    def _():
        place(own, other)


def first_body(groups, sched, core, states, own, own2, other, other2, out, edge, q0, q1, q2, goal, last, back2, back1, s0, s1, s2):
    slot_q, slot_t = (slot_of(sched, g, groups) for g in (groups - 2, groups - 1))
    for row in range(8):
        for field in range(FIELDS):
            q0[12 + row, field] = take_row(states, slot_q, field, row)
            goal[6 + row, field] = take_row(states, slot_t, field, row)

    def place(below, above):
        (b1, b2), (a1, a2) = below, above
        put_rows(q0, 0, b2, 0, 4)
        put_rows(q0, 4, b1, 0, 8)
        put_rows(q0, 20, a1, 0, 8)
        put_rows(q0, 28, a2, 0, 4)
        put_rows(goal, 0, b1, 8, 6)
        put_rows(goal, 14, a1, 8, 6)

    with_sides(core, (own, own2), (other, other2), place)
    stages(2, q0, q1, q2, (s0, s1))

    def misfit(first, row, values):
        for field in range(FIELDS):
            state = q0[first + (12 + row), field] * (1.0 / 3.0) + (2.0 / 3.0) * values[field]
            last[first + (6 + row), field] = state - goal[first + (6 + row), field]

    forward_rows(q2, 8, 6, s2, misfit)
    step_back(0, last, q0, q1, q2, (s0, s1, s2), back2, back1, store(out, 0))
    for c in (0, 1):

        @pl.when(core[0] == c)
        def _():
            put_rows(edge, 0, out, 4 * c, 4)


def second_body(
    groups, sched, core, states, adjoint, a_own, a_own2, a_other, a_other2, l_own, l_own2, l_other, l_other2, out,
    p0, p1, p2, x0, x1, x2, lam, mid, back2, back1, ps0, ps1, ps2, xs0, xs1, xs2,
):
    slot_p, slot_x = (slot_of(sched, g, groups) for g in (1, 0))
    for row in range(8):
        for field in range(FIELDS):
            p0[16 + row, field] = take_row(states, slot_p, field, row)
            x0[10 + row, field] = take_row(states, slot_x, field, row)

    def place(below, above):
        (b1, b2), (a1, a2) = below, above
        put_rows(p0, 0, b2, 0, 8)
        put_rows(p0, 8, b1, 0, 8)
        put_rows(p0, 24, a1, 0, 8)
        put_rows(p0, 32, a2, 0, 8)
        put_rows(x0, 0, b2, 8, 2)
        put_rows(x0, 2, b1, 8, 8)
        put_rows(x0, 18, a1, 8, 8)
        put_rows(x0, 26, a2, 8, 2)

    with_sides(core, (l_own, l_own2), (l_other, l_other2), place)
    stages(6, p0, p1, p2, (ps0, ps1))
    forward_rows(p2, 12, 10, ps2, None)
    stages(0, x0, x1, x2, (xs0, xs1))
    forward_rows(x2, 6, 4, xs2, None)

    def place_adjoint(below, above):
        (b1, b2), (a1, a2) = below, above
        put_rows(lam, 0, b2, 0, 4)
        put_rows(lam, 4, b1, 0, 8)
        put_rows(lam, 20, a1, 0, 8)
        put_rows(lam, 28, a2, 0, 4)

    put_rows(lam, 12, adjoint, 0, 8)
    with_sides(core, (a_own, a_own2), (a_other, a_other2), place_adjoint)
    step_back(6, lam, p0, p1, p2, (ps0, ps1, ps2), back2, back1, store(mid, 6))

    def finish(first, row, values):
        for field in range(FIELDS):
            out[field, pl.ds(first + row, NZ, stride=8), :] = values[field]

    step_back(0, mid, x0, x1, x2, (xs0, xs1, xs2), back2, back1, finish)


def rows(count, planes=FIELDS):
    return pltpu.VMEM((count, planes, NZ, NY), jnp.float32)


def kernel(body, name, inputs, outs, scratch):
    smem, vmem = pl.BlockSpec(memory_space=pltpu.SMEM), pl.BlockSpec(memory_space=pltpu.VMEM)
    return pl.pallas_call(
        body,
        out_shape=[jax.ShapeDtypeStruct(shape, jnp.float32) for shape in outs],
        in_specs=[smem, smem] + [vmem] * inputs,
        out_specs=[vmem] * len(outs),
        scratch_shapes=scratch,
        compiler_params=pltpu.CompilerParams(vmem_limit_bytes=40 * 1024 * 1024),
        name=name,
    )


def body(saved, sched):
    sections, tiles = lax.axis_size("section"), lax.axis_size("tile")
    core = (lax.axis_index("section") % 2).astype(jnp.int32).reshape(1)

    def shift(array, hops):
        pairs = []
        for s in range(sections):
            for t in range(tiles):
                to = (t - hops if s % 2 == 0 else t + hops) % tiles
                pairs.append((s * tiles + t, s * tiles + to))
        return lax.ppermute(array, ("section", "tile"), pairs)

    def swap(array):
        return lax.ppermute(array, "section", [(s, s ^ 1) for s in range(sections)])

    def block(count):
        return (count, FIELDS, NZ, NY)

    states = lax.all_gather(saved[0], "section", axis=0, tiled=False)
    states = states.reshape(sections, FIELDS, NZ * 8, NY)
    pack = kernel(functools.partial(pack_body, sections), "pack", 1, [block(14), block(4), block(16), block(10)], [])
    near, next_near, late_near, late_next = pack(sched, core, states)
    own, own2 = shift(near, 1), shift(next_near, 2)
    other, other2 = swap(own), swap(own2)
    first = kernel(
        functools.partial(first_body, sections), "first_step", 5, [block(8), block(4)],
        [rows(32), rows(28), rows(24), rows(20), rows(20), rows(16), rows(12), rows(28, 12), rows(24, 12), rows(20, 12)],
    )
    adjoint, edge = first(sched, core, states, own, own2, other, other2)
    l_own, l_own2 = shift(late_near, 1), shift(late_next, 2)
    l_other, l_other2 = swap(l_own), swap(l_own2)
    a_own, a_own2 = shift(adjoint, 1), shift(edge, 2)
    a_other, a_other2 = swap(a_own), swap(a_own2)
    second = kernel(
        functools.partial(second_body, sections), "last_steps", 10, [(FIELDS, NZ * 8, NY)],
        [rows(40), rows(36), rows(32), rows(28), rows(24), rows(20), rows(32), rows(20), rows(28), rows(24)]
        + [rows(36, 12), rows(32, 12), rows(28, 12), rows(24, 12), rows(20, 12), rows(16, 12)],
    )
    (gradient,) = second(
        sched, core, states, adjoint, a_own, a_own2, a_other, a_other2, l_own, l_own2, l_other, l_other2
    )
    return gradient.reshape(FIELDS, NZ, 8, NY)


def solution(mesh):
    placed = (P("section", None, None, "tile", None), P())
    return jax.shard_map(
        body, mesh=mesh, in_specs=placed, out_specs=P(None, None, "tile", None), check_vma=False
    )
```

profile of v0, /device:TPU:0, one launch (start us, length us, event | category | flops | bytes accessed | tf_op | source)
XLA Modules:
  0.0 60.9 jit_solution(15947746508834809510)
XLA Ops:
  0.0 9.5 %all_gather.3 = f32[4,5,8,8,128]{4,3,2,1,0:T(8,128)S(1)} all-gather(f32[1,5,8,8,128]{4,3,2,1,0:T(8,128)} %param.2), channel_id=1, replica_groups=mesh['section'=4,'tile'=8] {'section'}, dimensions={0}, use_global_device_ids=true | all-gather | bytes 819200 | tf_op jit(solution)/shard_map/all_gather | solution.py:353
  9.5 0.0 copy-start
  9.5 0.7 %copy-done = s32[4]{0:T(128)S(1)} copy-done((s32[4]{0:T(128)S(1)}, s32[4]{0:T(128)}, u32[]{:S(2)}) %copy-start) | copy-done | bytes 40
  10.2 0.7 %pack.1 = (f32[14,5,8,128]{3,2,1,0:T(8,128)S(1)}, f32[4,5,8,128]{3,2,1,0:T(8,128)S(1)}, f32[16,5,8,128]{3,2,1,0:T(8,128)S(1)}, f32[10,5,8,128]{3,2,1,0:T(8,128)S(1)}) custom-call(s32[4]{0:T(128)S(1)} %copy-done, s32[1]{0:T(128)} %bitcast.core, f32[4,5,64,128]{3,2,1,0:T(8,128)S(1)} %bitcast.3), custom_call_target="tpu_custom_call" | custom-call | tf_op jit(solution)/shard_map/pack/pallas_call | solution.py:356
  10.9 4.6 %collective-permute-start = (f32[14,5,8,128]{3,2,1,0:T(8,128)S(1)}, f32[14,5,8,128]{3,2,1,0:T(8,128)S(1)}, u32[]{:S(2)}, u32[]{:S(2)}) collective-permute-start(f32[14,5,8,128]{3,2,1,0:T(8,128)S(1)} %get-tuple-element.11), channel_id=1, source_target_pairs={{0,7},{1,0},{2,1},{3,2},{4,3},{5,4},{6,5},{7,6},{8,9},{9,10},{10,1... | collective-permute-start | bytes 860168 | tf_op jit(solution)/shard_map/ppermute | solution.py:345
  15.5 0.5 collective-permute-start.8
  16.0 8.2 %collective-permute-done.own = f32[14,5,8,128]{3,2,1,0:T(8,128)S(1)} collective-permute-done((f32[14,5,8,128]{3,2,1,0:T(8,128)S(1)}, f32[14,5,8,128]{3,2,1,0:T(8,128)S(1)}, u32[]{:S(2)}, u32[]{:S(2)}) %collective-permute-start) | collective-permute-done | bytes 286752 | tf_op jit(solution)/shard_map/ppermute | solution.py:345
  24.1 0.0 collective-permute-start.2
  24.1 3.6 %collective-permute-start.1 = (f32[4,5,8,128]{3,2,1,0:T(8,128)S(1)}, f32[4,5,8,128]{3,2,1,0:T(8,128)S(1)}, u32[]{:S(2)}, u32[]{:S(2)}) collective-permute-start(f32[4,5,8,128]{3,2,1,0:T(8,128)S(1)} %get-tuple-element.12), channel_id=1, source_target_pairs={{0,6},{1,7},{2,0},{3,1},{4,2},{5,3},{6,4},{7,5},{8,10},{9,11},{10,... | collective-permute-start | bytes 245768 | tf_op jit(solution)/shard_map/ppermute | solution.py:345
  27.7 2.1 %collective-permute-done.1.own2 = f32[4,5,8,128]{3,2,1,0:T(8,128)S(1)} collective-permute-done((f32[4,5,8,128]{3,2,1,0:T(8,128)S(1)}, f32[4,5,8,128]{3,2,1,0:T(8,128)S(1)}, u32[]{:S(2)}, u32[]{:S(2)}) %collective-permute-start.1) | collective-permute-done | bytes 81952 | tf_op jit(solution)/shard_map/ppermute | solution.py:345
  29.8 0.3 collective-permute-start.3
  30.1 3.9 %collective-permute-start.9 = (f32[10,5,8,128]{3,2,1,0:T(8,128)S(1)}, f32[10,5,8,128]{3,2,1,0:T(8,128)S(1)}, u32[]{:S(2)}, u32[]{:S(2)}) collective-permute-start(f32[10,5,8,128]{3,2,1,0:T(8,128)S(1)} %get-tuple-element.16), channel_id=1, source_target_pairs={{0,6},{1,7},{2,0},{3,1},{4,2},{5,3},{6,4},{7,5},{8,10},{9,11},{10,... | collective-permute-start | bytes 614408 | tf_op jit(solution)/shard_map/ppermute | solution.py:345
  34.0 0.0 collective-permute-done.8.l_own
  34.0 0.0 collective-permute-start.10
  34.0 0.0 collective-permute-done.3.other2
  34.0 0.0 collective-permute-done.2.other
  34.0 5.2 %first_step.1 = (f32[8,5,8,128]{3,2,1,0:T(8,128)S(1)}, f32[4,5,8,128]{3,2,1,0:T(8,128)S(1)}) custom-call(s32[4]{0:T(128)S(1)} %copy-done, s32[1]{0:T(128)} %bitcast.core, f32[4,5,64,128]{3,2,1,0:T(8,128)S(1)} %bitcast.4, f32[14,5,8,128]{3,2,1,0:T(8,128)S(1)} %collective-permute-done.own, f32[4,5,8,128]{3,2,1,0:T(8,128)S(1)} %collective-permute-done.1.own2, ...), custom_call_target="tpu_custom_call" | custom-call | tf_op jit(solution)/shard_map/first_step/pallas_call | solution.py:363
  39.2 0.3 collective-permute-start.4
  39.5 0.0 collective-permute-done.9.l_own2
  39.5 0.3 collective-permute-start.11
  39.8 1.7 %collective-permute-start.5 = (f32[4,5,8,128]{3,2,1,0:T(8,128)S(1)}, f32[4,5,8,128]{3,2,1,0:T(8,128)S(1)}, u32[]{:S(2)}, u32[]{:S(2)}) collective-permute-start(f32[4,5,8,128]{3,2,1,0:T(8,128)S(1)} %get-tuple-element.14), channel_id=1, source_target_pairs={{0,6},{1,7},{2,0},{3,1},{4,2},{5,3},{6,4},{7,5},{8,10},{9,11},{10,... | collective-permute-start | bytes 245768 | tf_op jit(solution)/shard_map/ppermute | solution.py:345
  41.6 3.0 %collective-permute-done.4.a_own = f32[8,5,8,128]{3,2,1,0:T(8,128)S(1)} collective-permute-done((f32[8,5,8,128]{3,2,1,0:T(8,128)S(1)}, f32[8,5,8,128]{3,2,1,0:T(8,128)S(1)}, u32[]{:S(2)}, u32[]{:S(2)}) %collective-permute-start.4) | collective-permute-done | bytes 163872 | tf_op jit(solution)/shard_map/ppermute | solution.py:345
  44.6 2.9 %collective-permute-start.6 = (f32[8,5,8,128]{3,2,1,0:T(8,128)S(1)}, f32[8,5,8,128]{3,2,1,0:T(8,128)S(1)}, u32[]{:S(2)}, u32[]{:S(2)}) collective-permute-start(f32[8,5,8,128]{3,2,1,0:T(8,128)S(1)} %collective-permute-done.4.a_own), channel_id=1, source_target_pairs={{0,8},{8,0},{16,24},{24,16},{1,9},{9,1},{17,25},{25,17},{2,10},{10... | collective-permute-start | bytes 491528 | tf_op jit(solution)/shard_map/ppermute | solution.py:348
  47.5 0.0 collective-permute-done.5.a_own2
  47.5 0.0 collective-permute-start.7
  47.5 0.0 collective-permute-done.11.l_other2
  47.5 0.0 collective-permute-done.10.l_other
  47.5 1.3 %collective-permute-done.7.a_other2 = f32[4,5,8,128]{3,2,1,0:T(8,128)S(1)} collective-permute-done((f32[4,5,8,128]{3,2,1,0:T(8,128)S(1)}, f32[4,5,8,128]{3,2,1,0:T(8,128)S(1)}, u32[]{:S(2)}, u32[]{:S(2)}) %collective-permute-start.7) | collective-permute-done | bytes 81952 | tf_op jit(solution)/shard_map/ppermute | solution.py:348
  48.8 0.0 collective-permute-done.6.a_other
  48.8 12.1 %last_steps.1 = f32[5,64,128]{2,1,0:T(8,128)} custom-call(s32[4]{0:T(128)S(1)} %copy-done, s32[1]{0:T(128)} %bitcast.core, f32[4,5,64,128]{3,2,1,0:T(8,128)S(1)} %bitcast.5, f32[8,5,8,128]{3,2,1,0:T(8,128)S(1)} %get-tuple-element.13.adjoint, f32[8,5,8,128]{3,2,1,0:T(8,128)S(1)} %collective-permute-done.4.a_own, ...), custom_call_target="tpu_custom_call" | custom-call | tf_op jit(solution)/shard_map/last_steps/pallas_call | solution.py:373
Async XLA Ops:
  9.5 0.7 %copy-start = (s32[4]{0:T(128)S(1)}, s32[4]{0:T(128)}, u32[]{:S(2)}) copy-start(s32[4]{0:T(128)} %sched.5) | copy-start | bytes 52
  10.9 13.3 %collective-permute-start = (f32[14,5,8,128]{3,2,1,0:T(8,128)S(1)}, f32[14,5,8,128]{3,2,1,0:T(8,128)S(1)}, u32[]{:S(2)}, u32[]{:S(2)}) collective-permute-start(f32[14,5,8,128]{3,2,1,0:T(8,128)S(1)} %get-tuple-element.11), channel_id=1, source_target_pairs={{0,7},{1,0},{2,1},{3,2},{4,3},{5,4},{6,5},{7,6},{8,9},{9,10},{10,1... | collective-permute-start | bytes 860168 | tf_op jit(solution)/shard_map/ppermute | solution.py:345
  15.5 18.5 %collective-permute-start.8 = (f32[16,5,8,128]{3,2,1,0:T(8,128)S(1)}, f32[16,5,8,128]{3,2,1,0:T(8,128)S(1)}, u32[]{:S(2)}, u32[]{:S(2)}) collective-permute-start(f32[16,5,8,128]{3,2,1,0:T(8,128)S(1)} %get-tuple-element.15), channel_id=1, source_target_pairs={{0,7},{1,0},{2,1},{3,2},{4,3},{5,4},{6,5},{7,6},{8,9},{9,10},{10,1... | collective-permute-start | bytes 983048 | tf_op jit(solution)/shard_map/ppermute | solution.py:345
  24.1 9.9 %collective-permute-start.2 = (f32[14,5,8,128]{3,2,1,0:T(8,128)S(1)}, f32[14,5,8,128]{3,2,1,0:T(8,128)S(1)}, u32[]{:S(2)}, u32[]{:S(2)}) collective-permute-start(f32[14,5,8,128]{3,2,1,0:T(8,128)S(1)} %collective-permute-done.own), channel_id=1, source_target_pairs={{0,8},{8,0},{16,24},{24,16},{1,9},{9,1},{17,25},{25,17},{2,10},{10... | collective-permute-start | bytes 860168 | tf_op jit(solution)/shard_map/ppermute | solution.py:348
  24.1 5.7 %collective-permute-start.1 = (f32[4,5,8,128]{3,2,1,0:T(8,128)S(1)}, f32[4,5,8,128]{3,2,1,0:T(8,128)S(1)}, u32[]{:S(2)}, u32[]{:S(2)}) collective-permute-start(f32[4,5,8,128]{3,2,1,0:T(8,128)S(1)} %get-tuple-element.12), channel_id=1, source_target_pairs={{0,6},{1,7},{2,0},{3,1},{4,2},{5,3},{6,4},{7,5},{8,10},{9,11},{10,... | collective-permute-start | bytes 245768 | tf_op jit(solution)/shard_map/ppermute | solution.py:345
  29.8 4.2 %collective-permute-start.3 = (f32[4,5,8,128]{3,2,1,0:T(8,128)S(1)}, f32[4,5,8,128]{3,2,1,0:T(8,128)S(1)}, u32[]{:S(2)}, u32[]{:S(2)}) collective-permute-start(f32[4,5,8,128]{3,2,1,0:T(8,128)S(1)} %collective-permute-done.1.own2), channel_id=1, source_target_pairs={{0,8},{8,0},{16,24},{24,16},{1,9},{9,1},{17,25},{25,17},{2,10},{10... | collective-permute-start | bytes 245768 | tf_op jit(solution)/shard_map/ppermute | solution.py:348
  30.1 9.4 %collective-permute-start.9 = (f32[10,5,8,128]{3,2,1,0:T(8,128)S(1)}, f32[10,5,8,128]{3,2,1,0:T(8,128)S(1)}, u32[]{:S(2)}, u32[]{:S(2)}) collective-permute-start(f32[10,5,8,128]{3,2,1,0:T(8,128)S(1)} %get-tuple-element.16), channel_id=1, source_target_pairs={{0,6},{1,7},{2,0},{3,1},{4,2},{5,3},{6,4},{7,5},{8,10},{9,11},{10,... | collective-permute-start | bytes 614408 | tf_op jit(solution)/shard_map/ppermute | solution.py:345
  34.0 13.5 %collective-permute-start.10 = (f32[16,5,8,128]{3,2,1,0:T(8,128)S(1)}, f32[16,5,8,128]{3,2,1,0:T(8,128)S(1)}, u32[]{:S(2)}, u32[]{:S(2)}) collective-permute-start(f32[16,5,8,128]{3,2,1,0:T(8,128)S(1)} %collective-permute-done.8.l_own), channel_id=1, source_target_pairs={{0,8},{8,0},{16,24},{24,16},{1,9},{9,1},{17,25},{25,17},{2,10},{10... | collective-permute-start | bytes 983048 | tf_op jit(solution)/shard_map/ppermute | solution.py:348
  39.2 5.4 %collective-permute-start.4 = (f32[8,5,8,128]{3,2,1,0:T(8,128)S(1)}, f32[8,5,8,128]{3,2,1,0:T(8,128)S(1)}, u32[]{:S(2)}, u32[]{:S(2)}) collective-permute-start(f32[8,5,8,128]{3,2,1,0:T(8,128)S(1)} %get-tuple-element.13.adjoint), channel_id=1, source_target_pairs={{0,7},{1,0},{2,1},{3,2},{4,3},{5,4},{6,5},{7,6},{8,9},{9,10},{10,1... | collective-permute-start | bytes 491528 | tf_op jit(solution)/shard_map/ppermute | solution.py:345
  39.5 8.0 %collective-permute-start.11 = (f32[10,5,8,128]{3,2,1,0:T(8,128)S(1)}, f32[10,5,8,128]{3,2,1,0:T(8,128)S(1)}, u32[]{:S(2)}, u32[]{:S(2)}) collective-permute-start(f32[10,5,8,128]{3,2,1,0:T(8,128)S(1)} %collective-permute-done.9.l_own2), channel_id=1, source_target_pairs={{0,8},{8,0},{16,24},{24,16},{1,9},{9,1},{17,25},{25,17},{2,10},{10... | collective-permute-start | bytes 614408 | tf_op jit(solution)/shard_map/ppermute | solution.py:348
  39.8 7.7 %collective-permute-start.5 = (f32[4,5,8,128]{3,2,1,0:T(8,128)S(1)}, f32[4,5,8,128]{3,2,1,0:T(8,128)S(1)}, u32[]{:S(2)}, u32[]{:S(2)}) collective-permute-start(f32[4,5,8,128]{3,2,1,0:T(8,128)S(1)} %get-tuple-element.14), channel_id=1, source_target_pairs={{0,6},{1,7},{2,0},{3,1},{4,2},{5,3},{6,4},{7,5},{8,10},{9,11},{10,... | collective-permute-start | bytes 245768 | tf_op jit(solution)/shard_map/ppermute | solution.py:345
  44.6 4.2 %collective-permute-start.6 = (f32[8,5,8,128]{3,2,1,0:T(8,128)S(1)}, f32[8,5,8,128]{3,2,1,0:T(8,128)S(1)}, u32[]{:S(2)}, u32[]{:S(2)}) collective-permute-start(f32[8,5,8,128]{3,2,1,0:T(8,128)S(1)} %collective-permute-done.4.a_own), channel_id=1, source_target_pairs={{0,8},{8,0},{16,24},{24,16},{1,9},{9,1},{17,25},{25,17},{2,10},{10... | collective-permute-start | bytes 491528 | tf_op jit(solution)/shard_map/ppermute | solution.py:348
  47.5 1.3 %collective-permute-start.7 = (f32[4,5,8,128]{3,2,1,0:T(8,128)S(1)}, f32[4,5,8,128]{3,2,1,0:T(8,128)S(1)}, u32[]{:S(2)}, u32[]{:S(2)}) collective-permute-start(f32[4,5,8,128]{3,2,1,0:T(8,128)S(1)} %collective-permute-done.5.a_own2), channel_id=1, source_target_pairs={{0,8},{8,0},{16,24},{24,16},{1,9},{9,1},{17,25},{25,17},{2,10},{10... | collective-permute-start | bytes 245768 | tf_op jit(solution)/shard_map/ppermute | solution.py:348
where the time goes:
time: 61.1 us; the launch traced here: 60.9 us
  starting transfers between devices  18.2 us (30%)
  Pallas kernels  18 us (29%)
  waiting for transfers between devices  14.5 us (24%)
  blocking collectives  9.53 us (16%)
  local copies, waits for them, and re-layouts  0.66 us (1%)
    ppermute x6, starting transfers between devices, shift(): return lax.ppermute(array, ('section', 'tile'), pairs)  14.6 us
    ppermute x6, waiting for transfers between devices, shift(): return lax.ppermute(array, ('section', 'tile'), pairs)  13.3 us
    pallas_call x1, Pallas kernels, body(): second(sched, core, states, adjoint, a_own, a_own2, a_other, a_other2, l_...  12.1 us
    all_gather x1, blocking collectives, body(): states = lax.all_gather(saved[0], 'section', axis=0, tiled=False)  9.53 us
    pallas_call x1, Pallas kernels, body(): adjoint, edge = first(sched, core, states, own, own2, other, other2)  5.2 us
    ppermute x6, starting transfers between devices, swap(): return lax.ppermute(array, 'section', [(s, s ^ 1) for s in range(sections)])  3.56 us
    ppermute x6, waiting for transfers between devices, swap(): return lax.ppermute(array, 'section', [(s, s ^ 1) for s in range(sections)])  1.27 us
  transfers between devices with their start and end apart: 12, of which 4 were waited for; matrix products, arithmetic and copies ran while one was open for 0% of the time, Pallas kernels for 9%

commit v1 on v0

v1 whole, which is shorter than its diff:
```python
import jax
import jax.numpy as jnp
from jax import lax
from jax.experimental import pallas as pl
from jax.experimental.pallas import tpu as pltpu
from jax.sharding import PartitionSpec as P

time_step = 0.1
hyper_coeff = 0.1
slope_unit = time_step / 12.0
hyper_unit = time_step * hyper_coeff
BLOCK = 4
FIELDS, NZ, NY = 5, 8, 128


def roll_y(plane, ahead):
    return pltpu.roll(plane, (-ahead) % NY, 1)


def roll_z(plane, ahead):
    return pltpu.roll(plane, (-ahead) % NZ, 0)


def sum_of(terms):
    return (terms[0] + terms[1]) + terms[2]


def blocks(low, high, visit):
    @pl.loop(0, (high - low) // BLOCK)
    def _(step):
        visit(low + step * BLOCK)


def margin(ref):
    return ref.shape[0] // 2 - 4


def forward_rows(state, slopes, finish):
    reach = margin(slopes)

    def visit(first):
        seen = {}

        def at(row, field):
            if (row, field) not in seen:
                seen[row, field] = state[first + (margin(state) + row), field]
            return seen[row, field]

        for row in range(BLOCK):
            slope, near, far = {}, {}, {}
            for field in range(FIELDS if finish else 4):
                here = at(row, field)
                around = (
                    (at(row + 1, field), at(row - 1, field), at(row + 2, field), at(row - 2, field)),
                    tuple(roll_y(here, k) for k in (1, -1, 2, -2)),
                    tuple(roll_z(here, k) for k in (1, -1, 2, -2)),
                )
                for dim, (up, down, up2, down2) in enumerate(around):
                    slope[field, dim] = 8.0 * (up - down) - (up2 - down2)
                if finish:
                    near[field] = sum_of([a[0] + a[1] for a in around])
                    far[field] = sum_of([a[2] + a[3] for a in around])
            for field in range(4):
                for dim in range(3):
                    slopes[first + (reach + row), field * 3 + dim] = slope[field, dim]
            if not finish:
                continue
            vel = [at(row, dim) * slope_unit for dim in range(3)]
            moved = []
            for field in range(FIELDS):
                value = (1.0 - 18.0 * hyper_unit) * at(row, field)
                value = value + (4.0 * hyper_unit) * near[field] - hyper_unit * far[field]
                if field < 4:
                    value = value - sum_of([vel[dim] * slope[field, dim] for dim in range(3)])
                if field < 3:
                    value = value - slope_unit * slope[4, field]
                if field == 2:
                    value = value + time_step * at(row, 3)
                if field == 3:
                    value = value - time_step * at(row, 2)
                if field == 4:
                    value = value - slope_unit * sum_of([slope[dim, dim] for dim in range(3)])
                moved.append(value)
            finish(first, row, moved)

    blocks(-reach, 8 + reach, visit)


def back_rows(adjoint, state, slopes, reach, finish):
    def visit(first):
        seen_adjoint, seen_vel, seen_prod, seen_hyper = {}, {}, {}, {}

        def adj(row, field):
            if (row, field) not in seen_adjoint:
                seen_adjoint[row, field] = adjoint[first + (margin(adjoint) + row), field]
            return seen_adjoint[row, field]

        def vel(row, dim):
            if (row, dim) not in seen_vel:
                seen_vel[row, dim] = state[first + (margin(state) + row), dim] * slope_unit
            return seen_vel[row, dim]

        def prod(row, field, dim):
            key = (row, field, dim)
            if key not in seen_prod:
                if field < 4:
                    value = vel(row, dim) * adj(row, field)
                    if field == dim:
                        value = value + slope_unit * adj(row, 4)
                else:
                    value = slope_unit * adj(row, dim)
                seen_prod[key] = value
            return seen_prod[key]

        def hyper(row, field):
            if (row, field) not in seen_hyper:
                seen_hyper[row, field] = hyper_unit * adj(row, field)
            return seen_hyper[row, field]

        for row in range(BLOCK):
            pulled = []
            for field in range(FIELDS):

                def up(r, dim):
                    return 4.0 * hyper(r, field) + 8.0 * prod(r, field, dim)

                def down(r, dim):
                    return 4.0 * hyper(r, field) - 8.0 * prod(r, field, dim)

                def up2(r, dim):
                    return prod(r, field, dim) + hyper(r, field)

                def down2(r, dim):
                    return prod(r, field, dim) - hyper(r, field)

                along_x = (up(row + 1, 0) + down(row - 1, 0)) + (down2(row - 2, 0) - up2(row + 2, 0))
                along_y = (roll_y(up(row, 1), 1) + roll_y(down(row, 1), -1)) + (
                    roll_y(down2(row, 1), -2) - roll_y(up2(row, 1), 2)
                )
                along_z = (roll_z(up(row, 2), 1) + roll_z(down(row, 2), -1)) + (
                    roll_z(down2(row, 2), -2) - roll_z(up2(row, 2), 2)
                )
                value = (1.0 - 18.0 * hyper_unit) * adj(row, field) + sum_of([along_x, along_y, along_z])
                if field < 3:
                    s = [adj(row, k) * slopes[first + (margin(slopes) + row), k * 3 + field] for k in range(4)]
                    value = value - slope_unit * ((s[0] + s[1]) + (s[2] + s[3]))
                if field == 2:
                    value = value - time_step * adj(row, 3)
                if field == 3:
                    value = value + time_step * adj(row, 2)
                pulled.append(value)
            finish(first, row, pulled)

    blocks(-reach, 8 + reach, visit)


def store(ref, scale=None):
    def finish(first, row, values):
        for field in range(FIELDS):
            ref[first + (margin(ref) + row), field] = values[field] if scale is None else scale * values[field]

    return finish


def stages(q0, q1, q2, slopes):
    def second(first, row, values):
        for field in range(FIELDS):
            kept = q0[first + (margin(q0) + row), field]
            q2[first + (margin(q2) + row), field] = 0.75 * kept + 0.25 * values[field]

    forward_rows(q0, slopes[0], store(q1))
    forward_rows(q1, slopes[1], second)


def step_back(adjoint, states, slopes, back2, back1, reach, finish):
    back_rows(adjoint, states[2], slopes[2], reach[0], store(back2, 2.0 / 3.0))
    back_rows(back2, states[1], slopes[1], reach[1], store(back1, 0.25))

    def last(first, row, values):
        total = []
        for field in range(FIELDS):
            held = adjoint[first + (margin(adjoint) + row), field] * (1.0 / 3.0)
            total.append((held + 0.75 * back2[first + (margin(back2) + row), field]) + values[field])
        finish(first, row, total)

    back_rows(back1, states[0], slopes[0], reach[2], last)


def clear_sides(ref, inner):
    count = margin(ref) - inner
    zero = jnp.zeros((NZ, NY), jnp.float32)
    for row in list(range(count)) + list(range(ref.shape[0] - count, ref.shape[0])):
        for plane in range(ref.shape[1]):
            ref[row, plane] = zero


def copy_rows(dst, at, src, begin, count):
    for k in range(count):
        for field in range(FIELDS):
            dst[at + k, field] = src[begin + k, field]


def turn(states, mask, source):
    for row in range(8):
        for field in range(FIELDS):
            states[mask, row, field] = source[field, pl.ds(row, NZ, stride=8), :]


def turn_body(sched, saved, place, rows):
    section = lax.axis_index("section")
    place[0] = section & 1
    for mask in range(4):
        place[1 + sched[section ^ mask]] = mask
    turn(rows, 0, saved)


def pack_body(place, rows, beside, across, corner, states, near, next_near, late):
    copy_rows(states.at[0], 0, rows.at[0], 0, 8)
    for mask, source in ((1, beside), (2, across), (3, corner)):
        turn(states, mask, source)
    core = place[0]
    last, goal, middle, start = (states.at[place[1 + group]] for group in (2, 3, 1, 0))
    copy_rows(near, 0, last, 0, 8)
    copy_rows(near, 8, goal, 2 * core, 6)
    copy_rows(near, 14, middle, 2 * core, 6)
    copy_rows(next_near, 0, last, 4 * core, 4)
    copy_rows(next_near, 4, start, 6 * core, 2)
    copy_rows(late, 0, start, 0, 8)


def with_sides(place, own, other, put):
    @pl.when(place[0] == 0)
    def _():
        put(other, own)

    @pl.when(place[0] != 0)
    def _():
        put(own, other)


def first_body(
    place, states, own, own2, other, other2, out, edge, next_edge,
    q0, q1, q2, goal, last, qb2, qb1, qs0, qs1, qs2, lam, p0, p1, p2, pb2, pb1, ps0, ps1, ps2,
):
    copy_rows(q0, 12, states.at[place[3]], 0, 8)
    copy_rows(goal, 6, states.at[place[4]], 0, 8)
    copy_rows(p0, 8, states.at[place[2]], 0, 8)

    def put(below, above):
        (b1, b2), (a1, a2) = below, above
        copy_rows(q0, 0, b2, 0, 4)
        copy_rows(q0, 4, b1, 0, 8)
        copy_rows(q0, 20, a1, 0, 8)
        copy_rows(q0, 28, a2, 0, 4)
        copy_rows(goal, 0, b1, 8, 6)
        copy_rows(goal, 14, a1, 8, 6)
        copy_rows(p0, 2, b1, 14, 6)
        copy_rows(p0, 16, a1, 14, 6)

    with_sides(place, (own, own2), (other, other2), put)
    for ref, inner in ((p0, 6), (p1, 4), (p2, 2), (ps0, 4), (ps1, 2), (ps2, 0), (lam, 0), (pb2, 2), (pb1, 4)):
        clear_sides(ref, inner)
    stages(q0, q1, q2, (qs0, qs1))

    def misfit(first, row, values):
        for field in range(FIELDS):
            state = q0[first + (12 + row), field] * (1.0 / 3.0) + (2.0 / 3.0) * values[field]
            last[first + (6 + row), field] = state - goal[first + (6 + row), field]

    forward_rows(q2, qs2, misfit)
    step_back(last, (q0, q1, q2), (qs0, qs1, qs2), qb2, qb1, (4, 2, 0), store(lam))
    inner = [ref.at[pl.ds(2, ref.shape[0] - 4)] for ref in (p0, p1, p2, ps0, ps1, ps2)]
    stages(*inner[:3], inner[3:5])
    forward_rows(inner[2], inner[5], None)
    step_back(lam, (p0, p1, p2), (ps0, ps1, ps2), pb2, pb1, (2, 4, 6), store(out))
    copy_rows(edge, 0, out, 8 * place[0], 12)
    copy_rows(next_edge, 0, out, 16 * place[0], 4)


def ahead_body(place, states, own, own2, other, other2, after, x0, x1, x2, xs0, xs1, xs2):
    copy_rows(x0, 10, states.at[place[1]], 0, 8)

    def put(below, above):
        (b1, b2), (a1, a2) = below, above
        copy_rows(x0, 0, b2, 4, 2)
        copy_rows(x0, 2, b1, 0, 8)
        copy_rows(x0, 18, a1, 0, 8)
        copy_rows(x0, 26, a2, 4, 2)

    with_sides(place, (own, own2), (other, other2), put)
    stages(x0, x1, x2, (xs0, xs1))
    forward_rows(x2, xs2, None)


def last_body(place, share, own, own2, other, other2, x0, x1, x2, xs0, xs1, xs2, out, lam, back2, back1):
    def put(below, above):
        (b1, b2), (a1, a2) = below, above
        for row in range(20):
            for field in range(FIELDS):
                value = share[row, field]
                if row < 12:
                    value = value + b1[row, field]
                if row < 4:
                    value = value + b2[row, field]
                if row >= 8:
                    value = value + a1[row - 8, field]
                if row >= 16:
                    value = value + a2[row - 16, field]
                lam[row, field] = value

    with_sides(place, (own, own2), (other, other2), put)

    def finish(first, row, values):
        for field in range(FIELDS):
            out[field, pl.ds(first + row, NZ, stride=8), :] = values[field]

    step_back(lam, (x0, x1, x2), (xs0, xs1, xs2), back2, back1, (4, 2, 0), finish)


def block(count, planes=FIELDS):
    return (count, planes, NZ, NY)


def kernel(body, name, arrays, outs, scratch=(), place=0, micros=1, megabytes=16):
    smem, vmem = pl.BlockSpec(memory_space=pltpu.SMEM), pl.BlockSpec(memory_space=pltpu.VMEM)
    shapes = [jax.ShapeDtypeStruct(shape, jnp.float32) for shape in outs]
    return pl.pallas_call(
        body,
        out_shape=[jax.ShapeDtypeStruct((place,), jnp.int32)] * bool(place) + shapes,
        in_specs=[smem] + [vmem] * arrays,
        out_specs=[smem] * bool(place) + [vmem] * len(outs),
        scratch_shapes=[pltpu.VMEM(shape, jnp.float32) for shape in scratch],
        compiler_params=pltpu.CompilerParams(vmem_limit_bytes=megabytes * 1024 * 1024),
        cost_estimate=pl.CostEstimate(flops=micros * 4_000_000, bytes_accessed=micros * 3_000_000, transcendentals=0),
        name=name,
    )


def body(saved, sched):
    sections, tiles = lax.axis_size("section"), lax.axis_size("tile")

    def shift(array, hops):
        pairs = []
        for s in range(sections):
            for t in range(tiles):
                to = (t - hops if s % 2 == 0 else t + hops) % tiles
                pairs.append((s * tiles + t, s * tiles + to))
        return lax.ppermute(array, ("section", "tile"), pairs)

    def swap(array, mask=1):
        return lax.ppermute(array, "section", [(s, s ^ mask) for s in range(sections)])

    mine = saved.reshape(FIELDS, NZ * 8, NY)
    across = swap(mine, 2)
    beside = swap(mine, 1)
    place, rows = kernel(turn_body, "turn", 1, [(1, *block(8))], place=5)(sched, mine)
    across, place, rows = lax.optimization_barrier((across, place, rows))
    corner = swap(across, 1)
    states, near, next_near, late = kernel(pack_body, "pack", 4, [(4, *block(8)), block(20), block(6), block(8)])(
        place, rows, beside, across, corner
    )
    own, own2 = lax.optimization_barrier((shift(near, 1), shift(next_near, 2)))
    late, own = lax.optimization_barrier((late, own))
    l_own = shift(late, 1)
    other, other2 = swap(own), swap(own2)
    share, edge, next_edge = kernel(
        first_body, "first_steps", 5, [block(20), block(12), block(4)],
        [block(32), block(28), block(24), block(20), block(20), block(16), block(12)]
        + [block(28, 12), block(24, 12), block(20, 12)]
        + [block(20), block(24), block(20), block(16), block(20), block(24)]
        + [block(20, 12), block(16, 12), block(12, 12)], micros=7,
    )(place, states, own, own2, other, other2)
    a_own, a_own2 = shift(edge, 1), shift(next_edge, 2)
    l_own, after = lax.optimization_barrier((l_own, next_edge))
    l_other = swap(l_own)
    stage = [block(28), block(24), block(20), block(24, 12), block(20, 12), block(16, 12)]
    held = kernel(ahead_body, "ahead", 6, stage, micros=2)(place, states, l_own, own2, l_other, other2, after)
    a_own, a_own2, *held = lax.optimization_barrier((a_own, a_own2, *held))
    a_other, a_other2 = swap(a_own), swap(a_own2)
    (gradient,) = kernel(
        last_body, "last_step", 11, [(FIELDS, NZ * 8, NY)], [block(20), block(16), block(12)], micros=2
    )(place, share, a_own, a_own2, a_other, a_other2, *held)
    return gradient.reshape(FIELDS, NZ, 8, NY)


def solution(mesh):
    placed = (P("section", None, None, "tile", None), P())
    return jax.shard_map(
        body, mesh=mesh, in_specs=placed, out_specs=P(None, None, "tile", None), check_vma=False
    )
```

time: 61.1 us -> 47.9 us (0.78)
  blocking collectives: 9.53 us -> 0 us
  starting transfers between devices: 18.2 us -> 15.1 us
  Pallas kernels: 18 us -> 16.5 us
  local copies, waits for them, and re-layouts: 0.66 us -> 1.6 us
    all_gather x1 -> x0, blocking collectives: 9.53 us -> none  [body(): states = lax.all_gather(saved[0], 'section', axis=0, tiled=False)]
    ppermute x6 -> x8, waiting for transfers between devices: 1.27 us -> 5.08 us  [swap(): lax.ppermute(array, 'section', [(s, s ^ mask) for s in range(sections)])]
    ppermute x6 -> x5, waiting for transfers between devices: 13.3 us -> 9.5 us  [shift(): return lax.ppermute(array, ('section', 'tile'), pairs)]
    ppermute x6 -> x5, starting transfers between devices: 14.6 us -> 11.1 us  [shift(): return lax.ppermute(array, ('section', 'tile'), pairs)]
    pallas_call x3 -> x5, Pallas kernels: 18 us -> 16.5 us  [the longest x1 8.75 us: body(): kernel(first_body, 'first_steps', 5, [block(20), block(12), block(4)], [b...]
    unnamed x2 -> x4, local copies, waits for them, and re-layouts: 0.66 us -> 1.6 us
    ppermute x6 -> x8, starting transfers between devices: 3.56 us -> 3.97 us  [swap(): lax.ppermute(array, 'section', [(s, s ^ mask) for s in range(sections)])]
  transfers between devices with their start and end apart: 12 -> 13, of which waited for: 4 -> 8; matrix products, arithmetic and copies ran while one was open for 0% -> 0% of each run, Pallas kernels for 9% -> 27%
where the time goes in v1:
time: 47.9 us; the launch traced here: 47.8 us
  Pallas kernels  16.5 us (34%)
  starting transfers between devices  15.1 us (32%)
  waiting for transfers between devices  14.6 us (30%)
  local copies, waits for them, and re-layouts  1.6 us (3%)
    ppermute x5, starting transfers between devices, shift(): return lax.ppermute(array, ('section', 'tile'), pairs)  11.1 us
    ppermute x5, waiting for transfers between devices, shift(): return lax.ppermute(array, ('section', 'tile'), pairs)  9.5 us
    pallas_call x1, Pallas kernels, body(): kernel(first_body, 'first_steps', 5, [block(20), block(12), block(4)], [b...  8.75 us
    ppermute x8, waiting for transfers between devices, swap(): lax.ppermute(array, 'section', [(s, s ^ mask) for s in range(sections)])  5.08 us
    ppermute x8, starting transfers between devices, swap(): lax.ppermute(array, 'section', [(s, s ^ mask) for s in range(sections)])  3.97 us
    pallas_call x1, Pallas kernels, body(): kernel(ahead_body, 'ahead', 6, stage, micros=2)  2.96 us
    pallas_call x1, Pallas kernels, body(): kernel(last_body, 'last_step', 11, [(FIELDS, NZ * 8, NY)], [block(20), bl...  2.9 us
    unnamed x4, local copies, waits for them, and re-layouts  1.6 us
  transfers between devices with their start and end apart: 13, of which 8 were waited for; matrix products, arithmetic and copies ran while one was open for 0% of the time, Pallas kernels for 27%

profile of v1, /device:TPU:0, one launch (start us, length us, event | category | flops | bytes accessed | tf_op | source)
XLA Modules:
  0.0 47.8 jit_solution(17537472950355859984)
XLA Ops:
  0.0 2.9 %collective-permute-start = (f32[5,64,128]{2,1,0:T(8,128)}, f32[5,64,128]{2,1,0:T(8,128)S(1)}, u32[]{:S(2)}, u32[]{:S(2)}) collective-permute-start(f32[5,64,128]{2,1,0:T(8,128)} %bitcast.2), channel_id=1, source_target_pairs={{0,16},{8,24},{16,0},{24,8},{1,17},{9,25},{17,1},{25,9},{2,18},{10... | collective-permute-start | bytes 491528 | tf_op jit(solution)/shard_map/ppermute | solution.py:351
  2.9 0.0 collective-permute-start.1
  2.9 0.9 %copy-done = f32[1,5,8,8,128]{4,3,2,1,0:T(8,128)S(1)} copy-done((f32[1,5,8,8,128]{4,3,2,1,0:T(8,128)S(1)}, f32[1,5,8,8,128]{4,3,2,1,0:T(8,128)}, u32[]{:S(2)}) %copy-start) | copy-done | bytes 163864
  3.9 0.7 %copy-done.1 = s32[4]{0:T(128)S(1)} copy-done((s32[4]{0:T(128)S(1)}, s32[4]{0:T(128)}, u32[]{:S(2)}) %copy-start.1) | copy-done | bytes 40
  4.5 1.2 %turn.1 = (s32[5]{0:T(128)S(1)}, f32[1,8,5,8,128]{4,3,2,1,0:T(8,128)S(1)}) custom-call(s32[4]{0:T(128)S(1)} %copy-done.1, f32[5,64,128]{2,1,0:T(8,128)S(1)} %bitcast.4), custom_call_target="tpu_custom_call" | custom-call | flops 4000000 | bytes 3000000 | tf_op jit(solution)/shard_map/turn/pallas_call | solution.py:356
  5.7 1.6 %collective-permute-done.across = f32[5,64,128]{2,1,0:T(8,128)S(1)} collective-permute-done((f32[5,64,128]{2,1,0:T(8,128)}, f32[5,64,128]{2,1,0:T(8,128)S(1)}, u32[]{:S(2)}, u32[]{:S(2)}) %collective-permute-start) | collective-permute-done | bytes 163872 | tf_op jit(solution)/shard_map/ppermute | solution.py:351
  7.3 0.0 collective-permute-start.2
  7.3 0.0 collective-permute-done.1.beside
  7.4 1.4 %collective-permute-done.2.corner = f32[5,64,128]{2,1,0:T(8,128)S(1)} collective-permute-done((f32[5,64,128]{2,1,0:T(8,128)S(1)}, f32[5,64,128]{2,1,0:T(8,128)S(1)}, u32[]{:S(2)}, u32[]{:S(2)}) %collective-permute-start.2) | collective-permute-done | bytes 163872 | tf_op jit(solution)/shard_map/ppermute | solution.py:351
  8.7 0.7 %pack.1 = (f32[4,8,5,8,128]{4,3,2,1,0:T(8,128)S(1)}, f32[20,5,8,128]{3,2,1,0:T(8,128)S(1)}, f32[6,5,8,128]{3,2,1,0:T(8,128)S(1)}, f32[8,5,8,128]{3,2,1,0:T(8,128)S(1)}) custom-call(s32[5]{0:T(128)S(1)} %get-tuple-element.39.place, f32[1,8,5,8,128]{4,3,2,1,0:T(8,128)S(1)} %get-tuple-element.40.rows, f32[5,64,128]{2,1,0:T(8,128)S(1)} %collective-permute-done.1.beside, ...), custom_call_target="tpu_custom_call" | custom-call | flops 4000000 | bytes 3000000 | tf_op jit(solution)/shard_map/pack/pallas_call | solution.py:359
  9.4 4.9 %collective-permute-start.3 = (f32[20,5,8,128]{3,2,1,0:T(8,128)S(1)}, f32[20,5,8,128]{3,2,1,0:T(8,128)S(1)}, u32[]{:S(2)}, u32[]{:S(2)}) collective-permute-start(f32[20,5,8,128]{3,2,1,0:T(8,128)S(1)} %get-tuple-element.44), channel_id=1, source_target_pairs={{0,7},{1,0},{2,1},{3,2},{4,3},{5,4},{6,5},{7,6},{8,9},{9,10},{10,1... | collective-permute-start | bytes 1228808 | tf_op jit(solution)/shard_map/ppermute | solution.py:348
  14.3 0.4 collective-permute-start.4
  14.8 6.6 %collective-permute-done.4.own2 = f32[6,5,8,128]{3,2,1,0:T(8,128)S(1)} collective-permute-done((f32[6,5,8,128]{3,2,1,0:T(8,128)S(1)}, f32[6,5,8,128]{3,2,1,0:T(8,128)S(1)}, u32[]{:S(2)}, u32[]{:S(2)}) %collective-permute-start.4) | collective-permute-done | bytes 122912 | tf_op jit(solution)/shard_map/ppermute | solution.py:348
  21.4 0.5 collective-permute-done.3.own
  21.8 0.0 collective-permute-start.5
  21.8 0.5 %collective-permute-start.6 = (f32[6,5,8,128]{3,2,1,0:T(8,128)S(1)}, f32[6,5,8,128]{3,2,1,0:T(8,128)S(1)}, u32[]{:S(2)}, u32[]{:S(2)}) collective-permute-start(f32[6,5,8,128]{3,2,1,0:T(8,128)S(1)} %collective-permute-done.4.own2), channel_id=1, source_target_pairs={{0,8},{8,0},{16,24},{24,16},{1,9},{9,1},{17,25},{25,17},{2,10},{10... | collective-permute-start | bytes 368648 | tf_op jit(solution)/shard_map/ppermute | solution.py:351
  22.3 3.3 %collective-permute-start.9 = (f32[8,5,8,128]{3,2,1,0:T(8,128)S(1)}, f32[8,5,8,128]{3,2,1,0:T(8,128)S(1)}, u32[]{:S(2)}, u32[]{:S(2)}) collective-permute-start(f32[8,5,8,128]{3,2,1,0:T(8,128)S(1)} %get-tuple-element.52), channel_id=1, source_target_pairs={{0,7},{1,0},{2,1},{3,2},{4,3},{5,4},{6,5},{7,6},{8,9},{9,10},{10,1... | collective-permute-start | bytes 491528 | tf_op jit(solution)/shard_map/ppermute | solution.py:348
  25.6 0.0 collective-permute-done.6.other2
  25.6 0.0 collective-permute-done.5.other
  25.6 8.7 %first_steps.1 = (f32[20,5,8,128]{3,2,1,0:T(8,128)S(1)}, f32[12,5,8,128]{3,2,1,0:T(8,128)S(1)}, f32[4,5,8,128]{3,2,1,0:T(8,128)S(1)}) custom-call(s32[5]{0:T(128)S(1)} %get-tuple-element.39.place, f32[4,8,5,8,128]{4,3,2,1,0:T(8,128)S(1)} %get-tuple-element.42.states, f32[20,5,8,128]{3,2,1,0:T(8,128)S(1)} %collective-permute-done.3.own, ...), custom_call_target="tpu_custom_call" | custom-call | flops 28000000 | bytes 21000000 | tf_op jit(solution)/shard_map/first_steps/pallas_call | solution.py:366
  34.4 2.1 %collective-permute-start.7 = (f32[12,5,8,128]{3,2,1,0:T(8,128)S(1)}, f32[12,5,8,128]{3,2,1,0:T(8,128)S(1)}, u32[]{:S(2)}, u32[]{:S(2)}) collective-permute-start(f32[12,5,8,128]{3,2,1,0:T(8,128)S(1)} %get-tuple-element.50), channel_id=1, source_target_pairs={{0,7},{1,0},{2,1},{3,2},{4,3},{5,4},{6,5},{7,6},{8,9},{9,10},{10,1... | collective-permute-start | bytes 737288 | tf_op jit(solution)/shard_map/ppermute | solution.py:348
  36.5 0.0 collective-permute-done.9.own
  36.5 0.5 collective-permute-start.8
  36.9 0.9 %collective-permute-done.10.other = f32[8,5,8,128]{3,2,1,0:T(8,128)S(1)} collective-permute-done((f32[8,5,8,128]{3,2,1,0:T(8,128)S(1)}, f32[8,5,8,128]{3,2,1,0:T(8,128)S(1)}, u32[]{:S(2)}, u32[]{:S(2)}) %collective-permute-start.10) | collective-permute-done | bytes 163872 | tf_op jit(solution)/shard_map/ppermute | solution.py:351
  37.9 3.0 %ahead.1 = (f32[28,5,8,128]{3,2,1,0:T(8,128)S(1)}, f32[24,5,8,128]{3,2,1,0:T(8,128)S(1)}, f32[20,5,8,128]{3,2,1,0:T(8,128)S(1)}, f32[24,12,8,128]{3,2,1,0:T(8,12...) custom-call(s32[5]{0:T(128)S(1)} %get-tuple-element.39.place, ...), custom_call_target="tpu_custom_call" | custom-call | flops 8000000 | bytes 6000000 | tf_op jit(solution)/shard_map/ahead/pallas_call | solution.py:377
  40.8 0.9 %collective-permute-done.8.own2 = f32[4,5,8,128]{3,2,1,0:T(8,128)S(1)} collective-permute-done((f32[4,5,8,128]{3,2,1,0:T(8,128)S(1)}, f32[4,5,8,128]{3,2,1,0:T(8,128)S(1)}, u32[]{:S(2)}, u32[]{:S(2)}) %collective-permute-start.8) | collective-permute-done | bytes 81952 | tf_op jit(solution)/shard_map/ppermute | solution.py:348
  41.8 1.5 %collective-permute-done.7.own = f32[12,5,8,128]{3,2,1,0:T(8,128)S(1)} collective-permute-done((f32[12,5,8,128]{3,2,1,0:T(8,128)S(1)}, f32[12,5,8,128]{3,2,1,0:T(8,128)S(1)}, u32[]{:S(2)}, u32[]{:S(2)}) %collective-permute-start.7) | collective-permute-done | bytes 245792 | tf_op jit(solution)/shard_map/ppermute | solution.py:348
  43.3 0.0 collective-permute-start.11
  43.3 0.5 %collective-permute-start.12 = (f32[4,5,8,128]{3,2,1,0:T(8,128)S(1)}, f32[4,5,8,128]{3,2,1,0:T(8,128)S(1)}, u32[]{:S(2)}, u32[]{:S(2)}) collective-permute-start(f32[4,5,8,128]{3,2,1,0:T(8,128)S(1)} %collective-permute-done.8.own2), channel_id=1, source_target_pairs={{0,8},{8,0},{16,24},{24,16},{1,9},{9,1},{17,25},{25,17},{2,10},{10... | collective-permute-start | bytes 245768 | tf_op jit(solution)/shard_map/ppermute | solution.py:351
  43.8 1.1 %collective-permute-done.12.other2 = f32[4,5,8,128]{3,2,1,0:T(8,128)S(1)} collective-permute-done((f32[4,5,8,128]{3,2,1,0:T(8,128)S(1)}, f32[4,5,8,128]{3,2,1,0:T(8,128)S(1)}, u32[]{:S(2)}, u32[]{:S(2)}) %collective-permute-start.12) | collective-permute-done | bytes 81952 | tf_op jit(solution)/shard_map/ppermute | solution.py:351
  44.9 0.0 collective-permute-done.11.other
  44.9 2.9 %last_step.1 = f32[5,64,128]{2,1,0:T(8,128)} custom-call(s32[5]{0:T(128)S(1)} %get-tuple-element.39.place, f32[20,5,8,128]{3,2,1,0:T(8,128)S(1)} %get-tuple-element.49.share, f32[12,5,8,128]{3,2,1,0:T(8,128)S(1)} %collective-permute-done.7.own, f32[4,5,8,128]{3,2,1,0:T(8,128)S(1)} %collective-permute-done.8.own2, ...), custom_call_target="tpu_custom_call" | custom-call | flops 8000000 | bytes 6000000 | tf_op jit(solution)/shard_map/last_step/pallas_call | solution.py:380
  (3 shorter events, 0.0 us)
Async XLA Ops:
  0.0 7.3 %collective-permute-start = (f32[5,64,128]{2,1,0:T(8,128)}, f32[5,64,128]{2,1,0:T(8,128)S(1)}, u32[]{:S(2)}, u32[]{:S(2)}) collective-permute-start(f32[5,64,128]{2,1,0:T(8,128)} %bitcast.2), channel_id=1, source_target_pairs={{0,16},{8,24},{16,0},{24,8},{1,17},{9,25},{17,1},{25,9},{2,18},{10... | collective-permute-start | bytes 491528 | tf_op jit(solution)/shard_map/ppermute | solution.py:351
  2.9 4.4 %collective-permute-start.1 = (f32[5,64,128]{2,1,0:T(8,128)}, f32[5,64,128]{2,1,0:T(8,128)S(1)}, u32[]{:S(2)}, u32[]{:S(2)}) collective-permute-start(f32[5,64,128]{2,1,0:T(8,128)} %bitcast.3), channel_id=1, source_target_pairs={{0,8},{8,0},{16,24},{24,16},{1,9},{9,1},{17,25},{25,17},{2,10},{10... | collective-permute-start | bytes 491528 | tf_op jit(solution)/shard_map/ppermute | solution.py:351
  2.9 0.9 %copy-start = (f32[1,5,8,8,128]{4,3,2,1,0:T(8,128)S(1)}, f32[1,5,8,8,128]{4,3,2,1,0:T(8,128)}, u32[]{:S(2)}) copy-start(f32[1,5,8,8,128]{4,3,2,1,0:T(8,128)} %param.2) | copy-start | bytes 491524
  3.9 0.7 %copy-start.1 = (s32[4]{0:T(128)S(1)}, s32[4]{0:T(128)}, u32[]{:S(2)}) copy-start(s32[4]{0:T(128)} %sched.1) | copy-start | bytes 52
  7.3 1.4 %collective-permute-start.2 = (f32[5,64,128]{2,1,0:T(8,128)S(1)}, f32[5,64,128]{2,1,0:T(8,128)S(1)}, u32[]{:S(2)}, u32[]{:S(2)}) collective-permute-start(f32[5,64,128]{2,1,0:T(8,128)S(1)} %collective-permute-done.across), channel_id=1, source_target_pairs={{0,8},{8,0},{16,24},{24,16},{1,9},{9,1},{17,25},{25,17},{2,10},{10... | collective-permute-start | bytes 491528 | tf_op jit(solution)/shard_map/ppermute | solution.py:351
  9.4 12.4 %collective-permute-start.3 = (f32[20,5,8,128]{3,2,1,0:T(8,128)S(1)}, f32[20,5,8,128]{3,2,1,0:T(8,128)S(1)}, u32[]{:S(2)}, u32[]{:S(2)}) collective-permute-start(f32[20,5,8,128]{3,2,1,0:T(8,128)S(1)} %get-tuple-element.44), channel_id=1, source_target_pairs={{0,7},{1,0},{2,1},{3,2},{4,3},{5,4},{6,5},{7,6},{8,9},{9,10},{10,1... | collective-permute-start | bytes 1228808 | tf_op jit(solution)/shard_map/ppermute | solution.py:348
  14.3 7.1 %collective-permute-start.4 = (f32[6,5,8,128]{3,2,1,0:T(8,128)S(1)}, f32[6,5,8,128]{3,2,1,0:T(8,128)S(1)}, u32[]{:S(2)}, u32[]{:S(2)}) collective-permute-start(f32[6,5,8,128]{3,2,1,0:T(8,128)S(1)} %get-tuple-element.45), channel_id=1, source_target_pairs={{0,6},{1,7},{2,0},{3,1},{4,2},{5,3},{6,4},{7,5},{8,10},{9,11},{10,... | collective-permute-start | bytes 368648 | tf_op jit(solution)/shard_map/ppermute | solution.py:348
  21.8 3.8 %collective-permute-start.5 = (f32[20,5,8,128]{3,2,1,0:T(8,128)S(1)}, f32[20,5,8,128]{3,2,1,0:T(8,128)S(1)}, u32[]{:S(2)}, u32[]{:S(2)}) collective-permute-start(f32[20,5,8,128]{3,2,1,0:T(8,128)S(1)} %collective-permute-done.3.own), channel_id=1, source_target_pairs={{0,8},{8,0},{16,24},{24,16},{1,9},{9,1},{17,25},{25,17},{2,10},{10... | collective-permute-start | bytes 1228808 | tf_op jit(solution)/shard_map/ppermute | solution.py:351
  21.8 3.8 %collective-permute-start.6 = (f32[6,5,8,128]{3,2,1,0:T(8,128)S(1)}, f32[6,5,8,128]{3,2,1,0:T(8,128)S(1)}, u32[]{:S(2)}, u32[]{:S(2)}) collective-permute-start(f32[6,5,8,128]{3,2,1,0:T(8,128)S(1)} %collective-permute-done.4.own2), channel_id=1, source_target_pairs={{0,8},{8,0},{16,24},{24,16},{1,9},{9,1},{17,25},{25,17},{2,10},{10... | collective-permute-start | bytes 368648 | tf_op jit(solution)/shard_map/ppermute | solution.py:351
  22.3 14.1 %collective-permute-start.9 = (f32[8,5,8,128]{3,2,1,0:T(8,128)S(1)}, f32[8,5,8,128]{3,2,1,0:T(8,128)S(1)}, u32[]{:S(2)}, u32[]{:S(2)}) collective-permute-start(f32[8,5,8,128]{3,2,1,0:T(8,128)S(1)} %get-tuple-element.52), channel_id=1, source_target_pairs={{0,7},{1,0},{2,1},{3,2},{4,3},{5,4},{6,5},{7,6},{8,9},{9,10},{10,1... | collective-permute-start | bytes 491528 | tf_op jit(solution)/shard_map/ppermute | solution.py:348
  34.4 8.9 %collective-permute-start.7 = (f32[12,5,8,128]{3,2,1,0:T(8,128)S(1)}, f32[12,5,8,128]{3,2,1,0:T(8,128)S(1)}, u32[]{:S(2)}, u32[]{:S(2)}) collective-permute-start(f32[12,5,8,128]{3,2,1,0:T(8,128)S(1)} %get-tuple-element.50), channel_id=1, source_target_pairs={{0,7},{1,0},{2,1},{3,2},{4,3},{5,4},{6,5},{7,6},{8,9},{9,10},{10,1... | collective-permute-start | bytes 737288 | tf_op jit(solution)/shard_map/ppermute | solution.py:348
  36.5 1.4 %collective-permute-start.10 = (f32[8,5,8,128]{3,2,1,0:T(8,128)S(1)}, f32[8,5,8,128]{3,2,1,0:T(8,128)S(1)}, u32[]{:S(2)}, u32[]{:S(2)}) collective-permute-start(f32[8,5,8,128]{3,2,1,0:T(8,128)S(1)} %collective-permute-done.9.own), channel_id=1, source_target_pairs={{0,8},{8,0},{16,24},{24,16},{1,9},{9,1},{17,25},{25,17},{2,10},{10... | collective-permute-start | bytes 491528 | tf_op jit(solution)/shard_map/ppermute | solution.py:351
  36.5 5.3 %collective-permute-start.8 = (f32[4,5,8,128]{3,2,1,0:T(8,128)S(1)}, f32[4,5,8,128]{3,2,1,0:T(8,128)S(1)}, u32[]{:S(2)}, u32[]{:S(2)}) collective-permute-start(f32[4,5,8,128]{3,2,1,0:T(8,128)S(1)} %get-tuple-element.54.after), channel_id=1, source_target_pairs={{0,6},{1,7},{2,0},{3,1},{4,2},{5,3},{6,4},{7,5},{8,10},{9,11},{10,... | collective-permute-start | bytes 245768 | tf_op jit(solution)/shard_map/ppermute | solution.py:348
  43.3 1.6 %collective-permute-start.11 = (f32[12,5,8,128]{3,2,1,0:T(8,128)S(1)}, f32[12,5,8,128]{3,2,1,0:T(8,128)S(1)}, u32[]{:S(2)}, u32[]{:S(2)}) collective-permute-start(f32[12,5,8,128]{3,2,1,0:T(8,128)S(1)} %collective-permute-done.7.own), channel_id=1, source_target_pairs={{0,8},{8,0},{16,24},{24,16},{1,9},{9,1},{17,25},{25,17},{2,10},{10... | collective-permute-start | bytes 737288 | tf_op jit(solution)/shard_map/ppermute | solution.py:351
  43.3 1.6 %collective-permute-start.12 = (f32[4,5,8,128]{3,2,1,0:T(8,128)S(1)}, f32[4,5,8,128]{3,2,1,0:T(8,128)S(1)}, u32[]{:S(2)}, u32[]{:S(2)}) collective-permute-start(f32[4,5,8,128]{3,2,1,0:T(8,128)S(1)} %collective-permute-done.8.own2), channel_id=1, source_target_pairs={{0,8},{8,0},{16,24},{24,16},{1,9},{9,1},{17,25},{25,17},{2,10},{10... | collective-permute-start | bytes 245768 | tf_op jit(solution)/shard_map/ppermute | solution.py:351

commit v2 on v1

--- a/solution.py
+++ b/solution.py
@@ -9,7 +9,7 @@
 hyper_coeff = 0.1
 slope_unit = time_step / 12.0
 hyper_unit = time_step * hyper_coeff
-BLOCK = 4
+BLOCK = 28
 FIELDS, NZ, NY = 5, 8, 128
 
 
@@ -26,9 +26,11 @@
 
 
 def blocks(low, high, visit):
-    @pl.loop(0, (high - low) // BLOCK)
+    size = max(k for k in range(1, BLOCK + 1) if (high - low) % k == 0)
+
+    @pl.loop(0, (high - low) // size)
     def _(step):
-        visit(low + step * BLOCK)
+        visit(low + step * size, size)
 
 
 def margin(ref):
@@ -38,7 +40,7 @@
 def forward_rows(state, slopes, finish):
     reach = margin(slopes)
 
-    def visit(first):
+    def visit(first, size):
         seen = {}
 
         def at(row, field):
@@ -46,7 +48,7 @@
                 seen[row, field] = state[first + (margin(state) + row), field]
             return seen[row, field]
 
-        for row in range(BLOCK):
+        for row in range(size):
             slope, near, far = {}, {}, {}
             for field in range(FIELDS if finish else 4):
                 here = at(row, field)
@@ -87,7 +89,7 @@
 
 
 def back_rows(adjoint, state, slopes, reach, finish):
-    def visit(first):
+    def visit(first, size):
         seen_adjoint, seen_vel, seen_prod, seen_hyper = {}, {}, {}, {}
 
         def adj(row, field):
@@ -117,7 +119,7 @@
                 seen_hyper[row, field] = hyper_unit * adj(row, field)
             return seen_hyper[row, field]
 
-        for row in range(BLOCK):
+        for row in range(size):
             pulled = []
             for field in range(FIELDS):
 
@@ -214,17 +216,17 @@
     turn(rows, 0, saved)
 
 
-def pack_body(place, rows, beside, across, corner, states, near, next_near, late):
+def pack_body(place, rows, beside, across, corner, states, near, next_near, soon, late):
     copy_rows(states.at[0], 0, rows.at[0], 0, 8)
     for mask, source in ((1, beside), (2, across), (3, corner)):
         turn(states, mask, source)
     core = place[0]
     last, goal, middle, start = (states.at[place[1 + group]] for group in (2, 3, 1, 0))
     copy_rows(near, 0, last, 0, 8)
-    copy_rows(near, 8, goal, 2 * core, 6)
-    copy_rows(near, 14, middle, 2 * core, 6)
     copy_rows(next_near, 0, last, 4 * core, 4)
     copy_rows(next_near, 4, start, 6 * core, 2)
+    copy_rows(soon, 0, goal, 2 * core, 6)
+    copy_rows(soon, 6, middle, 2 * core, 6)
     copy_rows(late, 0, start, 0, 8)
 
 
@@ -238,13 +240,8 @@
         put(own, other)
 
 
-def first_body(
-    place, states, own, own2, other, other2, out, edge, next_edge,
-    q0, q1, q2, goal, last, qb2, qb1, qs0, qs1, qs2, lam, p0, p1, p2, pb2, pb1, ps0, ps1, ps2,
-):
+def forward_body(place, states, own, own2, other, other2, end, q0, q1, q2, qs0, qs1, qs2):
     copy_rows(q0, 12, states.at[place[3]], 0, 8)
-    copy_rows(goal, 6, states.at[place[4]], 0, 8)
-    copy_rows(p0, 8, states.at[place[2]], 0, 8)
 
     def put(below, above):
         (b1, b2), (a1, a2) = below, above
@@ -252,22 +249,40 @@
         copy_rows(q0, 4, b1, 0, 8)
         copy_rows(q0, 20, a1, 0, 8)
         copy_rows(q0, 28, a2, 0, 4)
-        copy_rows(goal, 0, b1, 8, 6)
-        copy_rows(goal, 14, a1, 8, 6)
-        copy_rows(p0, 2, b1, 14, 6)
-        copy_rows(p0, 16, a1, 14, 6)
 
     with_sides(place, (own, own2), (other, other2), put)
+    stages(q0, q1, q2, (qs0, qs1))
+
+    def finish(first, row, values):
+        for field in range(FIELDS):
+            kept = q0[first + (12 + row), field] * (1.0 / 3.0)
+            end[first + (6 + row), field] = kept + (2.0 / 3.0) * values[field]
+
+    forward_rows(q2, qs2, finish)
+
+
+def first_body(
+    place, states, own, other, end, q0, q1, q2, qs0, qs1, qs2, out, edge, next_edge,
+    last, qb2, qb1, lam, p0, p1, p2, pb2, pb1, ps0, ps1, ps2,
+):
+    copy_rows(p0, 8, states.at[place[2]], 0, 8)
+
+    def put(below, above):
+        for row in range(20):
+            for field in range(FIELDS):
+                if row < 6:
+                    goal = below[row, field]
+                elif row < 14:
+                    goal = states[place[4], row - 6, field]
+                else:
+                    goal = above[row - 14, field]
+                last[row, field] = end[row, field] - goal
+        copy_rows(p0, 2, below, 6, 6)
+        copy_rows(p0, 16, above, 6, 6)
+
+    with_sides(place, own, other, put)
     for ref, inner in ((p0, 6), (p1, 4), (p2, 2), (ps0, 4), (ps1, 2), (ps2, 0), (lam, 0), (pb2, 2), (pb1, 4)):
         clear_sides(ref, inner)
-    stages(q0, q1, q2, (qs0, qs1))
-
-    def misfit(first, row, values):
-        for field in range(FIELDS):
-            state = q0[first + (12 + row), field] * (1.0 / 3.0) + (2.0 / 3.0) * values[field]
-            last[first + (6 + row), field] = state - goal[first + (6 + row), field]
-
-    forward_rows(q2, qs2, misfit)
     step_back(last, (q0, q1, q2), (qs0, qs1, qs2), qb2, qb1, (4, 2, 0), store(lam))
     inner = [ref.at[pl.ds(2, ref.shape[0] - 4)] for ref in (p0, p1, p2, ps0, ps1, ps2)]
     stages(*inner[:3], inner[3:5])
@@ -356,20 +371,25 @@
     place, rows = kernel(turn_body, "turn", 1, [(1, *block(8))], place=5)(sched, mine)
     across, place, rows = lax.optimization_barrier((across, place, rows))
     corner = swap(across, 1)
-    states, near, next_near, late = kernel(pack_body, "pack", 4, [(4, *block(8)), block(20), block(6), block(8)])(
-        place, rows, beside, across, corner
+    states, near, next_near, soon, late = kernel(
+        pack_body, "pack", 4, [(4, *block(8)), block(8), block(6), block(12), block(8)]
+    )(place, rows, beside, across, corner)
+    own, own2 = shift(near, 1), shift(next_near, 2)
+    late, own2 = lax.optimization_barrier((late, own2))
+    l_own = shift(late, 1)
+    s_own = shift(soon, 1)
+    other, other2 = swap(own), swap(own2)
+    stage = [block(32), block(28), block(24), block(28, 12), block(24, 12), block(20, 12)]
+    end, *held = kernel(forward_body, "last_forward", 5, [block(20)] + stage, micros=3)(
+        place, states, own, own2, other, other2
     )
-    own, own2 = lax.optimization_barrier((shift(near, 1), shift(next_near, 2)))
-    late, own = lax.optimization_barrier((late, own))
-    l_own = shift(late, 1)
-    other, other2 = swap(own), swap(own2)
+    s_own, end = lax.optimization_barrier((s_own, end))
     share, edge, next_edge = kernel(
-        first_body, "first_steps", 5, [block(20), block(12), block(4)],
-        [block(32), block(28), block(24), block(20), block(20), block(16), block(12)]
-        + [block(28, 12), block(24, 12), block(20, 12)]
+        first_body, "first_steps", 10, [block(20), block(12), block(4)],
+        [block(20), block(16), block(12)]
         + [block(20), block(24), block(20), block(16), block(20), block(24)]
-        + [block(20, 12), block(16, 12), block(12, 12)], micros=7,
-    )(place, states, own, own2, other, other2)
+        + [block(20, 12), block(16, 12), block(12, 12)], micros=5,
+    )(place, states, s_own, swap(s_own), end, *held)
     a_own, a_own2 = shift(edge, 1), shift(next_edge, 2)
     l_own, after = lax.optimization_barrier((l_own, next_edge))
     l_other = swap(l_own)

time: 47.9 us -> 44.9 us (0.937)
  Pallas kernels: 16.5 us -> 13.9 us
  waiting for transfers between devices: 14.6 us -> 13.8 us
    pallas_call x2 -> x3, Pallas kernels: 9.44 us -> 7.9 us  [the longest x1 4.5 us: body(): kernel(first_body, 'first_steps', 10, [block(20), block(12), block(4)], [...]
    ppermute x5 -> x6, waiting for transfers between devices: 9.5 us -> 8.02 us  [shift(): return lax.ppermute(array, ('section', 'tile'), pairs)]
    pallas_call x1, Pallas kernels: 2.96 us -> 2.11 us  [body(): kernel(ahead_body, 'ahead', 6, stage, micros=2)]
    ppermute x8 -> x9, waiting for transfers between devices: 5.08 us -> 5.82 us  [swap(): lax.ppermute(array, 'section', [(s, s ^ mask) for s in range(sections)])]
    ppermute x5 -> x6, starting transfers between devices: 11.1 us -> 11.8 us  [shift(): return lax.ppermute(array, ('section', 'tile'), pairs)]
    ppermute x8 -> x9, starting transfers between devices: 3.97 us -> 3.46 us  [swap(): lax.ppermute(array, 'section', [(s, s ^ mask) for s in range(sections)])]
  transfers between devices with their start and end apart: 13 -> 15, of which waited for: 8 -> 10; matrix products, arithmetic and copies ran while one was open for 0% -> 0% of each run, Pallas kernels for 27% -> 23%
where the time goes in v2:
time: 44.9 us; the launch traced here: 44.7 us
  starting transfers between devices  15.3 us (34%)
  Pallas kernels  13.9 us (31%)
  waiting for transfers between devices  13.8 us (31%)
  local copies, waits for them, and re-layouts  1.6 us (4%)
    ppermute x6, starting transfers between devices, shift(): return lax.ppermute(array, ('section', 'tile'), pairs)  11.8 us
    ppermute x6, waiting for transfers between devices, shift(): return lax.ppermute(array, ('section', 'tile'), pairs)  8.02 us
    ppermute x9, waiting for transfers between devices, swap(): lax.ppermute(array, 'section', [(s, s ^ mask) for s in range(sections)])  5.82 us
    pallas_call x1, Pallas kernels, body(): kernel(first_body, 'first_steps', 10, [block(20), block(12), block(4)], [...  4.5 us
    ppermute x9, starting transfers between devices, swap(): lax.ppermute(array, 'section', [(s, s ^ mask) for s in range(sections)])  3.46 us
    pallas_call x1, Pallas kernels, body(): kernel(last_body, 'last_step', 11, [(FIELDS, NZ * 8, NY)], [block(20), bl...  2.76 us
    pallas_call x1, Pallas kernels, body(): kernel(forward_body, 'last_forward', 5, [block(20)] + stage, micros=3)  2.71 us
    pallas_call x1, Pallas kernels, body(): kernel(ahead_body, 'ahead', 6, stage, micros=2)  2.11 us
  transfers between devices with their start and end apart: 15, of which 10 were waited for; matrix products, arithmetic and copies ran while one was open for 0% of the time, Pallas kernels for 23%

profile of v2, /device:TPU:0, one launch (start us, length us, event | category | flops | bytes accessed | tf_op | source)
XLA Modules:
  0.0 44.7 jit_solution(6115693971817078597)
XLA Ops:
  0.0 2.9 %collective-permute-start = (f32[5,64,128]{2,1,0:T(8,128)}, f32[5,64,128]{2,1,0:T(8,128)S(1)}, u32[]{:S(2)}, u32[]{:S(2)}) collective-permute-start(f32[5,64,128]{2,1,0:T(8,128)} %bitcast.2), channel_id=1, source_target_pairs={{0,16},{8,24},{16,0},{24,8},{1,17},{9,25},{17,1},{25,9},{2,18},{10... | collective-permute-start | bytes 491528 | tf_op jit(solution)/shard_map/ppermute | solution.py:366
  2.9 0.0 collective-permute-start.1
  2.9 0.9 %copy-done = f32[1,5,8,8,128]{4,3,2,1,0:T(8,128)S(1)} copy-done((f32[1,5,8,8,128]{4,3,2,1,0:T(8,128)S(1)}, f32[1,5,8,8,128]{4,3,2,1,0:T(8,128)}, u32[]{:S(2)}) %copy-start) | copy-done | bytes 163864
  3.9 0.7 %copy-done.1 = s32[4]{0:T(128)S(1)} copy-done((s32[4]{0:T(128)S(1)}, s32[4]{0:T(128)}, u32[]{:S(2)}) %copy-start.1) | copy-done | bytes 40
  4.5 1.2 %turn.1 = (s32[5]{0:T(128)S(1)}, f32[1,8,5,8,128]{4,3,2,1,0:T(8,128)S(1)}) custom-call(s32[4]{0:T(128)S(1)} %copy-done.1, f32[5,64,128]{2,1,0:T(8,128)S(1)} %bitcast.4), custom_call_target="tpu_custom_call" | custom-call | flops 4000000 | bytes 3000000 | tf_op jit(solution)/shard_map/turn/pallas_call | solution.py:371
  5.7 1.6 %collective-permute-done.across = f32[5,64,128]{2,1,0:T(8,128)S(1)} collective-permute-done((f32[5,64,128]{2,1,0:T(8,128)}, f32[5,64,128]{2,1,0:T(8,128)S(1)}, u32[]{:S(2)}, u32[]{:S(2)}) %collective-permute-start) | collective-permute-done | bytes 163872 | tf_op jit(solution)/shard_map/ppermute | solution.py:366
  7.3 0.0 collective-permute-start.2
  7.3 0.0 collective-permute-done.1.beside
  7.4 1.4 %collective-permute-done.2.corner = f32[5,64,128]{2,1,0:T(8,128)S(1)} collective-permute-done((f32[5,64,128]{2,1,0:T(8,128)S(1)}, f32[5,64,128]{2,1,0:T(8,128)S(1)}, u32[]{:S(2)}, u32[]{:S(2)}) %collective-permute-start.2) | collective-permute-done | bytes 163872 | tf_op jit(solution)/shard_map/ppermute | solution.py:366
  8.7 0.7 %pack.1 = (f32[4,8,5,8,128]{4,3,2,1,0:T(8,128)S(1)}, f32[8,5,8,128]{3,2,1,0:T(8,128)S(1)}, f32[6,5,8,128]{3,2,1,0:T(8,128)S(1)}, f32[12,5,8,128]{3,2,1,0:T(8,128)S(1)}, f32[8,5,8,128]{3,2,1,0:T(8,128)S(1)}) custom-call(s32[5]{0:T(128)S(1)} %get-tuple-element.47.place, f32[1,8,5,8,128]{4,3,2,1,0:T(8,128)S(1)} %get-tuple-element.48.rows, ...), custom_call_target="tpu_custom_call" | custom-call | flops 4000000 | bytes 3000000 | tf_op jit(solution)/shard_map/pack/pallas_call | solution.py:374
  9.4 4.9 %collective-permute-start.4 = (f32[8,5,8,128]{3,2,1,0:T(8,128)S(1)}, f32[8,5,8,128]{3,2,1,0:T(8,128)S(1)}, u32[]{:S(2)}, u32[]{:S(2)}) collective-permute-start(f32[8,5,8,128]{3,2,1,0:T(8,128)S(1)} %get-tuple-element.52), channel_id=1, source_target_pairs={{0,7},{1,0},{2,1},{3,2},{4,3},{5,4},{6,5},{7,6},{8,9},{9,10},{10,1... | collective-permute-start | bytes 491528 | tf_op jit(solution)/shard_map/ppermute | solution.py:363
  14.3 0.4 %collective-permute-start.5 = (f32[6,5,8,128]{3,2,1,0:T(8,128)S(1)}, f32[6,5,8,128]{3,2,1,0:T(8,128)S(1)}, u32[]{:S(2)}, u32[]{:S(2)}) collective-permute-start(f32[6,5,8,128]{3,2,1,0:T(8,128)S(1)} %get-tuple-element.54), channel_id=1, source_target_pairs={{0,6},{1,7},{2,0},{3,1},{4,2},{5,3},{6,4},{7,5},{8,10},{9,11},{10,... | collective-permute-start | bytes 368648 | tf_op jit(solution)/shard_map/ppermute | solution.py:363
  14.8 0.5 %collective-permute-start.3 = (f32[12,5,8,128]{3,2,1,0:T(8,128)S(1)}, f32[12,5,8,128]{3,2,1,0:T(8,128)S(1)}, u32[]{:S(2)}, u32[]{:S(2)}) collective-permute-start(f32[12,5,8,128]{3,2,1,0:T(8,128)S(1)} %get-tuple-element.51), channel_id=1, source_target_pairs={{0,7},{1,0},{2,1},{3,2},{4,3},{5,4},{6,5},{7,6},{8,9},{9,10},{10,1... | collective-permute-start | bytes 737288 | tf_op jit(solution)/shard_map/ppermute | solution.py:363
  15.3 1.9 %collective-permute-done.4.own = f32[8,5,8,128]{3,2,1,0:T(8,128)S(1)} collective-permute-done((f32[8,5,8,128]{3,2,1,0:T(8,128)S(1)}, f32[8,5,8,128]{3,2,1,0:T(8,128)S(1)}, u32[]{:S(2)}, u32[]{:S(2)}) %collective-permute-start.4) | collective-permute-done | bytes 163872 | tf_op jit(solution)/shard_map/ppermute | solution.py:363
  17.1 0.0 collective-permute-start.6
  17.1 2.0 %collective-permute-done.5.own2 = f32[6,5,8,128]{3,2,1,0:T(8,128)S(1)} collective-permute-done((f32[6,5,8,128]{3,2,1,0:T(8,128)S(1)}, f32[6,5,8,128]{3,2,1,0:T(8,128)S(1)}, u32[]{:S(2)}, u32[]{:S(2)}) %collective-permute-start.5) | collective-permute-done | bytes 122912 | tf_op jit(solution)/shard_map/ppermute | solution.py:363
  19.2 1.3 %collective-permute-done.7.other2 = f32[6,5,8,128]{3,2,1,0:T(8,128)S(1)} collective-permute-done((f32[6,5,8,128]{3,2,1,0:T(8,128)S(1)}, f32[6,5,8,128]{3,2,1,0:T(8,128)S(1)}, u32[]{:S(2)}, u32[]{:S(2)}) %collective-permute-start.7) | collective-permute-done | bytes 122912 | tf_op jit(solution)/shard_map/ppermute | solution.py:366
  20.5 2.7 %last_forward.1 = (f32[20,5,8,128]{3,2,1,0:T(8,128)S(1)}, f32[32,5,8,128]{3,2,1,0:T(8,128)S(1)}, f32[28,5,8,128]{3,2,1,0:T(8,128)S(1)}, f32[24,5,8,128]{3,2,1,0:...) custom-call(s32[5]{0:T(128)S(1)} %get-tuple-element.47.place, ...), custom_call_target="tpu_custom_call" | custom-call | flops 12000000 | bytes 9000000 | tf_op jit(solution)/shard_map/last_forward/pallas_call | solution.py:383
  23.2 0.3 collective-permute-done.3.own
  23.6 3.6 %collective-permute-start.11 = (f32[8,5,8,128]{3,2,1,0:T(8,128)S(1)}, f32[8,5,8,128]{3,2,1,0:T(8,128)S(1)}, u32[]{:S(2)}, u32[]{:S(2)}) collective-permute-start(f32[8,5,8,128]{3,2,1,0:T(8,128)S(1)} %get-tuple-element.68), channel_id=1, source_target_pairs={{0,7},{1,0},{2,1},{3,2},{4,3},{5,4},{6,5},{7,6},{8,9},{9,10},{10,1... | collective-permute-start | bytes 491528 | tf_op jit(solution)/shard_map/ppermute | solution.py:363
  27.2 0.0 collective-permute-done.8.other
  27.2 4.5 %first_steps.1 = (f32[20,5,8,128]{3,2,1,0:T(8,128)S(1)}, f32[12,5,8,128]{3,2,1,0:T(8,128)S(1)}, f32[4,5,8,128]{3,2,1,0:T(8,128)S(1)}) custom-call(s32[5]{0:T(128)S(1)} %get-tuple-element.47.place, f32[4,8,5,8,128]{4,3,2,1,0:T(8,128)S(1)} %get-tuple-element.50.states, f32[12,5,8,128]{3,2,1,0:T(8,128)S(1)} %collective-permute-done.3.own, ...), custom_call_target="tpu_custom_call" | custom-call | flops 20000000 | bytes 15000000 | tf_op jit(solution)/shard_map/first_steps/pallas_call | solution.py:387
  31.7 1.4 %collective-permute-start.9 = (f32[12,5,8,128]{3,2,1,0:T(8,128)S(1)}, f32[12,5,8,128]{3,2,1,0:T(8,128)S(1)}, u32[]{:S(2)}, u32[]{:S(2)}) collective-permute-start(f32[12,5,8,128]{3,2,1,0:T(8,128)S(1)} %get-tuple-element.66), channel_id=1, source_target_pairs={{0,7},{1,0},{2,1},{3,2},{4,3},{5,4},{6,5},{7,6},{8,9},{9,10},{10,1... | collective-permute-start | bytes 737288 | tf_op jit(solution)/shard_map/ppermute | solution.py:363
  33.1 0.0 collective-permute-done.11.own
  33.1 1.0 %collective-permute-start.10 = (f32[4,5,8,128]{3,2,1,0:T(8,128)S(1)}, f32[4,5,8,128]{3,2,1,0:T(8,128)S(1)}, u32[]{:S(2)}, u32[]{:S(2)}) collective-permute-start(f32[4,5,8,128]{3,2,1,0:T(8,128)S(1)} %get-tuple-element.70.after), channel_id=1, source_target_pairs={{0,6},{1,7},{2,0},{3,1},{4,2},{5,3},{6,4},{7,5},{8,10},{9,11},{10,... | collective-permute-start | bytes 245768 | tf_op jit(solution)/shard_map/ppermute | solution.py:363
  34.1 0.3 collective-permute-done.12.other
  34.5 2.1 %ahead.1 = (f32[28,5,8,128]{3,2,1,0:T(8,128)S(1)}, f32[24,5,8,128]{3,2,1,0:T(8,128)S(1)}, f32[20,5,8,128]{3,2,1,0:T(8,128)S(1)}, f32[24,12,8,128]{3,2,1,0:T(8,12...) custom-call(s32[5]{0:T(128)S(1)} %get-tuple-element.47.place, ...), custom_call_target="tpu_custom_call" | custom-call | flops 8000000 | bytes 6000000 | tf_op jit(solution)/shard_map/ahead/pallas_call | solution.py:397
  36.6 1.8 %collective-permute-done.10.own2 = f32[4,5,8,128]{3,2,1,0:T(8,128)S(1)} collective-permute-done((f32[4,5,8,128]{3,2,1,0:T(8,128)S(1)}, f32[4,5,8,128]{3,2,1,0:T(8,128)S(1)}, u32[]{:S(2)}, u32[]{:S(2)}) %collective-permute-start.10) | collective-permute-done | bytes 81952 | tf_op jit(solution)/shard_map/ppermute | solution.py:363
  38.4 2.0 %collective-permute-done.9.own = f32[12,5,8,128]{3,2,1,0:T(8,128)S(1)} collective-permute-done((f32[12,5,8,128]{3,2,1,0:T(8,128)S(1)}, f32[12,5,8,128]{3,2,1,0:T(8,128)S(1)}, u32[]{:S(2)}, u32[]{:S(2)}) %collective-permute-start.9) | collective-permute-done | bytes 245792 | tf_op jit(solution)/shard_map/ppermute | solution.py:363
  40.4 0.5 %collective-permute-start.14 = (f32[4,5,8,128]{3,2,1,0:T(8,128)S(1)}, f32[4,5,8,128]{3,2,1,0:T(8,128)S(1)}, u32[]{:S(2)}, u32[]{:S(2)}) collective-permute-start(f32[4,5,8,128]{3,2,1,0:T(8,128)S(1)} %collective-permute-done.10.own2), channel_id=1, source_target_pairs={{0,8},{8,0},{16,24},{24,16},{1,9},{9,1},{17,25},{25,17},{2,10},{10... | collective-permute-start | bytes 245768 | tf_op jit(solution)/shard_map/ppermute | solution.py:366
  40.9 1.1 %collective-permute-done.14.other2 = f32[4,5,8,128]{3,2,1,0:T(8,128)S(1)} collective-permute-done((f32[4,5,8,128]{3,2,1,0:T(8,128)S(1)}, f32[4,5,8,128]{3,2,1,0:T(8,128)S(1)}, u32[]{:S(2)}, u32[]{:S(2)}) %collective-permute-start.14) | collective-permute-done | bytes 81952 | tf_op jit(solution)/shard_map/ppermute | solution.py:366
  42.0 2.8 %last_step.1 = f32[5,64,128]{2,1,0:T(8,128)} custom-call(s32[5]{0:T(128)S(1)} %get-tuple-element.47.place, f32[20,5,8,128]{3,2,1,0:T(8,128)S(1)} %get-tuple-element.65.share, f32[12,5,8,128]{3,2,1,0:T(8,128)S(1)} %collective-permute-done.9.own, f32[4,5,8,128]{3,2,1,0:T(8,128)S(1)} %collective-permute-done.10.own2, ...), custom_call_target="tpu_custom_call" | custom-call | flops 8000000 | bytes 6000000 | tf_op jit(solution)/shard_map/last_step/pallas_call | solution.py:400
  (8 shorter events, 0.0 us)
Async XLA Ops:
  0.0 7.3 %collective-permute-start = (f32[5,64,128]{2,1,0:T(8,128)}, f32[5,64,128]{2,1,0:T(8,128)S(1)}, u32[]{:S(2)}, u32[]{:S(2)}) collective-permute-start(f32[5,64,128]{2,1,0:T(8,128)} %bitcast.2), channel_id=1, source_target_pairs={{0,16},{8,24},{16,0},{24,8},{1,17},{9,25},{17,1},{25,9},{2,18},{10... | collective-permute-start | bytes 491528 | tf_op jit(solution)/shard_map/ppermute | solution.py:366
  2.9 4.4 %collective-permute-start.1 = (f32[5,64,128]{2,1,0:T(8,128)}, f32[5,64,128]{2,1,0:T(8,128)S(1)}, u32[]{:S(2)}, u32[]{:S(2)}) collective-permute-start(f32[5,64,128]{2,1,0:T(8,128)} %bitcast.3), channel_id=1, source_target_pairs={{0,8},{8,0},{16,24},{24,16},{1,9},{9,1},{17,25},{25,17},{2,10},{10... | collective-permute-start | bytes 491528 | tf_op jit(solution)/shard_map/ppermute | solution.py:366
  2.9 0.9 %copy-start = (f32[1,5,8,8,128]{4,3,2,1,0:T(8,128)S(1)}, f32[1,5,8,8,128]{4,3,2,1,0:T(8,128)}, u32[]{:S(2)}) copy-start(f32[1,5,8,8,128]{4,3,2,1,0:T(8,128)} %param.2) | copy-start | bytes 491524
  3.9 0.7 %copy-start.1 = (s32[4]{0:T(128)S(1)}, s32[4]{0:T(128)}, u32[]{:S(2)}) copy-start(s32[4]{0:T(128)} %sched.1) | copy-start | bytes 52
  7.3 1.4 %collective-permute-start.2 = (f32[5,64,128]{2,1,0:T(8,128)S(1)}, f32[5,64,128]{2,1,0:T(8,128)S(1)}, u32[]{:S(2)}, u32[]{:S(2)}) collective-permute-start(f32[5,64,128]{2,1,0:T(8,128)S(1)} %collective-permute-done.across), channel_id=1, source_target_pairs={{0,8},{8,0},{16,24},{24,16},{1,9},{9,1},{17,25},{25,17},{2,10},{10... | collective-permute-start | bytes 491528 | tf_op jit(solution)/shard_map/ppermute | solution.py:366
  9.4 7.7 %collective-permute-start.4 = (f32[8,5,8,128]{3,2,1,0:T(8,128)S(1)}, f32[8,5,8,128]{3,2,1,0:T(8,128)S(1)}, u32[]{:S(2)}, u32[]{:S(2)}) collective-permute-start(f32[8,5,8,128]{3,2,1,0:T(8,128)S(1)} %get-tuple-element.52), channel_id=1, source_target_pairs={{0,7},{1,0},{2,1},{3,2},{4,3},{5,4},{6,5},{7,6},{8,9},{9,10},{10,1... | collective-permute-start | bytes 491528 | tf_op jit(solution)/shard_map/ppermute | solution.py:363
  14.3 4.9 %collective-permute-start.5 = (f32[6,5,8,128]{3,2,1,0:T(8,128)S(1)}, f32[6,5,8,128]{3,2,1,0:T(8,128)S(1)}, u32[]{:S(2)}, u32[]{:S(2)}) collective-permute-start(f32[6,5,8,128]{3,2,1,0:T(8,128)S(1)} %get-tuple-element.54), channel_id=1, source_target_pairs={{0,6},{1,7},{2,0},{3,1},{4,2},{5,3},{6,4},{7,5},{8,10},{9,11},{10,... | collective-permute-start | bytes 368648 | tf_op jit(solution)/shard_map/ppermute | solution.py:363
  14.8 8.8 %collective-permute-start.3 = (f32[12,5,8,128]{3,2,1,0:T(8,128)S(1)}, f32[12,5,8,128]{3,2,1,0:T(8,128)S(1)}, u32[]{:S(2)}, u32[]{:S(2)}) collective-permute-start(f32[12,5,8,128]{3,2,1,0:T(8,128)S(1)} %get-tuple-element.51), channel_id=1, source_target_pairs={{0,7},{1,0},{2,1},{3,2},{4,3},{5,4},{6,5},{7,6},{8,9},{9,10},{10,1... | collective-permute-start | bytes 737288 | tf_op jit(solution)/shard_map/ppermute | solution.py:363
  17.1 3.4 %collective-permute-start.6 = (f32[8,5,8,128]{3,2,1,0:T(8,128)S(1)}, f32[8,5,8,128]{3,2,1,0:T(8,128)S(1)}, u32[]{:S(2)}, u32[]{:S(2)}) collective-permute-start(f32[8,5,8,128]{3,2,1,0:T(8,128)S(1)} %collective-permute-done.4.own), channel_id=1, source_target_pairs={{0,8},{8,0},{16,24},{24,16},{1,9},{9,1},{17,25},{25,17},{2,10},{10... | collective-permute-start | bytes 491528 | tf_op jit(solution)/shard_map/ppermute | solution.py:366
  19.2 1.3 %collective-permute-start.7 = (f32[6,5,8,128]{3,2,1,0:T(8,128)S(1)}, f32[6,5,8,128]{3,2,1,0:T(8,128)S(1)}, u32[]{:S(2)}, u32[]{:S(2)}) collective-permute-start(f32[6,5,8,128]{3,2,1,0:T(8,128)S(1)} %collective-permute-done.5.own2), channel_id=1, source_target_pairs={{0,8},{8,0},{16,24},{24,16},{1,9},{9,1},{17,25},{25,17},{2,10},{10... | collective-permute-start | bytes 368648 | tf_op jit(solution)/shard_map/ppermute | solution.py:366
  23.6 3.6 %collective-permute-start.8 = (f32[12,5,8,128]{3,2,1,0:T(8,128)S(1)}, f32[12,5,8,128]{3,2,1,0:T(8,128)S(1)}, u32[]{:S(2)}, u32[]{:S(2)}) collective-permute-start(f32[12,5,8,128]{3,2,1,0:T(8,128)S(1)} %collective-permute-done.3.own), channel_id=1, source_target_pairs={{0,8},{8,0},{16,24},{24,16},{1,9},{9,1},{17,25},{25,17},{2,10},{10... | collective-permute-start | bytes 737288 | tf_op jit(solution)/shard_map/ppermute | solution.py:366
  23.6 9.5 %collective-permute-start.11 = (f32[8,5,8,128]{3,2,1,0:T(8,128)S(1)}, f32[8,5,8,128]{3,2,1,0:T(8,128)S(1)}, u32[]{:S(2)}, u32[]{:S(2)}) collective-permute-start(f32[8,5,8,128]{3,2,1,0:T(8,128)S(1)} %get-tuple-element.68), channel_id=1, source_target_pairs={{0,7},{1,0},{2,1},{3,2},{4,3},{5,4},{6,5},{7,6},{8,9},{9,10},{10,1... | collective-permute-start | bytes 491528 | tf_op jit(solution)/shard_map/ppermute | solution.py:363
  31.7 8.7 %collective-permute-start.9 = (f32[12,5,8,128]{3,2,1,0:T(8,128)S(1)}, f32[12,5,8,128]{3,2,1,0:T(8,128)S(1)}, u32[]{:S(2)}, u32[]{:S(2)}) collective-permute-start(f32[12,5,8,128]{3,2,1,0:T(8,128)S(1)} %get-tuple-element.66), channel_id=1, source_target_pairs={{0,7},{1,0},{2,1},{3,2},{4,3},{5,4},{6,5},{7,6},{8,9},{9,10},{10,1... | collective-permute-start | bytes 737288 | tf_op jit(solution)/shard_map/ppermute | solution.py:363
  33.1 1.4 %collective-permute-start.12 = (f32[8,5,8,128]{3,2,1,0:T(8,128)S(1)}, f32[8,5,8,128]{3,2,1,0:T(8,128)S(1)}, u32[]{:S(2)}, u32[]{:S(2)}) collective-permute-start(f32[8,5,8,128]{3,2,1,0:T(8,128)S(1)} %collective-permute-done.11.own), channel_id=1, source_target_pairs={{0,8},{8,0},{16,24},{24,16},{1,9},{9,1},{17,25},{25,17},{2,10},{10... | collective-permute-start | bytes 491528 | tf_op jit(solution)/shard_map/ppermute | solution.py:366
  33.1 5.3 %collective-permute-start.10 = (f32[4,5,8,128]{3,2,1,0:T(8,128)S(1)}, f32[4,5,8,128]{3,2,1,0:T(8,128)S(1)}, u32[]{:S(2)}, u32[]{:S(2)}) collective-permute-start(f32[4,5,8,128]{3,2,1,0:T(8,128)S(1)} %get-tuple-element.70.after), channel_id=1, source_target_pairs={{0,6},{1,7},{2,0},{3,1},{4,2},{5,3},{6,4},{7,5},{8,10},{9,11},{10,... | collective-permute-start | bytes 245768 | tf_op jit(solution)/shard_map/ppermute | solution.py:363
  40.3 1.6 %collective-permute-start.13 = (f32[12,5,8,128]{3,2,1,0:T(8,128)S(1)}, f32[12,5,8,128]{3,2,1,0:T(8,128)S(1)}, u32[]{:S(2)}, u32[]{:S(2)}) collective-permute-start(f32[12,5,8,128]{3,2,1,0:T(8,128)S(1)} %collective-permute-done.9.own), channel_id=1, source_target_pairs={{0,8},{8,0},{16,24},{24,16},{1,9},{9,1},{17,25},{25,17},{2,10},{10... | collective-permute-start | bytes 737288 | tf_op jit(solution)/shard_map/ppermute | solution.py:366
  40.4 1.6 %collective-permute-start.14 = (f32[4,5,8,128]{3,2,1,0:T(8,128)S(1)}, f32[4,5,8,128]{3,2,1,0:T(8,128)S(1)}, u32[]{:S(2)}, u32[]{:S(2)}) collective-permute-start(f32[4,5,8,128]{3,2,1,0:T(8,128)S(1)} %collective-permute-done.10.own2), channel_id=1, source_target_pairs={{0,8},{8,0},{16,24},{24,16},{1,9},{9,1},{17,25},{25,17},{2,10},{10... | collective-permute-start | bytes 245768 | tf_op jit(solution)/shard_map/ppermute | solution.py:366

commit v3 on v2

--- a/solution.py
+++ b/solution.py
@@ -202,26 +202,33 @@
             dst[at + k, field] = src[begin + k, field]
 
 
-def turn(states, mask, source):
+def core_index():
+    return lax.axis_index("section") & 1
+
+
+def turn_body(sched, saved, groups, rows):
+    section = lax.axis_index("section")
+    for mask in range(4):
+        groups[mask] = jnp.full((NZ, NY), sched[section ^ mask], jnp.int32)
     for row in range(8):
         for field in range(FIELDS):
-            states[mask, row, field] = source[field, pl.ds(row, NZ, stride=8), :]
-
-
-def turn_body(sched, saved, place, rows):
-    section = lax.axis_index("section")
-    place[0] = section & 1
-    for mask in range(4):
-        place[1 + sched[section ^ mask]] = mask
-    turn(rows, 0, saved)
-
-
-def pack_body(place, rows, beside, across, corner, states, near, next_near, soon, late):
-    copy_rows(states.at[0], 0, rows.at[0], 0, 8)
-    for mask, source in ((1, beside), (2, across), (3, corner)):
-        turn(states, mask, source)
-    core = place[0]
-    last, goal, middle, start = (states.at[place[1 + group]] for group in (2, 3, 1, 0))
+            rows[row, field] = saved[field, pl.ds(row, NZ, stride=8), :]
+
+
+def pack_body(groups, rows, beside, across, corner, states, near, next_near, soon, late):
+    held = [groups[mask] for mask in range(4)]
+    is_group = [[held[mask] == group for mask in range(4)] for group in range(4)]
+    for row in range(8):
+        for field in range(FIELDS):
+            found = [rows[row, field]]
+            found += [source[field, pl.ds(row, NZ, stride=8), :] for source in (beside, across, corner)]
+            for group in range(4):
+                value = found[0]
+                for mask in range(1, 4):
+                    value = jnp.where(is_group[group][mask], found[mask], value)
+                states[group, row, field] = value
+    core = core_index()
+    start, middle, last, goal = (states.at[group] for group in range(4))
     copy_rows(near, 0, last, 0, 8)
     copy_rows(next_near, 0, last, 4 * core, 4)
     copy_rows(next_near, 4, start, 6 * core, 2)
@@ -230,18 +237,18 @@
     copy_rows(late, 0, start, 0, 8)
 
 
-def with_sides(place, own, other, put):
-    @pl.when(place[0] == 0)
+def with_sides(own, other, put):
+    @pl.when(core_index() == 0)
     def _():
         put(other, own)
 
-    @pl.when(place[0] != 0)
+    @pl.when(core_index() != 0)
     def _():
         put(own, other)
 
 
-def forward_body(place, states, own, own2, other, other2, end, q0, q1, q2, qs0, qs1, qs2):
-    copy_rows(q0, 12, states.at[place[3]], 0, 8)
+def forward_body(states, own, own2, other, other2, end, q0, q1, q2, qs0, qs1, qs2):
+    copy_rows(q0, 12, states.at[2], 0, 8)
 
     def put(below, above):
         (b1, b2), (a1, a2) = below, above
@@ -250,7 +257,7 @@
         copy_rows(q0, 20, a1, 0, 8)
         copy_rows(q0, 28, a2, 0, 4)
 
-    with_sides(place, (own, own2), (other, other2), put)
+    with_sides((own, own2), (other, other2), put)
     stages(q0, q1, q2, (qs0, qs1))
 
     def finish(first, row, values):
@@ -262,10 +269,10 @@
 
 
 def first_body(
-    place, states, own, other, end, q0, q1, q2, qs0, qs1, qs2, out, edge, next_edge,
+    states, own, other, end, q0, q1, q2, qs0, qs1, qs2, out, edge, next_edge,
     last, qb2, qb1, lam, p0, p1, p2, pb2, pb1, ps0, ps1, ps2,
 ):
-    copy_rows(p0, 8, states.at[place[2]], 0, 8)
+    copy_rows(p0, 8, states.at[1], 0, 8)
 
     def put(below, above):
         for row in range(20):
@@ -273,14 +280,14 @@
                 if row < 6:
                     goal = below[row, field]
                 elif row < 14:
-                    goal = states[place[4], row - 6, field]
+                    goal = states[3, row - 6, field]
                 else:
                     goal = above[row - 14, field]
                 last[row, field] = end[row, field] - goal
         copy_rows(p0, 2, below, 6, 6)
         copy_rows(p0, 16, above, 6, 6)
 
-    with_sides(place, own, other, put)
+    with_sides(own, other, put)
     for ref, inner in ((p0, 6), (p1, 4), (p2, 2), (ps0, 4), (ps1, 2), (ps2, 0), (lam, 0), (pb2, 2), (pb1, 4)):
         clear_sides(ref, inner)
     step_back(last, (q0, q1, q2), (qs0, qs1, qs2), qb2, qb1, (4, 2, 0), store(lam))
@@ -288,12 +295,12 @@
     stages(*inner[:3], inner[3:5])
     forward_rows(inner[2], inner[5], None)
     step_back(lam, (p0, p1, p2), (ps0, ps1, ps2), pb2, pb1, (2, 4, 6), store(out))
-    copy_rows(edge, 0, out, 8 * place[0], 12)
-    copy_rows(next_edge, 0, out, 16 * place[0], 4)
-
-
-def ahead_body(place, states, own, own2, other, other2, after, x0, x1, x2, xs0, xs1, xs2):
-    copy_rows(x0, 10, states.at[place[1]], 0, 8)
+    copy_rows(edge, 0, out, 8 * core_index(), 12)
+    copy_rows(next_edge, 0, out, 16 * core_index(), 4)
+
+
+def ahead_body(states, own, own2, other, other2, after, x0, x1, x2, xs0, xs1, xs2):
+    copy_rows(x0, 10, states.at[0], 0, 8)
 
     def put(below, above):
         (b1, b2), (a1, a2) = below, above
@@ -302,12 +309,12 @@
         copy_rows(x0, 18, a1, 0, 8)
         copy_rows(x0, 26, a2, 4, 2)
 
-    with_sides(place, (own, own2), (other, other2), put)
+    with_sides((own, own2), (other, other2), put)
     stages(x0, x1, x2, (xs0, xs1))
     forward_rows(x2, xs2, None)
 
 
-def last_body(place, share, own, own2, other, other2, x0, x1, x2, xs0, xs1, xs2, out, lam, back2, back1):
+def last_body(share, own, own2, other, other2, x0, x1, x2, xs0, xs1, xs2, out, lam, back2, back1):
     def put(below, above):
         (b1, b2), (a1, a2) = below, above
         for row in range(20):
@@ -323,7 +330,7 @@
                     value = value + a2[row - 16, field]
                 lam[row, field] = value
 
-    with_sides(place, (own, own2), (other, other2), put)
+    with_sides((own, own2), (other, other2), put)
 
     def finish(first, row, values):
         for field in range(FIELDS):
@@ -336,14 +343,13 @@
     return (count, planes, NZ, NY)
 
 
-def kernel(body, name, arrays, outs, scratch=(), place=0, micros=1, megabytes=16):
-    smem, vmem = pl.BlockSpec(memory_space=pltpu.SMEM), pl.BlockSpec(memory_space=pltpu.VMEM)
-    shapes = [jax.ShapeDtypeStruct(shape, jnp.float32) for shape in outs]
+def kernel(body, name, arrays, outs, scratch=(), micros=1, megabytes=16):
+    vmem = pl.BlockSpec(memory_space=pltpu.VMEM)
     return pl.pallas_call(
         body,
-        out_shape=[jax.ShapeDtypeStruct((place,), jnp.int32)] * bool(place) + shapes,
-        in_specs=[smem] + [vmem] * arrays,
-        out_specs=[smem] * bool(place) + [vmem] * len(outs),
+        out_shape=[jax.ShapeDtypeStruct(shape, jnp.float32) for shape in outs],
+        in_specs=[vmem] * arrays,
+        out_specs=[vmem] * len(outs),
         scratch_shapes=[pltpu.VMEM(shape, jnp.float32) for shape in scratch],
         compiler_params=pltpu.CompilerParams(vmem_limit_bytes=megabytes * 1024 * 1024),
         cost_estimate=pl.CostEstimate(flops=micros * 4_000_000, bytes_accessed=micros * 3_000_000, transcendentals=0),
@@ -368,12 +374,20 @@
     mine = saved.reshape(FIELDS, NZ * 8, NY)
     across = swap(mine, 2)
     beside = swap(mine, 1)
-    place, rows = kernel(turn_body, "turn", 1, [(1, *block(8))], place=5)(sched, mine)
-    across, place, rows = lax.optimization_barrier((across, place, rows))
+    smem, vmem = pl.BlockSpec(memory_space=pltpu.SMEM), pl.BlockSpec(memory_space=pltpu.VMEM)
+    groups, rows = pl.pallas_call(
+        turn_body,
+        out_shape=[jax.ShapeDtypeStruct((4, NZ, NY), jnp.int32), jax.ShapeDtypeStruct(block(8), jnp.float32)],
+        in_specs=[smem, vmem],
+        out_specs=[vmem, vmem],
+        compiler_params=pltpu.CompilerParams(vmem_limit_bytes=4 * 1024 * 1024),
+        name="turn",
+    )(sched, mine)
+    across, groups, rows = lax.optimization_barrier((across, groups, rows))
     corner = swap(across, 1)
     states, near, next_near, soon, late = kernel(
-        pack_body, "pack", 4, [(4, *block(8)), block(8), block(6), block(12), block(8)]
-    )(place, rows, beside, across, corner)
+        pack_body, "pack", 5, [(4, *block(8)), block(8), block(6), block(12), block(8)]
+    )(groups, rows, beside, across, corner)
     own, own2 = shift(near, 1), shift(next_near, 2)
     late, own2 = lax.optimization_barrier((late, own2))
     l_own = shift(late, 1)
@@ -381,7 +395,7 @@
     other, other2 = swap(own), swap(own2)
     stage = [block(32), block(28), block(24), block(28, 12), block(24, 12), block(20, 12)]
     end, *held = kernel(forward_body, "last_forward", 5, [block(20)] + stage, micros=3)(
-        place, states, own, own2, other, other2
+        states, own, own2, other, other2
     )
     s_own, end = lax.optimization_barrier((s_own, end))
     share, edge, next_edge = kernel(
@@ -389,17 +403,17 @@
         [block(20), block(16), block(12)]
         + [block(20), block(24), block(20), block(16), block(20), block(24)]
         + [block(20, 12), block(16, 12), block(12, 12)], micros=5,
-    )(place, states, s_own, swap(s_own), end, *held)
+    )(states, s_own, swap(s_own), end, *held)
     a_own, a_own2 = shift(edge, 1), shift(next_edge, 2)
     l_own, after = lax.optimization_barrier((l_own, next_edge))
     l_other = swap(l_own)
     stage = [block(28), block(24), block(20), block(24, 12), block(20, 12), block(16, 12)]
-    held = kernel(ahead_body, "ahead", 6, stage, micros=2)(place, states, l_own, own2, l_other, other2, after)
+    held = kernel(ahead_body, "ahead", 6, stage, micros=2)(states, l_own, own2, l_other, other2, after)
     a_own, a_own2, *held = lax.optimization_barrier((a_own, a_own2, *held))
     a_other, a_other2 = swap(a_own), swap(a_own2)
     (gradient,) = kernel(
         last_body, "last_step", 11, [(FIELDS, NZ * 8, NY)], [block(20), block(16), block(12)], micros=2
-    )(place, share, a_own, a_own2, a_other, a_other2, *held)
+    )(share, a_own, a_own2, a_other, a_other2, *held)
     return gradient.reshape(FIELDS, NZ, 8, NY)
 
 

time: 44.9 us -> 42.8 us (0.953)
  Pallas kernels: 13.9 us -> 10.4 us
  waiting for transfers between devices: 13.8 us -> 15.2 us
    pallas_call x2, Pallas kernels: 1.86 us -> 0.72 us  [the longest x1 0.57 us: body(): pl.pallas_call(turn_body, out_shape=[jax.ShapeDtypeStruct((4, NZ, NY), jn...]
    ppermute x6, waiting for transfers between devices: 8.02 us -> 9.13 us  [shift(): return lax.ppermute(array, ('section', 'tile'), pairs)]
    pallas_call x1, Pallas kernels: 4.5 us -> 3.9 us  [body(): kernel(first_body, 'first_steps', 10, [block(20), block(12), block(4)], [...]
    pallas_call x1, Pallas kernels: 2.76 us -> 2.16 us  [body(): kernel(last_body, 'last_step', 11, [(FIELDS, NZ * 8, NY)], [block(20), bl...]
    pallas_call x1, Pallas kernels: 2.71 us -> 2.12 us  [body(): kernel(forward_body, 'last_forward', 5, [block(20)] + stage, micros=3)]
    pallas_call x1, Pallas kernels: 2.11 us -> 1.52 us  [body(): kernel(ahead_body, 'ahead', 6, stage, micros=2)]
  transfers between devices with their start and end apart: 15 -> 15, of which waited for: 10 -> 9; matrix products, arithmetic and copies ran while one was open for 0% -> 0% of each run, Pallas kernels for 23% -> 19%
where the time goes in v3:
time: 42.8 us; the launch traced here: 42.6 us
  starting transfers between devices  15.3 us (36%)
  waiting for transfers between devices  15.2 us (36%)
  Pallas kernels  10.4 us (24%)
  local copies, waits for them, and re-layouts  1.6 us (4%)
    ppermute x6, starting transfers between devices, shift(): return lax.ppermute(array, ('section', 'tile'), pairs)  11.9 us
    ppermute x6, waiting for transfers between devices, shift(): return lax.ppermute(array, ('section', 'tile'), pairs)  9.13 us
    ppermute x9, waiting for transfers between devices, swap(): lax.ppermute(array, 'section', [(s, s ^ mask) for s in range(sections)])  6.08 us
    pallas_call x1, Pallas kernels, body(): kernel(first_body, 'first_steps', 10, [block(20), block(12), block(4)], [...  3.9 us
    ppermute x9, starting transfers between devices, swap(): lax.ppermute(array, 'section', [(s, s ^ mask) for s in range(sections)])  3.46 us
    pallas_call x1, Pallas kernels, body(): kernel(last_body, 'last_step', 11, [(FIELDS, NZ * 8, NY)], [block(20), bl...  2.16 us
    pallas_call x1, Pallas kernels, body(): kernel(forward_body, 'last_forward', 5, [block(20)] + stage, micros=3)  2.12 us
    unnamed x4, local copies, waits for them, and re-layouts  1.6 us
  transfers between devices with their start and end apart: 15, of which 9 were waited for; matrix products, arithmetic and copies ran while one was open for 0% of the time, Pallas kernels for 19%

profile of v3, /device:TPU:0, one launch (start us, length us, event | category | flops | bytes accessed | tf_op | source)
XLA Modules:
  0.0 42.6 jit_solution(1634978616035766493)
XLA Ops:
  0.0 2.9 %collective-permute-start = (f32[5,64,128]{2,1,0:T(8,128)}, f32[5,64,128]{2,1,0:T(8,128)S(1)}, u32[]{:S(2)}, u32[]{:S(2)}) collective-permute-start(f32[5,64,128]{2,1,0:T(8,128)} %bitcast.2), channel_id=1, source_target_pairs={{0,16},{8,24},{16,0},{24,8},{1,17},{9,25},{17,1},{25,9},{2,18},{10... | collective-permute-start | bytes 491528 | tf_op jit(solution)/shard_map/ppermute | solution.py:372
  2.9 0.0 collective-permute-start.1
  2.9 0.9 %copy-done = f32[1,5,8,8,128]{4,3,2,1,0:T(8,128)S(1)} copy-done((f32[1,5,8,8,128]{4,3,2,1,0:T(8,128)S(1)}, f32[1,5,8,8,128]{4,3,2,1,0:T(8,128)}, u32[]{:S(2)}) %copy-start) | copy-done | bytes 163864
  3.9 0.7 %copy-done.1 = s32[4]{0:T(128)S(1)} copy-done((s32[4]{0:T(128)S(1)}, s32[4]{0:T(128)}, u32[]{:S(2)}) %copy-start.1) | copy-done | bytes 40
  4.5 0.6 %turn.1 = (s32[4,8,128]{2,1,0:T(8,128)S(1)}, f32[8,5,8,128]{3,2,1,0:T(8,128)S(1)}) custom-call(s32[4]{0:T(128)S(1)} %copy-done.1, f32[5,64,128]{2,1,0:T(8,128)S(1)} %bitcast.4), custom_call_target="tpu_custom_call" | custom-call | tf_op jit(solution)/shard_map/turn/pallas_call | solution.py:378
  5.1 2.2 %collective-permute-done.across = f32[5,64,128]{2,1,0:T(8,128)S(1)} collective-permute-done((f32[5,64,128]{2,1,0:T(8,128)}, f32[5,64,128]{2,1,0:T(8,128)S(1)}, u32[]{:S(2)}, u32[]{:S(2)}) %collective-permute-start) | collective-permute-done | bytes 163872 | tf_op jit(solution)/shard_map/ppermute | solution.py:372
  7.3 0.0 collective-permute-start.2
  7.3 0.0 collective-permute-done.1.beside
  7.4 1.4 %collective-permute-done.2.corner = f32[5,64,128]{2,1,0:T(8,128)S(1)} collective-permute-done((f32[5,64,128]{2,1,0:T(8,128)S(1)}, f32[5,64,128]{2,1,0:T(8,128)S(1)}, u32[]{:S(2)}, u32[]{:S(2)}) %collective-permute-start.2) | collective-permute-done | bytes 163872 | tf_op jit(solution)/shard_map/ppermute | solution.py:372
  8.7 0.1 pack.1
  8.9 4.9 %collective-permute-start.4 = (f32[8,5,8,128]{3,2,1,0:T(8,128)S(1)}, f32[8,5,8,128]{3,2,1,0:T(8,128)S(1)}, u32[]{:S(2)}, u32[]{:S(2)}) collective-permute-start(f32[8,5,8,128]{3,2,1,0:T(8,128)S(1)} %get-tuple-element.52), channel_id=1, source_target_pairs={{0,7},{1,0},{2,1},{3,2},{4,3},{5,4},{6,5},{7,6},{8,9},{9,10},{10,1... | collective-permute-start | bytes 491528 | tf_op jit(solution)/shard_map/ppermute | solution.py:369
  13.8 0.4 %collective-permute-start.5 = (f32[6,5,8,128]{3,2,1,0:T(8,128)S(1)}, f32[6,5,8,128]{3,2,1,0:T(8,128)S(1)}, u32[]{:S(2)}, u32[]{:S(2)}) collective-permute-start(f32[6,5,8,128]{3,2,1,0:T(8,128)S(1)} %get-tuple-element.54), channel_id=1, source_target_pairs={{0,6},{1,7},{2,0},{3,1},{4,2},{5,3},{6,4},{7,5},{8,10},{9,11},{10,... | collective-permute-start | bytes 368648 | tf_op jit(solution)/shard_map/ppermute | solution.py:369
  14.2 0.5 %collective-permute-start.3 = (f32[12,5,8,128]{3,2,1,0:T(8,128)S(1)}, f32[12,5,8,128]{3,2,1,0:T(8,128)S(1)}, u32[]{:S(2)}, u32[]{:S(2)}) collective-permute-start(f32[12,5,8,128]{3,2,1,0:T(8,128)S(1)} %get-tuple-element.51), channel_id=1, source_target_pairs={{0,7},{1,0},{2,1},{3,2},{4,3},{5,4},{6,5},{7,6},{8,9},{9,10},{10,1... | collective-permute-start | bytes 737288 | tf_op jit(solution)/shard_map/ppermute | solution.py:369
  14.7 1.9 %collective-permute-done.4.own = f32[8,5,8,128]{3,2,1,0:T(8,128)S(1)} collective-permute-done((f32[8,5,8,128]{3,2,1,0:T(8,128)S(1)}, f32[8,5,8,128]{3,2,1,0:T(8,128)S(1)}, u32[]{:S(2)}, u32[]{:S(2)}) %collective-permute-start.4) | collective-permute-done | bytes 163872 | tf_op jit(solution)/shard_map/ppermute | solution.py:369
  16.6 2.0 %collective-permute-done.5.own2 = f32[6,5,8,128]{3,2,1,0:T(8,128)S(1)} collective-permute-done((f32[6,5,8,128]{3,2,1,0:T(8,128)S(1)}, f32[6,5,8,128]{3,2,1,0:T(8,128)S(1)}, u32[]{:S(2)}, u32[]{:S(2)}) %collective-permute-start.5) | collective-permute-done | bytes 122912 | tf_op jit(solution)/shard_map/ppermute | solution.py:369
  18.6 0.0 collective-permute-start.7
  18.6 1.3 %collective-permute-done.7.other2 = f32[6,5,8,128]{3,2,1,0:T(8,128)S(1)} collective-permute-done((f32[6,5,8,128]{3,2,1,0:T(8,128)S(1)}, f32[6,5,8,128]{3,2,1,0:T(8,128)S(1)}, u32[]{:S(2)}, u32[]{:S(2)}) %collective-permute-start.7) | collective-permute-done | bytes 122912 | tf_op jit(solution)/shard_map/ppermute | solution.py:372
  20.0 0.0 collective-permute-done.6.other
  20.0 2.1 %last_forward.1 = (f32[20,5,8,128]{3,2,1,0:T(8,128)S(1)}, f32[32,5,8,128]{3,2,1,0:T(8,128)S(1)}, f32[28,5,8,128]{3,2,1,0:T(8,128)S(1)}, f32[24,5,8,128]{3,2,1,0:...) custom-call(f32[4,8,5,8,128]{4,3,2,1,0:T(8,128)S(1)} %get-tuple-element, ...), custom_call_target="tpu_custom_call" | custom-call | flops 12000000 | bytes 9000000 | tf_op jit(solution)/shard_map/last_forward/pallas_call | solution.py:397
  22.1 0.9 %collective-permute-done.3.own = f32[12,5,8,128]{3,2,1,0:T(8,128)S(1)} collective-permute-done((f32[12,5,8,128]{3,2,1,0:T(8,128)S(1)}, f32[12,5,8,128]{3,2,1,0:T(8,128)S(1)}, u32[]{:S(2)}, u32[]{:S(2)}) %collective-permute-start.3) | collective-permute-done | bytes 245792 | tf_op jit(solution)/shard_map/ppermute | solution.py:369
  23.0 0.0 collective-permute-start.8
  23.0 3.0 %collective-permute-start.11 = (f32[8,5,8,128]{3,2,1,0:T(8,128)S(1)}, f32[8,5,8,128]{3,2,1,0:T(8,128)S(1)}, u32[]{:S(2)}, u32[]{:S(2)}) collective-permute-start(f32[8,5,8,128]{3,2,1,0:T(8,128)S(1)} %get-tuple-element.68), channel_id=1, source_target_pairs={{0,7},{1,0},{2,1},{3,2},{4,3},{5,4},{6,5},{7,6},{8,9},{9,10},{10,1... | collective-permute-start | bytes 491528 | tf_op jit(solution)/shard_map/ppermute | solution.py:369
  26.0 3.9 %first_steps.1 = (f32[20,5,8,128]{3,2,1,0:T(8,128)S(1)}, f32[12,5,8,128]{3,2,1,0:T(8,128)S(1)}, f32[4,5,8,128]{3,2,1,0:T(8,128)S(1)}) custom-call(f32[4,8,5,8,128]{4,3,2,1,0:T(8,128)S(1)} %get-tuple-element.50.states, f32[12,5,8,128]{3,2,1,0:T(8,128)S(1)} %collective-permute-done.3.own, f32[12,5,8,128]{3,2,1,0:T(8,128)S(1)} %collective-permute-done.8.other, ...), custom_call_target="tpu_custom_call" | custom-call | flops 20000000 | bytes 15000000 | tf_op jit(solution)/shard_map/first_steps/pallas_call | solution.py:401
  29.9 1.4 %collective-permute-start.9 = (f32[12,5,8,128]{3,2,1,0:T(8,128)S(1)}, f32[12,5,8,128]{3,2,1,0:T(8,128)S(1)}, u32[]{:S(2)}, u32[]{:S(2)}) collective-permute-start(f32[12,5,8,128]{3,2,1,0:T(8,128)S(1)} %get-tuple-element.66), channel_id=1, source_target_pairs={{0,7},{1,0},{2,1},{3,2},{4,3},{5,4},{6,5},{7,6},{8,9},{9,10},{10,1... | collective-permute-start | bytes 737288 | tf_op jit(solution)/shard_map/ppermute | solution.py:369
  31.4 0.0 collective-permute-done.11.own
  31.4 1.6 %collective-permute-start.10 = (f32[4,5,8,128]{3,2,1,0:T(8,128)S(1)}, f32[4,5,8,128]{3,2,1,0:T(8,128)S(1)}, u32[]{:S(2)}, u32[]{:S(2)}) collective-permute-start(f32[4,5,8,128]{3,2,1,0:T(8,128)S(1)} %get-tuple-element.70.after), channel_id=1, source_target_pairs={{0,6},{1,7},{2,0},{3,1},{4,2},{5,3},{6,4},{7,5},{8,10},{9,11},{10,... | collective-permute-start | bytes 245768 | tf_op jit(solution)/shard_map/ppermute | solution.py:369
  33.0 1.5 %ahead.1 = (f32[28,5,8,128]{3,2,1,0:T(8,128)S(1)}, f32[24,5,8,128]{3,2,1,0:T(8,128)S(1)}, f32[20,5,8,128]{3,2,1,0:T(8,128)S(1)}, f32[24,12,8,128]{3,2,1,0:T(8,12...) custom-call(f32[4,8,5,8,128]{4,3,2,1,0:T(8,128)S(1)} %get-tuple-element.50.states, ...), custom_call_target="tpu_custom_call" | custom-call | flops 8000000 | bytes 6000000 | tf_op jit(solution)/shard_map/ahead/pallas_call | solution.py:411
  34.5 2.1 %collective-permute-done.10.own2 = f32[4,5,8,128]{3,2,1,0:T(8,128)S(1)} collective-permute-done((f32[4,5,8,128]{3,2,1,0:T(8,128)S(1)}, f32[4,5,8,128]{3,2,1,0:T(8,128)S(1)}, u32[]{:S(2)}, u32[]{:S(2)}) %collective-permute-start.10) | collective-permute-done | bytes 81952 | tf_op jit(solution)/shard_map/ppermute | solution.py:369
  36.7 2.2 %collective-permute-done.9.own = f32[12,5,8,128]{3,2,1,0:T(8,128)S(1)} collective-permute-done((f32[12,5,8,128]{3,2,1,0:T(8,128)S(1)}, f32[12,5,8,128]{3,2,1,0:T(8,128)S(1)}, u32[]{:S(2)}, u32[]{:S(2)}) %collective-permute-start.9) | collective-permute-done | bytes 245792 | tf_op jit(solution)/shard_map/ppermute | solution.py:369
  38.8 0.5 %collective-permute-start.14 = (f32[4,5,8,128]{3,2,1,0:T(8,128)S(1)}, f32[4,5,8,128]{3,2,1,0:T(8,128)S(1)}, u32[]{:S(2)}, u32[]{:S(2)}) collective-permute-start(f32[4,5,8,128]{3,2,1,0:T(8,128)S(1)} %collective-permute-done.10.own2), channel_id=1, source_target_pairs={{0,8},{8,0},{16,24},{24,16},{1,9},{9,1},{17,25},{25,17},{2,10},{10... | collective-permute-start | bytes 245768 | tf_op jit(solution)/shard_map/ppermute | solution.py:372
  39.3 1.1 %collective-permute-done.14.other2 = f32[4,5,8,128]{3,2,1,0:T(8,128)S(1)} collective-permute-done((f32[4,5,8,128]{3,2,1,0:T(8,128)S(1)}, f32[4,5,8,128]{3,2,1,0:T(8,128)S(1)}, u32[]{:S(2)}, u32[]{:S(2)}) %collective-permute-start.14) | collective-permute-done | bytes 81952 | tf_op jit(solution)/shard_map/ppermute | solution.py:372
  40.4 2.2 %last_step.1 = f32[5,64,128]{2,1,0:T(8,128)} custom-call(f32[20,5,8,128]{3,2,1,0:T(8,128)S(1)} %get-tuple-element.65.share, f32[12,5,8,128]{3,2,1,0:T(8,128)S(1)} %collective-permute-done.9.own, f32[4,5,8,128]{3,2,1,0:T(8,128)S(1)} %collective-permute-done.10.own2, f32[12,5,8,128]{3,2,1,0:T(8,128)S(1)} %collective-permute-done.13.other, ...), custom_call_target="tpu_custom_call" | custom-call | flops 8000000 | bytes 6000000 | tf_op jit(solution)/shard_map/last_step/pallas_call | solution.py:414
  (8 shorter events, 0.0 us)
Async XLA Ops:
  0.0 7.3 %collective-permute-start = (f32[5,64,128]{2,1,0:T(8,128)}, f32[5,64,128]{2,1,0:T(8,128)S(1)}, u32[]{:S(2)}, u32[]{:S(2)}) collective-permute-start(f32[5,64,128]{2,1,0:T(8,128)} %bitcast.2), channel_id=1, source_target_pairs={{0,16},{8,24},{16,0},{24,8},{1,17},{9,25},{17,1},{25,9},{2,18},{10... | collective-permute-start | bytes 491528 | tf_op jit(solution)/shard_map/ppermute | solution.py:372
  2.9 4.4 %collective-permute-start.1 = (f32[5,64,128]{2,1,0:T(8,128)}, f32[5,64,128]{2,1,0:T(8,128)S(1)}, u32[]{:S(2)}, u32[]{:S(2)}) collective-permute-start(f32[5,64,128]{2,1,0:T(8,128)} %bitcast.3), channel_id=1, source_target_pairs={{0,8},{8,0},{16,24},{24,16},{1,9},{9,1},{17,25},{25,17},{2,10},{10... | collective-permute-start | bytes 491528 | tf_op jit(solution)/shard_map/ppermute | solution.py:372
  2.9 0.9 %copy-start = (f32[1,5,8,8,128]{4,3,2,1,0:T(8,128)S(1)}, f32[1,5,8,8,128]{4,3,2,1,0:T(8,128)}, u32[]{:S(2)}) copy-start(f32[1,5,8,8,128]{4,3,2,1,0:T(8,128)} %param.2) | copy-start | bytes 491524
  3.9 0.7 %copy-start.1 = (s32[4]{0:T(128)S(1)}, s32[4]{0:T(128)}, u32[]{:S(2)}) copy-start(s32[4]{0:T(128)} %sched.1) | copy-start | bytes 52
  7.3 1.4 %collective-permute-start.2 = (f32[5,64,128]{2,1,0:T(8,128)S(1)}, f32[5,64,128]{2,1,0:T(8,128)S(1)}, u32[]{:S(2)}, u32[]{:S(2)}) collective-permute-start(f32[5,64,128]{2,1,0:T(8,128)S(1)} %collective-permute-done.across), channel_id=1, source_target_pairs={{0,8},{8,0},{16,24},{24,16},{1,9},{9,1},{17,25},{25,17},{2,10},{10... | collective-permute-start | bytes 491528 | tf_op jit(solution)/shard_map/ppermute | solution.py:372
  8.9 7.7 %collective-permute-start.4 = (f32[8,5,8,128]{3,2,1,0:T(8,128)S(1)}, f32[8,5,8,128]{3,2,1,0:T(8,128)S(1)}, u32[]{:S(2)}, u32[]{:S(2)}) collective-permute-start(f32[8,5,8,128]{3,2,1,0:T(8,128)S(1)} %get-tuple-element.52), channel_id=1, source_target_pairs={{0,7},{1,0},{2,1},{3,2},{4,3},{5,4},{6,5},{7,6},{8,9},{9,10},{10,1... | collective-permute-start | bytes 491528 | tf_op jit(solution)/shard_map/ppermute | solution.py:369
  13.8 4.9 %collective-permute-start.5 = (f32[6,5,8,128]{3,2,1,0:T(8,128)S(1)}, f32[6,5,8,128]{3,2,1,0:T(8,128)S(1)}, u32[]{:S(2)}, u32[]{:S(2)}) collective-permute-start(f32[6,5,8,128]{3,2,1,0:T(8,128)S(1)} %get-tuple-element.54), channel_id=1, source_target_pairs={{0,6},{1,7},{2,0},{3,1},{4,2},{5,3},{6,4},{7,5},{8,10},{9,11},{10,... | collective-permute-start | bytes 368648 | tf_op jit(solution)/shard_map/ppermute | solution.py:369
  14.2 8.8 %collective-permute-start.3 = (f32[12,5,8,128]{3,2,1,0:T(8,128)S(1)}, f32[12,5,8,128]{3,2,1,0:T(8,128)S(1)}, u32[]{:S(2)}, u32[]{:S(2)}) collective-permute-start(f32[12,5,8,128]{3,2,1,0:T(8,128)S(1)} %get-tuple-element.51), channel_id=1, source_target_pairs={{0,7},{1,0},{2,1},{3,2},{4,3},{5,4},{6,5},{7,6},{8,9},{9,10},{10,1... | collective-permute-start | bytes 737288 | tf_op jit(solution)/shard_map/ppermute | solution.py:369
  16.6 3.4 %collective-permute-start.6 = (f32[8,5,8,128]{3,2,1,0:T(8,128)S(1)}, f32[8,5,8,128]{3,2,1,0:T(8,128)S(1)}, u32[]{:S(2)}, u32[]{:S(2)}) collective-permute-start(f32[8,5,8,128]{3,2,1,0:T(8,128)S(1)} %collective-permute-done.4.own), channel_id=1, source_target_pairs={{0,8},{8,0},{16,24},{24,16},{1,9},{9,1},{17,25},{25,17},{2,10},{10... | collective-permute-start | bytes 491528 | tf_op jit(solution)/shard_map/ppermute | solution.py:372
  18.6 1.3 %collective-permute-start.7 = (f32[6,5,8,128]{3,2,1,0:T(8,128)S(1)}, f32[6,5,8,128]{3,2,1,0:T(8,128)S(1)}, u32[]{:S(2)}, u32[]{:S(2)}) collective-permute-start(f32[6,5,8,128]{3,2,1,0:T(8,128)S(1)} %collective-permute-done.5.own2), channel_id=1, source_target_pairs={{0,8},{8,0},{16,24},{24,16},{1,9},{9,1},{17,25},{25,17},{2,10},{10... | collective-permute-start | bytes 368648 | tf_op jit(solution)/shard_map/ppermute | solution.py:372
  23.0 3.0 %collective-permute-start.8 = (f32[12,5,8,128]{3,2,1,0:T(8,128)S(1)}, f32[12,5,8,128]{3,2,1,0:T(8,128)S(1)}, u32[]{:S(2)}, u32[]{:S(2)}) collective-permute-start(f32[12,5,8,128]{3,2,1,0:T(8,128)S(1)} %collective-permute-done.3.own), channel_id=1, source_target_pairs={{0,8},{8,0},{16,24},{24,16},{1,9},{9,1},{17,25},{25,17},{2,10},{10... | collective-permute-start | bytes 737288 | tf_op jit(solution)/shard_map/ppermute | solution.py:372
  23.0 8.3 %collective-permute-start.11 = (f32[8,5,8,128]{3,2,1,0:T(8,128)S(1)}, f32[8,5,8,128]{3,2,1,0:T(8,128)S(1)}, u32[]{:S(2)}, u32[]{:S(2)}) collective-permute-start(f32[8,5,8,128]{3,2,1,0:T(8,128)S(1)} %get-tuple-element.68), channel_id=1, source_target_pairs={{0,7},{1,0},{2,1},{3,2},{4,3},{5,4},{6,5},{7,6},{8,9},{9,10},{10,1... | collective-permute-start | bytes 491528 | tf_op jit(solution)/shard_map/ppermute | solution.py:369
  29.9 8.9 %collective-permute-start.9 = (f32[12,5,8,128]{3,2,1,0:T(8,128)S(1)}, f32[12,5,8,128]{3,2,1,0:T(8,128)S(1)}, u32[]{:S(2)}, u32[]{:S(2)}) collective-permute-start(f32[12,5,8,128]{3,2,1,0:T(8,128)S(1)} %get-tuple-element.66), channel_id=1, source_target_pairs={{0,7},{1,0},{2,1},{3,2},{4,3},{5,4},{6,5},{7,6},{8,9},{9,10},{10,1... | collective-permute-start | bytes 737288 | tf_op jit(solution)/shard_map/ppermute | solution.py:369
  31.4 1.7 %collective-permute-start.12 = (f32[8,5,8,128]{3,2,1,0:T(8,128)S(1)}, f32[8,5,8,128]{3,2,1,0:T(8,128)S(1)}, u32[]{:S(2)}, u32[]{:S(2)}) collective-permute-start(f32[8,5,8,128]{3,2,1,0:T(8,128)S(1)} %collective-permute-done.11.own), channel_id=1, source_target_pairs={{0,8},{8,0},{16,24},{24,16},{1,9},{9,1},{17,25},{25,17},{2,10},{10... | collective-permute-start | bytes 491528 | tf_op jit(solution)/shard_map/ppermute | solution.py:372
  31.4 5.3 %collective-permute-start.10 = (f32[4,5,8,128]{3,2,1,0:T(8,128)S(1)}, f32[4,5,8,128]{3,2,1,0:T(8,128)S(1)}, u32[]{:S(2)}, u32[]{:S(2)}) collective-permute-start(f32[4,5,8,128]{3,2,1,0:T(8,128)S(1)} %get-tuple-element.70.after), channel_id=1, source_target_pairs={{0,6},{1,7},{2,0},{3,1},{4,2},{5,3},{6,4},{7,5},{8,10},{9,11},{10,... | collective-permute-start | bytes 245768 | tf_op jit(solution)/shard_map/ppermute | solution.py:369
  38.8 1.6 %collective-permute-start.13 = (f32[12,5,8,128]{3,2,1,0:T(8,128)S(1)}, f32[12,5,8,128]{3,2,1,0:T(8,128)S(1)}, u32[]{:S(2)}, u32[]{:S(2)}) collective-permute-start(f32[12,5,8,128]{3,2,1,0:T(8,128)S(1)} %collective-permute-done.9.own), channel_id=1, source_target_pairs={{0,8},{8,0},{16,24},{24,16},{1,9},{9,1},{17,25},{25,17},{2,10},{10... | collective-permute-start | bytes 737288 | tf_op jit(solution)/shard_map/ppermute | solution.py:372
  38.8 1.6 %collective-permute-start.14 = (f32[4,5,8,128]{3,2,1,0:T(8,128)S(1)}, f32[4,5,8,128]{3,2,1,0:T(8,128)S(1)}, u32[]{:S(2)}, u32[]{:S(2)}) collective-permute-start(f32[4,5,8,128]{3,2,1,0:T(8,128)S(1)} %collective-permute-done.10.own2), channel_id=1, source_target_pairs={{0,8},{8,0},{16,24},{24,16},{1,9},{9,1},{17,25},{25,17},{2,10},{10... | collective-permute-start | bytes 245768 | tf_op jit(solution)/shard_map/ppermute | solution.py:372

commit v4 on v3

--- a/solution.py
+++ b/solution.py
@@ -25,12 +25,12 @@
     return (terms[0] + terms[1]) + terms[2]
 
 
-def blocks(low, high, visit):
-    size = max(k for k in range(1, BLOCK + 1) if (high - low) % k == 0)
-
-    @pl.loop(0, (high - low) // size)
+def blocks(first, count, visit):
+    size = max(k for k in range(1, BLOCK + 1) if count % k == 0)
+
+    @pl.loop(0, count // size)
     def _(step):
-        visit(low + step * size, size)
+        visit(first + step * size, size)
 
 
 def margin(ref):
@@ -85,10 +85,10 @@
                 moved.append(value)
             finish(first, row, moved)
 
-    blocks(-reach, 8 + reach, visit)
-
-
-def back_rows(adjoint, state, slopes, reach, finish):
+    blocks(-reach, 8 + 2 * reach, visit)
+
+
+def back_rows(adjoint, state, slopes, rows, finish):
     def visit(first, size):
         seen_adjoint, seen_vel, seen_prod, seen_hyper = {}, {}, {}, {}
 
@@ -153,7 +153,7 @@
                 pulled.append(value)
             finish(first, row, pulled)
 
-    blocks(-reach, 8 + reach, visit)
+    blocks(*rows, visit)
 
 
 def store(ref, scale=None):
@@ -174,10 +174,7 @@
     forward_rows(q1, slopes[1], second)
 
 
-def step_back(adjoint, states, slopes, back2, back1, reach, finish):
-    back_rows(adjoint, states[2], slopes[2], reach[0], store(back2, 2.0 / 3.0))
-    back_rows(back2, states[1], slopes[1], reach[1], store(back1, 0.25))
-
+def third_back(adjoint, back2, back1, state, slopes, rows, finish):
     def last(first, row, values):
         total = []
         for field in range(FIELDS):
@@ -185,7 +182,13 @@
             total.append((held + 0.75 * back2[first + (margin(back2) + row), field]) + values[field])
         finish(first, row, total)
 
-    back_rows(back1, states[0], slopes[0], reach[2], last)
+    back_rows(back1, state, slopes, rows, last)
+
+
+def step_back(adjoint, states, slopes, back2, back1, finish):
+    back_rows(adjoint, states[2], slopes[2], (-4, 16), store(back2, 2.0 / 3.0))
+    back_rows(back2, states[1], slopes[1], (-2, 12), store(back1, 0.25))
+    third_back(adjoint, back2, back1, states[0], slopes[0], (0, 8), finish)
 
 
 def clear_sides(ref, inner):
@@ -269,9 +272,10 @@
 
 
 def first_body(
-    states, own, other, end, q0, q1, q2, qs0, qs1, qs2, out, edge, next_edge,
-    last, qb2, qb1, lam, p0, p1, p2, pb2, pb1, ps0, ps1, ps2,
+    states, own, other, end, q0, q1, q2, qs0, qs1, qs2,
+    edge, next_edge, lam, pb2, pb1, p0, p1, ps0, ps1, last, qb2, qb1, p2, ps2,
 ):
+    core = core_index()
     copy_rows(p0, 8, states.at[1], 0, 8)
 
     def put(below, above):
@@ -290,13 +294,31 @@
     with_sides(own, other, put)
     for ref, inner in ((p0, 6), (p1, 4), (p2, 2), (ps0, 4), (ps1, 2), (ps2, 0), (lam, 0), (pb2, 2), (pb1, 4)):
         clear_sides(ref, inner)
-    step_back(last, (q0, q1, q2), (qs0, qs1, qs2), qb2, qb1, (4, 2, 0), store(lam))
+    step_back(last, (q0, q1, q2), (qs0, qs1, qs2), qb2, qb1, store(lam))
     inner = [ref.at[pl.ds(2, ref.shape[0] - 4)] for ref in (p0, p1, p2, ps0, ps1, ps2)]
     stages(*inner[:3], inner[3:5])
     forward_rows(inner[2], inner[5], None)
-    step_back(lam, (p0, p1, p2), (ps0, ps1, ps2), pb2, pb1, (2, 4, 6), store(out))
-    copy_rows(edge, 0, out, 8 * core_index(), 12)
-    copy_rows(next_edge, 0, out, 16 * core_index(), 4)
+    back_rows(lam, p2, ps2, (-2, 12), store(pb2, 2.0 / 3.0))
+    back_rows(pb2, p1, ps1, (-4 + 4 * core, 12), store(pb1, 0.25))
+
+    def finish(first, row, values):
+        for field in range(FIELDS):
+            edge[first + (6 - 8 * core + row), field] = values[field]
+
+    third_back(lam, pb2, pb1, p0, ps0, (-6 + 8 * core, 12), finish)
+    copy_rows(next_edge, 0, edge, 8 * core, 4)
+
+
+def rest_body(lam, pb2, pb1, p0, p1, ps0, ps1, out, back1):
+    core = core_index()
+    copy_rows(back1, 0, pb1, 0, 24)
+    back_rows(pb2, p1, ps1, (8 - 12 * core, 4), store(back1, 0.25))
+
+    def finish(first, row, values):
+        for field in range(FIELDS):
+            out[first + (-6 + 12 * core + row), field] = values[field]
+
+    third_back(lam, pb2, back1, p0, ps0, (6 - 12 * core, 8), finish)
 
 
 def ahead_body(states, own, own2, other, other2, after, x0, x1, x2, xs0, xs1, xs2):
@@ -314,12 +336,12 @@
     forward_rows(x2, xs2, None)
 
 
-def last_body(share, own, own2, other, other2, x0, x1, x2, xs0, xs1, xs2, out, lam, back2, back1):
-    def put(below, above):
+def last_body(edge, rest, own, own2, other, other2, x0, x1, x2, xs0, xs1, xs2, out, lam, back2, back1):
+    def put(below, above, low, high):
         (b1, b2), (a1, a2) = below, above
         for row in range(20):
             for field in range(FIELDS):
-                value = share[row, field]
+                value = low[row, field] if row < low.shape[0] else high[row - low.shape[0], field]
                 if row < 12:
                     value = value + b1[row, field]
                 if row < 4:
@@ -330,13 +352,19 @@
                     value = value + a2[row - 16, field]
                 lam[row, field] = value
 
-    with_sides((own, own2), (other, other2), put)
+    @pl.when(core_index() == 0)
+    def _():
+        put((other, other2), (own, own2), edge, rest)
+
+    @pl.when(core_index() != 0)
+    def _():
+        put((own, own2), (other, other2), rest, edge)
 
     def finish(first, row, values):
         for field in range(FIELDS):
             out[field, pl.ds(first + row, NZ, stride=8), :] = values[field]
 
-    step_back(lam, (x0, x1, x2), (xs0, xs1, xs2), back2, back1, (4, 2, 0), finish)
+    step_back(lam, (x0, x1, x2), (xs0, xs1, xs2), back2, back1, finish)
 
 
 def block(count, planes=FIELDS):
@@ -398,22 +426,22 @@
         states, own, own2, other, other2
     )
     s_own, end = lax.optimization_barrier((s_own, end))
-    share, edge, next_edge = kernel(
-        first_body, "first_steps", 10, [block(20), block(12), block(4)],
-        [block(20), block(16), block(12)]
-        + [block(20), block(24), block(20), block(16), block(20), block(24)]
-        + [block(20, 12), block(16, 12), block(12, 12)], micros=5,
+    edge, next_edge, *middle = kernel(
+        first_body, "first_steps", 10,
+        [block(12), block(4), block(20), block(20), block(24), block(24), block(20), block(20, 12), block(16, 12)],
+        [block(20), block(16), block(12), block(16), block(12, 12)], micros=5,
     )(states, s_own, swap(s_own), end, *held)
     a_own, a_own2 = shift(edge, 1), shift(next_edge, 2)
     l_own, after = lax.optimization_barrier((l_own, next_edge))
     l_other = swap(l_own)
     stage = [block(28), block(24), block(20), block(24, 12), block(20, 12), block(16, 12)]
     held = kernel(ahead_body, "ahead", 6, stage, micros=2)(states, l_own, own2, l_other, other2, after)
-    a_own, a_own2, *held = lax.optimization_barrier((a_own, a_own2, *held))
+    (rest,) = kernel(rest_body, "rest", 7, [block(8)], [block(24)])(*middle)
+    a_own, a_own2, rest, *held = lax.optimization_barrier((a_own, a_own2, rest, *held))
     a_other, a_other2 = swap(a_own), swap(a_own2)
     (gradient,) = kernel(
-        last_body, "last_step", 11, [(FIELDS, NZ * 8, NY)], [block(20), block(16), block(12)], micros=2
-    )(share, a_own, a_own2, a_other, a_other2, *held)
+        last_body, "last_step", 12, [(FIELDS, NZ * 8, NY)], [block(20), block(16), block(12)], micros=2
+    )(edge, rest, a_own, a_own2, a_other, a_other2, *held)
     return gradient.reshape(FIELDS, NZ, 8, NY)
 
 

time: 42.8 us -> 42.5 us (level)
  waiting for transfers between devices: 15.2 us -> 14.5 us
    ppermute x6, waiting for transfers between devices: 9.13 us -> 8.41 us  [shift(): return lax.ppermute(array, ('section', 'tile'), pairs)]
    pallas_call x2 -> x3, Pallas kernels: 6.06 us -> 6.35 us  [the longest x1 3.69 us: body(): kernel(first_body, 'first_steps', 10, [block(12), block(4), block(20), bl...]
  transfers between devices with their start and end apart: 15 -> 15, of which waited for: 9 -> 9; matrix products, arithmetic and copies ran while one was open for 0% -> 0% of each run, Pallas kernels for 19% -> 20%
where the time goes in v4:
time: 42.5 us; the launch traced here: 42.4 us
  starting transfers between devices  15.5 us (36%)
  waiting for transfers between devices  14.5 us (34%)
  Pallas kernels  10.7 us (25%)
  local copies, waits for them, and re-layouts  1.6 us (4%)
    ppermute x6, starting transfers between devices, shift(): return lax.ppermute(array, ('section', 'tile'), pairs)  12.1 us
    ppermute x6, waiting for transfers between devices, shift(): return lax.ppermute(array, ('section', 'tile'), pairs)  8.41 us
    ppermute x9, waiting for transfers between devices, swap(): lax.ppermute(array, 'section', [(s, s ^ mask) for s in range(sections)])  6.08 us
    pallas_call x1, Pallas kernels, body(): kernel(first_body, 'first_steps', 10, [block(12), block(4), block(20), bl...  3.69 us
    ppermute x9, starting transfers between devices, swap(): lax.ppermute(array, 'section', [(s, s ^ mask) for s in range(sections)])  3.46 us
    pallas_call x1, Pallas kernels, body(): kernel(last_body, 'last_step', 12, [(FIELDS, NZ * 8, NY)], [block(20), bl...  2.14 us
    pallas_call x1, Pallas kernels, body(): kernel(forward_body, 'last_forward', 5, [block(20)] + stage, micros=3)  2.1 us
    unnamed x4, local copies, waits for them, and re-layouts  1.6 us
  transfers between devices with their start and end apart: 15, of which 9 were waited for; matrix products, arithmetic and copies ran while one was open for 0% of the time, Pallas kernels for 20%

profile of v4, /device:TPU:0, one launch (start us, length us, event | category | flops | bytes accessed | tf_op | source)
XLA Modules:
  0.0 42.4 jit_solution(13928685228323125513)
XLA Ops:
  0.0 2.9 %collective-permute-start = (f32[5,64,128]{2,1,0:T(8,128)}, f32[5,64,128]{2,1,0:T(8,128)S(1)}, u32[]{:S(2)}, u32[]{:S(2)}) collective-permute-start(f32[5,64,128]{2,1,0:T(8,128)} %bitcast.2), channel_id=1, source_target_pairs={{0,16},{8,24},{16,0},{24,8},{1,17},{9,25},{17,1},{25,9},{2,18},{10... | collective-permute-start | bytes 491528 | tf_op jit(solution)/shard_map/ppermute | solution.py:400
  2.9 0.0 collective-permute-start.1
  2.9 0.9 %copy-done = f32[1,5,8,8,128]{4,3,2,1,0:T(8,128)S(1)} copy-done((f32[1,5,8,8,128]{4,3,2,1,0:T(8,128)S(1)}, f32[1,5,8,8,128]{4,3,2,1,0:T(8,128)}, u32[]{:S(2)}) %copy-start) | copy-done | bytes 163864
  3.9 0.7 %copy-done.1 = s32[4]{0:T(128)S(1)} copy-done((s32[4]{0:T(128)S(1)}, s32[4]{0:T(128)}, u32[]{:S(2)}) %copy-start.1) | copy-done | bytes 40
  4.5 0.6 %turn.1 = (s32[4,8,128]{2,1,0:T(8,128)S(1)}, f32[8,5,8,128]{3,2,1,0:T(8,128)S(1)}) custom-call(s32[4]{0:T(128)S(1)} %copy-done.1, f32[5,64,128]{2,1,0:T(8,128)S(1)} %bitcast.4), custom_call_target="tpu_custom_call" | custom-call | tf_op jit(solution)/shard_map/turn/pallas_call | solution.py:406
  5.1 2.2 %collective-permute-done.across = f32[5,64,128]{2,1,0:T(8,128)S(1)} collective-permute-done((f32[5,64,128]{2,1,0:T(8,128)}, f32[5,64,128]{2,1,0:T(8,128)S(1)}, u32[]{:S(2)}, u32[]{:S(2)}) %collective-permute-start) | collective-permute-done | bytes 163872 | tf_op jit(solution)/shard_map/ppermute | solution.py:400
  7.3 0.0 collective-permute-start.2
  7.3 0.0 collective-permute-done.1.beside
  7.4 1.4 %collective-permute-done.2.corner = f32[5,64,128]{2,1,0:T(8,128)S(1)} collective-permute-done((f32[5,64,128]{2,1,0:T(8,128)S(1)}, f32[5,64,128]{2,1,0:T(8,128)S(1)}, u32[]{:S(2)}, u32[]{:S(2)}) %collective-permute-start.2) | collective-permute-done | bytes 163872 | tf_op jit(solution)/shard_map/ppermute | solution.py:400
  8.7 0.1 pack.1
  8.9 4.9 %collective-permute-start.4 = (f32[8,5,8,128]{3,2,1,0:T(8,128)S(1)}, f32[8,5,8,128]{3,2,1,0:T(8,128)S(1)}, u32[]{:S(2)}, u32[]{:S(2)}) collective-permute-start(f32[8,5,8,128]{3,2,1,0:T(8,128)S(1)} %get-tuple-element.59), channel_id=1, source_target_pairs={{0,7},{1,0},{2,1},{3,2},{4,3},{5,4},{6,5},{7,6},{8,9},{9,10},{10,1... | collective-permute-start | bytes 491528 | tf_op jit(solution)/shard_map/ppermute | solution.py:397
  13.8 0.4 %collective-permute-start.5 = (f32[6,5,8,128]{3,2,1,0:T(8,128)S(1)}, f32[6,5,8,128]{3,2,1,0:T(8,128)S(1)}, u32[]{:S(2)}, u32[]{:S(2)}) collective-permute-start(f32[6,5,8,128]{3,2,1,0:T(8,128)S(1)} %get-tuple-element.61), channel_id=1, source_target_pairs={{0,6},{1,7},{2,0},{3,1},{4,2},{5,3},{6,4},{7,5},{8,10},{9,11},{10,... | collective-permute-start | bytes 368648 | tf_op jit(solution)/shard_map/ppermute | solution.py:397
  14.2 0.5 %collective-permute-start.3 = (f32[12,5,8,128]{3,2,1,0:T(8,128)S(1)}, f32[12,5,8,128]{3,2,1,0:T(8,128)S(1)}, u32[]{:S(2)}, u32[]{:S(2)}) collective-permute-start(f32[12,5,8,128]{3,2,1,0:T(8,128)S(1)} %get-tuple-element.58), channel_id=1, source_target_pairs={{0,7},{1,0},{2,1},{3,2},{4,3},{5,4},{6,5},{7,6},{8,9},{9,10},{10,1... | collective-permute-start | bytes 737288 | tf_op jit(solution)/shard_map/ppermute | solution.py:397
  14.7 1.9 %collective-permute-done.4.own = f32[8,5,8,128]{3,2,1,0:T(8,128)S(1)} collective-permute-done((f32[8,5,8,128]{3,2,1,0:T(8,128)S(1)}, f32[8,5,8,128]{3,2,1,0:T(8,128)S(1)}, u32[]{:S(2)}, u32[]{:S(2)}) %collective-permute-start.4) | collective-permute-done | bytes 163872 | tf_op jit(solution)/shard_map/ppermute | solution.py:397
  16.6 2.0 %collective-permute-done.5.own2 = f32[6,5,8,128]{3,2,1,0:T(8,128)S(1)} collective-permute-done((f32[6,5,8,128]{3,2,1,0:T(8,128)S(1)}, f32[6,5,8,128]{3,2,1,0:T(8,128)S(1)}, u32[]{:S(2)}, u32[]{:S(2)}) %collective-permute-start.5) | collective-permute-done | bytes 122912 | tf_op jit(solution)/shard_map/ppermute | solution.py:397
  18.6 0.0 collective-permute-start.7
  18.6 1.3 %collective-permute-done.7.other2 = f32[6,5,8,128]{3,2,1,0:T(8,128)S(1)} collective-permute-done((f32[6,5,8,128]{3,2,1,0:T(8,128)S(1)}, f32[6,5,8,128]{3,2,1,0:T(8,128)S(1)}, u32[]{:S(2)}, u32[]{:S(2)}) %collective-permute-start.7) | collective-permute-done | bytes 122912 | tf_op jit(solution)/shard_map/ppermute | solution.py:400
  20.0 0.0 collective-permute-done.6.other
  20.0 2.1 %last_forward.1 = (f32[20,5,8,128]{3,2,1,0:T(8,128)S(1)}, f32[32,5,8,128]{3,2,1,0:T(8,128)S(1)}, f32[28,5,8,128]{3,2,1,0:T(8,128)S(1)}, f32[24,5,8,128]{3,2,1,0:...) custom-call(f32[4,8,5,8,128]{4,3,2,1,0:T(8,128)S(1)} %get-tuple-element, ...), custom_call_target="tpu_custom_call" | custom-call | flops 12000000 | bytes 9000000 | tf_op jit(solution)/shard_map/last_forward/pallas_call | solution.py:425
  22.1 1.0 %collective-permute-done.3.own = f32[12,5,8,128]{3,2,1,0:T(8,128)S(1)} collective-permute-done((f32[12,5,8,128]{3,2,1,0:T(8,128)S(1)}, f32[12,5,8,128]{3,2,1,0:T(8,128)S(1)}, u32[]{:S(2)}, u32[]{:S(2)}) %collective-permute-start.3) | collective-permute-done | bytes 245792 | tf_op jit(solution)/shard_map/ppermute | solution.py:397
  23.0 0.0 collective-permute-start.8
  23.0 3.0 %collective-permute-start.11 = (f32[8,5,8,128]{3,2,1,0:T(8,128)S(1)}, f32[8,5,8,128]{3,2,1,0:T(8,128)S(1)}, u32[]{:S(2)}, u32[]{:S(2)}) collective-permute-start(f32[8,5,8,128]{3,2,1,0:T(8,128)S(1)} %get-tuple-element.81), channel_id=1, source_target_pairs={{0,7},{1,0},{2,1},{3,2},{4,3},{5,4},{6,5},{7,6},{8,9},{9,10},{10,1... | collective-permute-start | bytes 491528 | tf_op jit(solution)/shard_map/ppermute | solution.py:397
  26.0 3.7 %first_steps.1 = (f32[12,5,8,128]{3,2,1,0:T(8,128)S(1)}, f32[4,5,8,128]{3,2,1,0:T(8,128)S(1)}, f32[20,5,8,128]{3,2,1,0:T(8,128)S(1)}, f32[20,5,8,128]{3,2,1,0:T(...) custom-call(f32[4,8,5,8,128]{4,3,2,1,0:T(8,128)S(1)} %get-tuple-elem, ...), custom_call_target="tpu_custom_call" | custom-call | flops 20000000 | bytes 15000000 | tf_op jit(solution)/shard_map/first_steps/pallas_call | solution.py:429
  29.7 1.4 %collective-permute-start.9 = (f32[12,5,8,128]{3,2,1,0:T(8,128)S(1)}, f32[12,5,8,128]{3,2,1,0:T(8,128)S(1)}, u32[]{:S(2)}, u32[]{:S(2)}) collective-permute-start(f32[12,5,8,128]{3,2,1,0:T(8,128)S(1)} %get-tuple-element.72.edge), channel_id=1, source_target_pairs={{0,7},{1,0},{2,1},{3,2},{4,3},{5,4},{6,5},{7,6},{8,9},{9,10},{10,1... | collective-permute-start | bytes 737288 | tf_op jit(solution)/shard_map/ppermute | solution.py:397
  31.1 1.9 %collective-permute-start.10 = (f32[4,5,8,128]{3,2,1,0:T(8,128)S(1)}, f32[4,5,8,128]{3,2,1,0:T(8,128)S(1)}, u32[]{:S(2)}, u32[]{:S(2)}) collective-permute-start(f32[4,5,8,128]{3,2,1,0:T(8,128)S(1)} %get-tuple-element.83.after), channel_id=1, source_target_pairs={{0,6},{1,7},{2,0},{3,1},{4,2},{5,3},{6,4},{7,5},{8,10},{9,11},{10,... | collective-permute-start | bytes 245768 | tf_op jit(solution)/shard_map/ppermute | solution.py:397
  33.0 0.5 %rest.1 = f32[8,5,8,128]{3,2,1,0:T(8,128)S(1)} custom-call(f32[20,5,8,128]{3,2,1,0:T(8,128)S(1)} %get-tuple-element.74.lam, f32[20,5,8,128]{3,2,1,0:T(8,128)S(1)} %get-tuple-element.75.pb2, f32[24,5,8,128]{3,2,1,0:T(8,128)S(1)} %get-tuple-element.76.pb1, f32[24,5,8,128]{3,2,1,0:T(8,128)S(1)} %get-tuple-element.77.p0, ...), custom_call_target="tpu_custom_call" | custom-call | flops 4000000 | bytes 3000000 | tf_op jit(solution)/shard_map/rest/pallas_call | solution.py:439
  33.5 1.5 %ahead.1 = (f32[28,5,8,128]{3,2,1,0:T(8,128)S(1)}, f32[24,5,8,128]{3,2,1,0:T(8,128)S(1)}, f32[20,5,8,128]{3,2,1,0:T(8,128)S(1)}, f32[24,12,8,128]{3,2,1,0:T(8,12...) custom-call(f32[4,8,5,8,128]{4,3,2,1,0:T(8,128)S(1)} %get-tuple-element.57.states, ...), custom_call_target="tpu_custom_call" | custom-call | flops 8000000 | bytes 6000000 | tf_op jit(solution)/shard_map/ahead/pallas_call | solution.py:438
  35.1 1.4 %collective-permute-done.10.own2 = f32[4,5,8,128]{3,2,1,0:T(8,128)S(1)} collective-permute-done((f32[4,5,8,128]{3,2,1,0:T(8,128)S(1)}, f32[4,5,8,128]{3,2,1,0:T(8,128)S(1)}, u32[]{:S(2)}, u32[]{:S(2)}) %collective-permute-start.10) | collective-permute-done | bytes 81952 | tf_op jit(solution)/shard_map/ppermute | solution.py:397
  36.4 2.2 %collective-permute-done.9.own = f32[12,5,8,128]{3,2,1,0:T(8,128)S(1)} collective-permute-done((f32[12,5,8,128]{3,2,1,0:T(8,128)S(1)}, f32[12,5,8,128]{3,2,1,0:T(8,128)S(1)}, u32[]{:S(2)}, u32[]{:S(2)}) %collective-permute-start.9) | collective-permute-done | bytes 245792 | tf_op jit(solution)/shard_map/ppermute | solution.py:397
  38.6 0.5 %collective-permute-start.14 = (f32[4,5,8,128]{3,2,1,0:T(8,128)S(1)}, f32[4,5,8,128]{3,2,1,0:T(8,128)S(1)}, u32[]{:S(2)}, u32[]{:S(2)}) collective-permute-start(f32[4,5,8,128]{3,2,1,0:T(8,128)S(1)} %collective-permute-done.10.own2), channel_id=1, source_target_pairs={{0,8},{8,0},{16,24},{24,16},{1,9},{9,1},{17,25},{25,17},{2,10},{10... | collective-permute-start | bytes 245768 | tf_op jit(solution)/shard_map/ppermute | solution.py:400
  39.1 1.1 %collective-permute-done.14.other2 = f32[4,5,8,128]{3,2,1,0:T(8,128)S(1)} collective-permute-done((f32[4,5,8,128]{3,2,1,0:T(8,128)S(1)}, f32[4,5,8,128]{3,2,1,0:T(8,128)S(1)}, u32[]{:S(2)}, u32[]{:S(2)}) %collective-permute-start.14) | collective-permute-done | bytes 81952 | tf_op jit(solution)/shard_map/ppermute | solution.py:400
  40.2 2.1 %last_step.1 = f32[5,64,128]{2,1,0:T(8,128)} custom-call(f32[12,5,8,128]{3,2,1,0:T(8,128)S(1)} %get-tuple-element.72.edge, f32[8,5,8,128]{3,2,1,0:T(8,128)S(1)} %rest.1, f32[12,5,8,128]{3,2,1,0:T(8,128)S(1)} %collective-permute-done.9.own, f32[4,5,8,128]{3,2,1,0:T(8,128)S(1)} %collective-permute-done.10.own2, ...), custom_call_target="tpu_custom_call" | custom-call | flops 8000000 | bytes 6000000 | tf_op jit(solution)/shard_map/last_step/pallas_call | solution.py:442
  (9 shorter events, 0.0 us)
Async XLA Ops:
  0.0 7.3 %collective-permute-start = (f32[5,64,128]{2,1,0:T(8,128)}, f32[5,64,128]{2,1,0:T(8,128)S(1)}, u32[]{:S(2)}, u32[]{:S(2)}) collective-permute-start(f32[5,64,128]{2,1,0:T(8,128)} %bitcast.2), channel_id=1, source_target_pairs={{0,16},{8,24},{16,0},{24,8},{1,17},{9,25},{17,1},{25,9},{2,18},{10... | collective-permute-start | bytes 491528 | tf_op jit(solution)/shard_map/ppermute | solution.py:400
  2.9 4.4 %collective-permute-start.1 = (f32[5,64,128]{2,1,0:T(8,128)}, f32[5,64,128]{2,1,0:T(8,128)S(1)}, u32[]{:S(2)}, u32[]{:S(2)}) collective-permute-start(f32[5,64,128]{2,1,0:T(8,128)} %bitcast.3), channel_id=1, source_target_pairs={{0,8},{8,0},{16,24},{24,16},{1,9},{9,1},{17,25},{25,17},{2,10},{10... | collective-permute-start | bytes 491528 | tf_op jit(solution)/shard_map/ppermute | solution.py:400
  2.9 0.9 %copy-start = (f32[1,5,8,8,128]{4,3,2,1,0:T(8,128)S(1)}, f32[1,5,8,8,128]{4,3,2,1,0:T(8,128)}, u32[]{:S(2)}) copy-start(f32[1,5,8,8,128]{4,3,2,1,0:T(8,128)} %param.2) | copy-start | bytes 491524
  3.9 0.7 %copy-start.1 = (s32[4]{0:T(128)S(1)}, s32[4]{0:T(128)}, u32[]{:S(2)}) copy-start(s32[4]{0:T(128)} %sched.1) | copy-start | bytes 52
  7.3 1.4 %collective-permute-start.2 = (f32[5,64,128]{2,1,0:T(8,128)S(1)}, f32[5,64,128]{2,1,0:T(8,128)S(1)}, u32[]{:S(2)}, u32[]{:S(2)}) collective-permute-start(f32[5,64,128]{2,1,0:T(8,128)S(1)} %collective-permute-done.across), channel_id=1, source_target_pairs={{0,8},{8,0},{16,24},{24,16},{1,9},{9,1},{17,25},{25,17},{2,10},{10... | collective-permute-start | bytes 491528 | tf_op jit(solution)/shard_map/ppermute | solution.py:400
  8.9 7.7 %collective-permute-start.4 = (f32[8,5,8,128]{3,2,1,0:T(8,128)S(1)}, f32[8,5,8,128]{3,2,1,0:T(8,128)S(1)}, u32[]{:S(2)}, u32[]{:S(2)}) collective-permute-start(f32[8,5,8,128]{3,2,1,0:T(8,128)S(1)} %get-tuple-element.59), channel_id=1, source_target_pairs={{0,7},{1,0},{2,1},{3,2},{4,3},{5,4},{6,5},{7,6},{8,9},{9,10},{10,1... | collective-permute-start | bytes 491528 | tf_op jit(solution)/shard_map/ppermute | solution.py:397
  13.8 4.9 %collective-permute-start.5 = (f32[6,5,8,128]{3,2,1,0:T(8,128)S(1)}, f32[6,5,8,128]{3,2,1,0:T(8,128)S(1)}, u32[]{:S(2)}, u32[]{:S(2)}) collective-permute-start(f32[6,5,8,128]{3,2,1,0:T(8,128)S(1)} %get-tuple-element.61), channel_id=1, source_target_pairs={{0,6},{1,7},{2,0},{3,1},{4,2},{5,3},{6,4},{7,5},{8,10},{9,11},{10,... | collective-permute-start | bytes 368648 | tf_op jit(solution)/shard_map/ppermute | solution.py:397
  14.2 8.8 %collective-permute-start.3 = (f32[12,5,8,128]{3,2,1,0:T(8,128)S(1)}, f32[12,5,8,128]{3,2,1,0:T(8,128)S(1)}, u32[]{:S(2)}, u32[]{:S(2)}) collective-permute-start(f32[12,5,8,128]{3,2,1,0:T(8,128)S(1)} %get-tuple-element.58), channel_id=1, source_target_pairs={{0,7},{1,0},{2,1},{3,2},{4,3},{5,4},{6,5},{7,6},{8,9},{9,10},{10,1... | collective-permute-start | bytes 737288 | tf_op jit(solution)/shard_map/ppermute | solution.py:397
  16.6 3.4 %collective-permute-start.6 = (f32[8,5,8,128]{3,2,1,0:T(8,128)S(1)}, f32[8,5,8,128]{3,2,1,0:T(8,128)S(1)}, u32[]{:S(2)}, u32[]{:S(2)}) collective-permute-start(f32[8,5,8,128]{3,2,1,0:T(8,128)S(1)} %collective-permute-done.4.own), channel_id=1, source_target_pairs={{0,8},{8,0},{16,24},{24,16},{1,9},{9,1},{17,25},{25,17},{2,10},{10... | collective-permute-start | bytes 491528 | tf_op jit(solution)/shard_map/ppermute | solution.py:400
  18.6 1.3 %collective-permute-start.7 = (f32[6,5,8,128]{3,2,1,0:T(8,128)S(1)}, f32[6,5,8,128]{3,2,1,0:T(8,128)S(1)}, u32[]{:S(2)}, u32[]{:S(2)}) collective-permute-start(f32[6,5,8,128]{3,2,1,0:T(8,128)S(1)} %collective-permute-done.5.own2), channel_id=1, source_target_pairs={{0,8},{8,0},{16,24},{24,16},{1,9},{9,1},{17,25},{25,17},{2,10},{10... | collective-permute-start | bytes 368648 | tf_op jit(solution)/shard_map/ppermute | solution.py:400
  23.0 3.0 %collective-permute-start.8 = (f32[12,5,8,128]{3,2,1,0:T(8,128)S(1)}, f32[12,5,8,128]{3,2,1,0:T(8,128)S(1)}, u32[]{:S(2)}, u32[]{:S(2)}) collective-permute-start(f32[12,5,8,128]{3,2,1,0:T(8,128)S(1)} %collective-permute-done.3.own), channel_id=1, source_target_pairs={{0,8},{8,0},{16,24},{24,16},{1,9},{9,1},{17,25},{25,17},{2,10},{10... | collective-permute-start | bytes 737288 | tf_op jit(solution)/shard_map/ppermute | solution.py:400
  23.0 8.1 %collective-permute-start.11 = (f32[8,5,8,128]{3,2,1,0:T(8,128)S(1)}, f32[8,5,8,128]{3,2,1,0:T(8,128)S(1)}, u32[]{:S(2)}, u32[]{:S(2)}) collective-permute-start(f32[8,5,8,128]{3,2,1,0:T(8,128)S(1)} %get-tuple-element.81), channel_id=1, source_target_pairs={{0,7},{1,0},{2,1},{3,2},{4,3},{5,4},{6,5},{7,6},{8,9},{9,10},{10,1... | collective-permute-start | bytes 491528 | tf_op jit(solution)/shard_map/ppermute | solution.py:397
  29.7 8.9 %collective-permute-start.9 = (f32[12,5,8,128]{3,2,1,0:T(8,128)S(1)}, f32[12,5,8,128]{3,2,1,0:T(8,128)S(1)}, u32[]{:S(2)}, u32[]{:S(2)}) collective-permute-start(f32[12,5,8,128]{3,2,1,0:T(8,128)S(1)} %get-tuple-element.72.edge), channel_id=1, source_target_pairs={{0,7},{1,0},{2,1},{3,2},{4,3},{5,4},{6,5},{7,6},{8,9},{9,10},{10,1... | collective-permute-start | bytes 737288 | tf_op jit(solution)/shard_map/ppermute | solution.py:397
  31.1 2.4 %collective-permute-start.12 = (f32[8,5,8,128]{3,2,1,0:T(8,128)S(1)}, f32[8,5,8,128]{3,2,1,0:T(8,128)S(1)}, u32[]{:S(2)}, u32[]{:S(2)}) collective-permute-start(f32[8,5,8,128]{3,2,1,0:T(8,128)S(1)} %collective-permute-done.11.own), channel_id=1, source_target_pairs={{0,8},{8,0},{16,24},{24,16},{1,9},{9,1},{17,25},{25,17},{2,10},{10... | collective-permute-start | bytes 491528 | tf_op jit(solution)/shard_map/ppermute | solution.py:400
  31.1 5.3 %collective-permute-start.10 = (f32[4,5,8,128]{3,2,1,0:T(8,128)S(1)}, f32[4,5,8,128]{3,2,1,0:T(8,128)S(1)}, u32[]{:S(2)}, u32[]{:S(2)}) collective-permute-start(f32[4,5,8,128]{3,2,1,0:T(8,128)S(1)} %get-tuple-element.83.after), channel_id=1, source_target_pairs={{0,6},{1,7},{2,0},{3,1},{4,2},{5,3},{6,4},{7,5},{8,10},{9,11},{10,... | collective-permute-start | bytes 245768 | tf_op jit(solution)/shard_map/ppermute | solution.py:397
  38.6 1.6 %collective-permute-start.13 = (f32[12,5,8,128]{3,2,1,0:T(8,128)S(1)}, f32[12,5,8,128]{3,2,1,0:T(8,128)S(1)}, u32[]{:S(2)}, u32[]{:S(2)}) collective-permute-start(f32[12,5,8,128]{3,2,1,0:T(8,128)S(1)} %collective-permute-done.9.own), channel_id=1, source_target_pairs={{0,8},{8,0},{16,24},{24,16},{1,9},{9,1},{17,25},{25,17},{2,10},{10... | collective-permute-start | bytes 737288 | tf_op jit(solution)/shard_map/ppermute | solution.py:400
  38.6 1.6 %collective-permute-start.14 = (f32[4,5,8,128]{3,2,1,0:T(8,128)S(1)}, f32[4,5,8,128]{3,2,1,0:T(8,128)S(1)}, u32[]{:S(2)}, u32[]{:S(2)}) collective-permute-start(f32[4,5,8,128]{3,2,1,0:T(8,128)S(1)} %collective-permute-done.10.own2), channel_id=1, source_target_pairs={{0,8},{8,0},{16,24},{24,16},{1,9},{9,1},{17,25},{25,17},{2,10},{10... | collective-permute-start | bytes 245768 | tf_op jit(solution)/shard_map/ppermute | solution.py:400

commit v5 on v4

--- a/solution.py
+++ b/solution.py
@@ -164,9 +164,9 @@
     return finish
 
 
-def stages(q0, q1, q2, slopes):
+def stages(q0, q1, q2, slopes, fields=4):
     def second(first, row, values):
-        for field in range(FIELDS):
+        for field in range(fields):
             kept = q0[first + (margin(q0) + row), field]
             q2[first + (margin(q2) + row), field] = 0.75 * kept + 0.25 * values[field]
 
@@ -261,7 +261,7 @@
         copy_rows(q0, 28, a2, 0, 4)
 
     with_sides((own, own2), (other, other2), put)
-    stages(q0, q1, q2, (qs0, qs1))
+    stages(q0, q1, q2, (qs0, qs1), FIELDS)
 
     def finish(first, row, values):
         for field in range(FIELDS):

time: 42.5 us -> 42.5 us (level)
  no operation moved by 1% of the time
where the time goes in v5:
time: 42.5 us; the launch traced here: 42.4 us
  starting transfers between devices  15.5 us (36%)
  waiting for transfers between devices  14.5 us (34%)
  Pallas kernels  10.6 us (25%)
  local copies, waits for them, and re-layouts  1.6 us (4%)
    ppermute x6, starting transfers between devices, shift(): return lax.ppermute(array, ('section', 'tile'), pairs)  12.1 us
    ppermute x6, waiting for transfers between devices, shift(): return lax.ppermute(array, ('section', 'tile'), pairs)  8.46 us
    ppermute x9, waiting for transfers between devices, swap(): lax.ppermute(array, 'section', [(s, s ^ mask) for s in range(sections)])  6.08 us
    pallas_call x1, Pallas kernels, body(): kernel(first_body, 'first_steps', 10, [block(12), block(4), block(20), bl...  3.69 us
    ppermute x9, starting transfers between devices, swap(): lax.ppermute(array, 'section', [(s, s ^ mask) for s in range(sections)])  3.46 us
    pallas_call x1, Pallas kernels, body(): kernel(last_body, 'last_step', 12, [(FIELDS, NZ * 8, NY)], [block(20), bl...  2.14 us
    pallas_call x1, Pallas kernels, body(): kernel(forward_body, 'last_forward', 5, [block(20)] + stage, micros=3)  2.1 us
    unnamed x4, local copies, waits for them, and re-layouts  1.6 us
  transfers between devices with their start and end apart: 15, of which 9 were waited for; matrix products, arithmetic and copies ran while one was open for 0% of the time, Pallas kernels for 20%

profile of v5, /device:TPU:0, one launch (start us, length us, event | category | flops | bytes accessed | tf_op | source)
XLA Modules:
  0.0 42.4 jit_solution(17988851243640406944)
XLA Ops:
  0.0 2.9 %collective-permute-start = (f32[5,64,128]{2,1,0:T(8,128)}, f32[5,64,128]{2,1,0:T(8,128)S(1)}, u32[]{:S(2)}, u32[]{:S(2)}) collective-permute-start(f32[5,64,128]{2,1,0:T(8,128)} %bitcast.2), channel_id=1, source_target_pairs={{0,16},{8,24},{16,0},{24,8},{1,17},{9,25},{17,1},{25,9},{2,18},{10... | collective-permute-start | bytes 491528 | tf_op jit(solution)/shard_map/ppermute | solution.py:400
  2.9 0.0 collective-permute-start.1
  2.9 0.9 %copy-done = f32[1,5,8,8,128]{4,3,2,1,0:T(8,128)S(1)} copy-done((f32[1,5,8,8,128]{4,3,2,1,0:T(8,128)S(1)}, f32[1,5,8,8,128]{4,3,2,1,0:T(8,128)}, u32[]{:S(2)}) %copy-start) | copy-done | bytes 163864
  3.9 0.7 %copy-done.1 = s32[4]{0:T(128)S(1)} copy-done((s32[4]{0:T(128)S(1)}, s32[4]{0:T(128)}, u32[]{:S(2)}) %copy-start.1) | copy-done | bytes 40
  4.5 0.6 %turn.1 = (s32[4,8,128]{2,1,0:T(8,128)S(1)}, f32[8,5,8,128]{3,2,1,0:T(8,128)S(1)}) custom-call(s32[4]{0:T(128)S(1)} %copy-done.1, f32[5,64,128]{2,1,0:T(8,128)S(1)} %bitcast.4), custom_call_target="tpu_custom_call" | custom-call | tf_op jit(solution)/shard_map/turn/pallas_call | solution.py:406
  5.1 2.2 %collective-permute-done.across = f32[5,64,128]{2,1,0:T(8,128)S(1)} collective-permute-done((f32[5,64,128]{2,1,0:T(8,128)}, f32[5,64,128]{2,1,0:T(8,128)S(1)}, u32[]{:S(2)}, u32[]{:S(2)}) %collective-permute-start) | collective-permute-done | bytes 163872 | tf_op jit(solution)/shard_map/ppermute | solution.py:400
  7.3 0.0 collective-permute-start.2
  7.3 0.0 collective-permute-done.1.beside
  7.4 1.4 %collective-permute-done.2.corner = f32[5,64,128]{2,1,0:T(8,128)S(1)} collective-permute-done((f32[5,64,128]{2,1,0:T(8,128)S(1)}, f32[5,64,128]{2,1,0:T(8,128)S(1)}, u32[]{:S(2)}, u32[]{:S(2)}) %collective-permute-start.2) | collective-permute-done | bytes 163872 | tf_op jit(solution)/shard_map/ppermute | solution.py:400
  8.7 0.1 pack.1
  8.9 4.9 %collective-permute-start.4 = (f32[8,5,8,128]{3,2,1,0:T(8,128)S(1)}, f32[8,5,8,128]{3,2,1,0:T(8,128)S(1)}, u32[]{:S(2)}, u32[]{:S(2)}) collective-permute-start(f32[8,5,8,128]{3,2,1,0:T(8,128)S(1)} %get-tuple-element.59), channel_id=1, source_target_pairs={{0,7},{1,0},{2,1},{3,2},{4,3},{5,4},{6,5},{7,6},{8,9},{9,10},{10,1... | collective-permute-start | bytes 491528 | tf_op jit(solution)/shard_map/ppermute | solution.py:397
  13.8 0.4 %collective-permute-start.5 = (f32[6,5,8,128]{3,2,1,0:T(8,128)S(1)}, f32[6,5,8,128]{3,2,1,0:T(8,128)S(1)}, u32[]{:S(2)}, u32[]{:S(2)}) collective-permute-start(f32[6,5,8,128]{3,2,1,0:T(8,128)S(1)} %get-tuple-element.61), channel_id=1, source_target_pairs={{0,6},{1,7},{2,0},{3,1},{4,2},{5,3},{6,4},{7,5},{8,10},{9,11},{10,... | collective-permute-start | bytes 368648 | tf_op jit(solution)/shard_map/ppermute | solution.py:397
  14.2 0.5 %collective-permute-start.3 = (f32[12,5,8,128]{3,2,1,0:T(8,128)S(1)}, f32[12,5,8,128]{3,2,1,0:T(8,128)S(1)}, u32[]{:S(2)}, u32[]{:S(2)}) collective-permute-start(f32[12,5,8,128]{3,2,1,0:T(8,128)S(1)} %get-tuple-element.58), channel_id=1, source_target_pairs={{0,7},{1,0},{2,1},{3,2},{4,3},{5,4},{6,5},{7,6},{8,9},{9,10},{10,1... | collective-permute-start | bytes 737288 | tf_op jit(solution)/shard_map/ppermute | solution.py:397
  14.7 1.9 %collective-permute-done.4.own = f32[8,5,8,128]{3,2,1,0:T(8,128)S(1)} collective-permute-done((f32[8,5,8,128]{3,2,1,0:T(8,128)S(1)}, f32[8,5,8,128]{3,2,1,0:T(8,128)S(1)}, u32[]{:S(2)}, u32[]{:S(2)}) %collective-permute-start.4) | collective-permute-done | bytes 163872 | tf_op jit(solution)/shard_map/ppermute | solution.py:397
  16.6 2.0 %collective-permute-done.5.own2 = f32[6,5,8,128]{3,2,1,0:T(8,128)S(1)} collective-permute-done((f32[6,5,8,128]{3,2,1,0:T(8,128)S(1)}, f32[6,5,8,128]{3,2,1,0:T(8,128)S(1)}, u32[]{:S(2)}, u32[]{:S(2)}) %collective-permute-start.5) | collective-permute-done | bytes 122912 | tf_op jit(solution)/shard_map/ppermute | solution.py:397
  18.6 0.0 collective-permute-start.7
  18.6 1.3 %collective-permute-done.7.other2 = f32[6,5,8,128]{3,2,1,0:T(8,128)S(1)} collective-permute-done((f32[6,5,8,128]{3,2,1,0:T(8,128)S(1)}, f32[6,5,8,128]{3,2,1,0:T(8,128)S(1)}, u32[]{:S(2)}, u32[]{:S(2)}) %collective-permute-start.7) | collective-permute-done | bytes 122912 | tf_op jit(solution)/shard_map/ppermute | solution.py:400
  20.0 0.0 collective-permute-done.6.other
  20.0 2.1 %last_forward.1 = (f32[20,5,8,128]{3,2,1,0:T(8,128)S(1)}, f32[32,5,8,128]{3,2,1,0:T(8,128)S(1)}, f32[28,5,8,128]{3,2,1,0:T(8,128)S(1)}, f32[24,5,8,128]{3,2,1,0:...) custom-call(f32[4,8,5,8,128]{4,3,2,1,0:T(8,128)S(1)} %get-tuple-element, ...), custom_call_target="tpu_custom_call" | custom-call | flops 12000000 | bytes 9000000 | tf_op jit(solution)/shard_map/last_forward/pallas_call | solution.py:425
  22.1 1.0 %collective-permute-done.3.own = f32[12,5,8,128]{3,2,1,0:T(8,128)S(1)} collective-permute-done((f32[12,5,8,128]{3,2,1,0:T(8,128)S(1)}, f32[12,5,8,128]{3,2,1,0:T(8,128)S(1)}, u32[]{:S(2)}, u32[]{:S(2)}) %collective-permute-start.3) | collective-permute-done | bytes 245792 | tf_op jit(solution)/shard_map/ppermute | solution.py:397
  23.0 0.0 collective-permute-start.8
  23.0 3.0 %collective-permute-start.11 = (f32[8,5,8,128]{3,2,1,0:T(8,128)S(1)}, f32[8,5,8,128]{3,2,1,0:T(8,128)S(1)}, u32[]{:S(2)}, u32[]{:S(2)}) collective-permute-start(f32[8,5,8,128]{3,2,1,0:T(8,128)S(1)} %get-tuple-element.81), channel_id=1, source_target_pairs={{0,7},{1,0},{2,1},{3,2},{4,3},{5,4},{6,5},{7,6},{8,9},{9,10},{10,1... | collective-permute-start | bytes 491528 | tf_op jit(solution)/shard_map/ppermute | solution.py:397
  26.0 3.7 %first_steps.1 = (f32[12,5,8,128]{3,2,1,0:T(8,128)S(1)}, f32[4,5,8,128]{3,2,1,0:T(8,128)S(1)}, f32[20,5,8,128]{3,2,1,0:T(8,128)S(1)}, f32[20,5,8,128]{3,2,1,0:T(...) custom-call(f32[4,8,5,8,128]{4,3,2,1,0:T(8,128)S(1)} %get-tuple-elem, ...), custom_call_target="tpu_custom_call" | custom-call | flops 20000000 | bytes 15000000 | tf_op jit(solution)/shard_map/first_steps/pallas_call | solution.py:429
  29.7 1.4 %collective-permute-start.9 = (f32[12,5,8,128]{3,2,1,0:T(8,128)S(1)}, f32[12,5,8,128]{3,2,1,0:T(8,128)S(1)}, u32[]{:S(2)}, u32[]{:S(2)}) collective-permute-start(f32[12,5,8,128]{3,2,1,0:T(8,128)S(1)} %get-tuple-element.72.edge), channel_id=1, source_target_pairs={{0,7},{1,0},{2,1},{3,2},{4,3},{5,4},{6,5},{7,6},{8,9},{9,10},{10,1... | collective-permute-start | bytes 737288 | tf_op jit(solution)/shard_map/ppermute | solution.py:397
  31.1 1.9 %collective-permute-start.10 = (f32[4,5,8,128]{3,2,1,0:T(8,128)S(1)}, f32[4,5,8,128]{3,2,1,0:T(8,128)S(1)}, u32[]{:S(2)}, u32[]{:S(2)}) collective-permute-start(f32[4,5,8,128]{3,2,1,0:T(8,128)S(1)} %get-tuple-element.83.after), channel_id=1, source_target_pairs={{0,6},{1,7},{2,0},{3,1},{4,2},{5,3},{6,4},{7,5},{8,10},{9,11},{10,... | collective-permute-start | bytes 245768 | tf_op jit(solution)/shard_map/ppermute | solution.py:397
  33.0 0.5 %rest.1 = f32[8,5,8,128]{3,2,1,0:T(8,128)S(1)} custom-call(f32[20,5,8,128]{3,2,1,0:T(8,128)S(1)} %get-tuple-element.74.lam, f32[20,5,8,128]{3,2,1,0:T(8,128)S(1)} %get-tuple-element.75.pb2, f32[24,5,8,128]{3,2,1,0:T(8,128)S(1)} %get-tuple-element.76.pb1, f32[24,5,8,128]{3,2,1,0:T(8,128)S(1)} %get-tuple-element.77.p0, ...), custom_call_target="tpu_custom_call" | custom-call | flops 4000000 | bytes 3000000 | tf_op jit(solution)/shard_map/rest/pallas_call | solution.py:439
  33.5 1.5 %ahead.1 = (f32[28,5,8,128]{3,2,1,0:T(8,128)S(1)}, f32[24,5,8,128]{3,2,1,0:T(8,128)S(1)}, f32[20,5,8,128]{3,2,1,0:T(8,128)S(1)}, f32[24,12,8,128]{3,2,1,0:T(8,12...) custom-call(f32[4,8,5,8,128]{4,3,2,1,0:T(8,128)S(1)} %get-tuple-element.57.states, ...), custom_call_target="tpu_custom_call" | custom-call | flops 8000000 | bytes 6000000 | tf_op jit(solution)/shard_map/ahead/pallas_call | solution.py:438
  35.0 1.4 %collective-permute-done.10.own2 = f32[4,5,8,128]{3,2,1,0:T(8,128)S(1)} collective-permute-done((f32[4,5,8,128]{3,2,1,0:T(8,128)S(1)}, f32[4,5,8,128]{3,2,1,0:T(8,128)S(1)}, u32[]{:S(2)}, u32[]{:S(2)}) %collective-permute-start.10) | collective-permute-done | bytes 81952 | tf_op jit(solution)/shard_map/ppermute | solution.py:397
  36.4 2.2 %collective-permute-done.9.own = f32[12,5,8,128]{3,2,1,0:T(8,128)S(1)} collective-permute-done((f32[12,5,8,128]{3,2,1,0:T(8,128)S(1)}, f32[12,5,8,128]{3,2,1,0:T(8,128)S(1)}, u32[]{:S(2)}, u32[]{:S(2)}) %collective-permute-start.9) | collective-permute-done | bytes 245792 | tf_op jit(solution)/shard_map/ppermute | solution.py:397
  38.6 0.5 %collective-permute-start.14 = (f32[4,5,8,128]{3,2,1,0:T(8,128)S(1)}, f32[4,5,8,128]{3,2,1,0:T(8,128)S(1)}, u32[]{:S(2)}, u32[]{:S(2)}) collective-permute-start(f32[4,5,8,128]{3,2,1,0:T(8,128)S(1)} %collective-permute-done.10.own2), channel_id=1, source_target_pairs={{0,8},{8,0},{16,24},{24,16},{1,9},{9,1},{17,25},{25,17},{2,10},{10... | collective-permute-start | bytes 245768 | tf_op jit(solution)/shard_map/ppermute | solution.py:400
  39.1 1.1 %collective-permute-done.14.other2 = f32[4,5,8,128]{3,2,1,0:T(8,128)S(1)} collective-permute-done((f32[4,5,8,128]{3,2,1,0:T(8,128)S(1)}, f32[4,5,8,128]{3,2,1,0:T(8,128)S(1)}, u32[]{:S(2)}, u32[]{:S(2)}) %collective-permute-start.14) | collective-permute-done | bytes 81952 | tf_op jit(solution)/shard_map/ppermute | solution.py:400
  40.2 2.1 %last_step.1 = f32[5,64,128]{2,1,0:T(8,128)} custom-call(f32[12,5,8,128]{3,2,1,0:T(8,128)S(1)} %get-tuple-element.72.edge, f32[8,5,8,128]{3,2,1,0:T(8,128)S(1)} %rest.1, f32[12,5,8,128]{3,2,1,0:T(8,128)S(1)} %collective-permute-done.9.own, f32[4,5,8,128]{3,2,1,0:T(8,128)S(1)} %collective-permute-done.10.own2, ...), custom_call_target="tpu_custom_call" | custom-call | flops 8000000 | bytes 6000000 | tf_op jit(solution)/shard_map/last_step/pallas_call | solution.py:442
  (9 shorter events, 0.0 us)
Async XLA Ops:
  0.0 7.3 %collective-permute-start = (f32[5,64,128]{2,1,0:T(8,128)}, f32[5,64,128]{2,1,0:T(8,128)S(1)}, u32[]{:S(2)}, u32[]{:S(2)}) collective-permute-start(f32[5,64,128]{2,1,0:T(8,128)} %bitcast.2), channel_id=1, source_target_pairs={{0,16},{8,24},{16,0},{24,8},{1,17},{9,25},{17,1},{25,9},{2,18},{10... | collective-permute-start | bytes 491528 | tf_op jit(solution)/shard_map/ppermute | solution.py:400
  2.9 4.4 %collective-permute-start.1 = (f32[5,64,128]{2,1,0:T(8,128)}, f32[5,64,128]{2,1,0:T(8,128)S(1)}, u32[]{:S(2)}, u32[]{:S(2)}) collective-permute-start(f32[5,64,128]{2,1,0:T(8,128)} %bitcast.3), channel_id=1, source_target_pairs={{0,8},{8,0},{16,24},{24,16},{1,9},{9,1},{17,25},{25,17},{2,10},{10... | collective-permute-start | bytes 491528 | tf_op jit(solution)/shard_map/ppermute | solution.py:400
  2.9 0.9 %copy-start = (f32[1,5,8,8,128]{4,3,2,1,0:T(8,128)S(1)}, f32[1,5,8,8,128]{4,3,2,1,0:T(8,128)}, u32[]{:S(2)}) copy-start(f32[1,5,8,8,128]{4,3,2,1,0:T(8,128)} %param.2) | copy-start | bytes 491524
  3.9 0.7 %copy-start.1 = (s32[4]{0:T(128)S(1)}, s32[4]{0:T(128)}, u32[]{:S(2)}) copy-start(s32[4]{0:T(128)} %sched.1) | copy-start | bytes 52
  7.3 1.4 %collective-permute-start.2 = (f32[5,64,128]{2,1,0:T(8,128)S(1)}, f32[5,64,128]{2,1,0:T(8,128)S(1)}, u32[]{:S(2)}, u32[]{:S(2)}) collective-permute-start(f32[5,64,128]{2,1,0:T(8,128)S(1)} %collective-permute-done.across), channel_id=1, source_target_pairs={{0,8},{8,0},{16,24},{24,16},{1,9},{9,1},{17,25},{25,17},{2,10},{10... | collective-permute-start | bytes 491528 | tf_op jit(solution)/shard_map/ppermute | solution.py:400
  8.9 7.7 %collective-permute-start.4 = (f32[8,5,8,128]{3,2,1,0:T(8,128)S(1)}, f32[8,5,8,128]{3,2,1,0:T(8,128)S(1)}, u32[]{:S(2)}, u32[]{:S(2)}) collective-permute-start(f32[8,5,8,128]{3,2,1,0:T(8,128)S(1)} %get-tuple-element.59), channel_id=1, source_target_pairs={{0,7},{1,0},{2,1},{3,2},{4,3},{5,4},{6,5},{7,6},{8,9},{9,10},{10,1... | collective-permute-start | bytes 491528 | tf_op jit(solution)/shard_map/ppermute | solution.py:397
  13.8 4.9 %collective-permute-start.5 = (f32[6,5,8,128]{3,2,1,0:T(8,128)S(1)}, f32[6,5,8,128]{3,2,1,0:T(8,128)S(1)}, u32[]{:S(2)}, u32[]{:S(2)}) collective-permute-start(f32[6,5,8,128]{3,2,1,0:T(8,128)S(1)} %get-tuple-element.61), channel_id=1, source_target_pairs={{0,6},{1,7},{2,0},{3,1},{4,2},{5,3},{6,4},{7,5},{8,10},{9,11},{10,... | collective-permute-start | bytes 368648 | tf_op jit(solution)/shard_map/ppermute | solution.py:397
  14.2 8.8 %collective-permute-start.3 = (f32[12,5,8,128]{3,2,1,0:T(8,128)S(1)}, f32[12,5,8,128]{3,2,1,0:T(8,128)S(1)}, u32[]{:S(2)}, u32[]{:S(2)}) collective-permute-start(f32[12,5,8,128]{3,2,1,0:T(8,128)S(1)} %get-tuple-element.58), channel_id=1, source_target_pairs={{0,7},{1,0},{2,1},{3,2},{4,3},{5,4},{6,5},{7,6},{8,9},{9,10},{10,1... | collective-permute-start | bytes 737288 | tf_op jit(solution)/shard_map/ppermute | solution.py:397
  16.6 3.4 %collective-permute-start.6 = (f32[8,5,8,128]{3,2,1,0:T(8,128)S(1)}, f32[8,5,8,128]{3,2,1,0:T(8,128)S(1)}, u32[]{:S(2)}, u32[]{:S(2)}) collective-permute-start(f32[8,5,8,128]{3,2,1,0:T(8,128)S(1)} %collective-permute-done.4.own), channel_id=1, source_target_pairs={{0,8},{8,0},{16,24},{24,16},{1,9},{9,1},{17,25},{25,17},{2,10},{10... | collective-permute-start | bytes 491528 | tf_op jit(solution)/shard_map/ppermute | solution.py:400
  18.6 1.3 %collective-permute-start.7 = (f32[6,5,8,128]{3,2,1,0:T(8,128)S(1)}, f32[6,5,8,128]{3,2,1,0:T(8,128)S(1)}, u32[]{:S(2)}, u32[]{:S(2)}) collective-permute-start(f32[6,5,8,128]{3,2,1,0:T(8,128)S(1)} %collective-permute-done.5.own2), channel_id=1, source_target_pairs={{0,8},{8,0},{16,24},{24,16},{1,9},{9,1},{17,25},{25,17},{2,10},{10... | collective-permute-start | bytes 368648 | tf_op jit(solution)/shard_map/ppermute | solution.py:400
  23.0 3.0 %collective-permute-start.8 = (f32[12,5,8,128]{3,2,1,0:T(8,128)S(1)}, f32[12,5,8,128]{3,2,1,0:T(8,128)S(1)}, u32[]{:S(2)}, u32[]{:S(2)}) collective-permute-start(f32[12,5,8,128]{3,2,1,0:T(8,128)S(1)} %collective-permute-done.3.own), channel_id=1, source_target_pairs={{0,8},{8,0},{16,24},{24,16},{1,9},{9,1},{17,25},{25,17},{2,10},{10... | collective-permute-start | bytes 737288 | tf_op jit(solution)/shard_map/ppermute | solution.py:400
  23.0 8.1 %collective-permute-start.11 = (f32[8,5,8,128]{3,2,1,0:T(8,128)S(1)}, f32[8,5,8,128]{3,2,1,0:T(8,128)S(1)}, u32[]{:S(2)}, u32[]{:S(2)}) collective-permute-start(f32[8,5,8,128]{3,2,1,0:T(8,128)S(1)} %get-tuple-element.81), channel_id=1, source_target_pairs={{0,7},{1,0},{2,1},{3,2},{4,3},{5,4},{6,5},{7,6},{8,9},{9,10},{10,1... | collective-permute-start | bytes 491528 | tf_op jit(solution)/shard_map/ppermute | solution.py:397
  29.7 8.9 %collective-permute-start.9 = (f32[12,5,8,128]{3,2,1,0:T(8,128)S(1)}, f32[12,5,8,128]{3,2,1,0:T(8,128)S(1)}, u32[]{:S(2)}, u32[]{:S(2)}) collective-permute-start(f32[12,5,8,128]{3,2,1,0:T(8,128)S(1)} %get-tuple-element.72.edge), channel_id=1, source_target_pairs={{0,7},{1,0},{2,1},{3,2},{4,3},{5,4},{6,5},{7,6},{8,9},{9,10},{10,1... | collective-permute-start | bytes 737288 | tf_op jit(solution)/shard_map/ppermute | solution.py:397
  31.1 2.4 %collective-permute-start.12 = (f32[8,5,8,128]{3,2,1,0:T(8,128)S(1)}, f32[8,5,8,128]{3,2,1,0:T(8,128)S(1)}, u32[]{:S(2)}, u32[]{:S(2)}) collective-permute-start(f32[8,5,8,128]{3,2,1,0:T(8,128)S(1)} %collective-permute-done.11.own), channel_id=1, source_target_pairs={{0,8},{8,0},{16,24},{24,16},{1,9},{9,1},{17,25},{25,17},{2,10},{10... | collective-permute-start | bytes 491528 | tf_op jit(solution)/shard_map/ppermute | solution.py:400
  31.1 5.3 %collective-permute-start.10 = (f32[4,5,8,128]{3,2,1,0:T(8,128)S(1)}, f32[4,5,8,128]{3,2,1,0:T(8,128)S(1)}, u32[]{:S(2)}, u32[]{:S(2)}) collective-permute-start(f32[4,5,8,128]{3,2,1,0:T(8,128)S(1)} %get-tuple-element.83.after), channel_id=1, source_target_pairs={{0,6},{1,7},{2,0},{3,1},{4,2},{5,3},{6,4},{7,5},{8,10},{9,11},{10,... | collective-permute-start | bytes 245768 | tf_op jit(solution)/shard_map/ppermute | solution.py:397
  38.6 1.6 %collective-permute-start.13 = (f32[12,5,8,128]{3,2,1,0:T(8,128)S(1)}, f32[12,5,8,128]{3,2,1,0:T(8,128)S(1)}, u32[]{:S(2)}, u32[]{:S(2)}) collective-permute-start(f32[12,5,8,128]{3,2,1,0:T(8,128)S(1)} %collective-permute-done.9.own), channel_id=1, source_target_pairs={{0,8},{8,0},{16,24},{24,16},{1,9},{9,1},{17,25},{25,17},{2,10},{10... | collective-permute-start | bytes 737288 | tf_op jit(solution)/shard_map/ppermute | solution.py:400
  38.6 1.6 %collective-permute-start.14 = (f32[4,5,8,128]{3,2,1,0:T(8,128)S(1)}, f32[4,5,8,128]{3,2,1,0:T(8,128)S(1)}, u32[]{:S(2)}, u32[]{:S(2)}) collective-permute-start(f32[4,5,8,128]{3,2,1,0:T(8,128)S(1)} %collective-permute-done.10.own2), channel_id=1, source_target_pairs={{0,8},{8,0},{16,24},{24,16},{1,9},{9,1},{17,25},{25,17},{2,10},{10... | collective-permute-start | bytes 245768 | tf_op jit(solution)/shard_map/ppermute | solution.py:400
